TPU v7x, 32 devices: a whole 2x2x4 slice. The times are simulated.
32 devices in a mesh: seq: 8 (over y, x, core), fsdp: 4 (over z).
Axes of the slice: x: 2, y: 2, z: 4, core: 2. Of those that a mesh axis runs over, the one named last changes fastest.
Arguments:
- characters: bfloat16 [4, 4, 3840, 1600], P(None, 'fsdp', 'seq'), may hold values from -6 to 6
- lengths: int32 [4, 4, 16], P(None, 'fsdp'), may hold values from 1 to 3824, 3840 in all within a row
- cotangent: bfloat16 [4, 4, 3840, 1600], P(None, 'fsdp', 'seq'), may hold values from -6 to 6
- encproject: bfloat16 [1600, 800], P('fsdp'), may hold values from -0.21875 to 0.21875
- enckernel: bfloat16 [5, 800, 800], P(None, 'fsdp'), may hold values from -0.125 to 0.125
- encexpand: bfloat16 [800, 1600], P('fsdp'), may hold values from -0.3125 to 0.3125
- encwidegain: bfloat16 [1600], P('fsdp'), may hold values from 0.5 to 1.5
- encgains: bfloat16 [2, 800], P(None, 'fsdp'), may hold values from 0.5 to 1.5
- encwideshift: bfloat16 [2, 1600], P(None, 'fsdp'), may hold values from -3 to 3
- encshifts: bfloat16 [4, 800], P(None, 'fsdp'), may hold values from -3 to 3
- decproject: bfloat16 [1600, 800], P('fsdp'), may hold values from -0.21875 to 0.21875
- deckernel: bfloat16 [3, 800, 800], P(None, 'fsdp'), may hold values from -0.1875 to 0.1875
- decexpand: bfloat16 [800, 1600], P('fsdp'), may hold values from -0.3125 to 0.3125
- decwidegain: bfloat16 [1600], P('fsdp'), may hold values from 0.5 to 1.5
- decgains: bfloat16 [2, 800], P(None, 'fsdp'), may hold values from 0.5 to 1.5
- decwideshift: bfloat16 [2, 1600], P(None, 'fsdp'), may hold values from -3 to 3
- decshifts: bfloat16 [4, 800], P(None, 'fsdp'), may hold values from -3 to 3
Outputs:
- output: bfloat16 [4, 4, 3840, 1600], P(None, 'fsdp', 'seq')
- grad_characters: bfloat16 [4, 4, 3840, 1600], P(None, 'fsdp', 'seq')
- grad_encproject: float32 [1600, 800], P('fsdp')
- grad_enckernel: float32 [5, 800, 800], P(None, 'fsdp')
- grad_encexpand: float32 [800, 1600], P('fsdp')
- grad_encwidegain: float32 [1600], P('fsdp')
- grad_encgains: float32 [2, 800], P(None, 'fsdp')
- grad_encwideshift: float32 [2, 1600], P(None, 'fsdp')
- grad_encshifts: float32 [4, 800], P(None, 'fsdp')
- grad_decproject: float32 [1600, 800], P('fsdp')
- grad_deckernel: float32 [3, 800, 800], P(None, 'fsdp')
- grad_decexpand: float32 [800, 1600], P('fsdp')
- grad_decwidegain: float32 [1600], P('fsdp')
- grad_decgains: float32 [2, 800], P(None, 'fsdp')
- grad_decwideshift: float32 [2, 1600], P(None, 'fsdp')
- grad_decshifts: float32 [4, 800], P(None, 'fsdp')
Inputs may be any that keep to these rules, and one draw needn't show every extreme that they name: Each row of 16 lengths sums to 3840, and its largest entry is 3824.
All inputs are finite; a program needn't handle non-finite values.
Results may differ from a plain program's by a relative error of at most 0.012.
Values may be sent and summed in bfloat16 or wider, within the bound.
No kernel may reach another device: no remote copies, remote signals or barrier semaphores. Data moves between devices by JAX's collectives and lax.ppermute only.
A program may use at most 384 MiB of HBM per device.

v0:
```python
import jax
import jax.numpy as jnp
from jax import lax
from jax.sharding import PartitionSpec as P

ENC_TAPS = 5
ENC_DILATION = 8
DEC_TAPS = 3
DEC_DILATION = 16


epsilon = 1e-05


def extended_2(cells, sides, width):
    for axis, dim in sides:
        count = lax.axis_size(axis)
        ends = count - 1
        head = lax.slice_in_dim(cells, 0, width, axis=dim)
        tail = lax.slice_in_dim(cells, cells.shape[dim] - width, cells.shape[dim], axis=dim)
        cells = jnp.concatenate(
            [
                lax.ppermute(tail, axis, [(i, (i + 1) % count) for i in range(ends)]),
                cells,
                lax.ppermute(head, axis, [((i + 1) % count, i) for i in range(ends)]),
            ],
            axis=dim,
        )
    return cells


def from_behind(block, axis, distance):
    devices = range(lax.axis_size(axis))
    route = [(i - distance, i) for i in devices if i - distance in devices]
    return lax.ppermute(block, axis, route)


def norm_silu(values, norm_gain, norm_shift):
    average = jnp.mean(values, axis=-1, keepdims=True)
    centred = values - average
    spread = jnp.mean(centred * centred, axis=-1, keepdims=True)
    return jax.nn.silu(centred * lax.rsqrt(spread + epsilon) * norm_gain + norm_shift)


def matmul(factor, matrix):
    return jnp.dot(factor, matrix, preferred_element_type=jnp.float32)


def inner_product(factor, matrix):
    return lax.dot_general(
        factor, matrix, (((0,), (0,)), ((), ())), preferred_element_type=jnp.float32
    )


def matmul_back(factor, matrix):
    return lax.dot_general(
        factor, matrix, (((1,), (1,)), ((), ())), preferred_element_type=jnp.float32
    )


def owners(places, doc_ends):
    return jnp.sum((places[:, None] >= doc_ends[None, :]).astype(jnp.int32), axis=1)


def tap_offsets(encoder):
    if encoder:
        return [(tap_index - ENC_TAPS // 2) * ENC_DILATION for tap_index in range(ENC_TAPS)]
    return [(tap_index - DEC_TAPS + 1) * DEC_DILATION for tap_index in range(DEC_TAPS)]


def reach_of(encoder):
    if encoder:
        return ENC_DILATION * (ENC_TAPS // 2)
    return DEC_DILATION * (DEC_TAPS - 1)


def build_masks(places, doc_ends, stream_len, offsets):
    own_doc = owners(places, doc_ends)
    result = []
    for offset in offsets:
        partner = places + offset
        inside = (partner >= 0) & (partner < stream_len)
        result.append(inside & (owners(partner, doc_ends) == own_doc))
    return result


def gather_taps(extended, front_pad, offsets, masks_list, row_count):
    pieces = []
    for offset, usable in zip(offsets, masks_list):
        window = lax.slice_in_dim(
            extended, front_pad + offset, front_pad + offset + row_count, axis=0
        )
        pieces.append(jnp.where(usable[:, None], window, jnp.zeros_like(window)))
    return jnp.concatenate(pieces, axis=1)


def forward_block(stream, weights, fwd_masks, encoder):
    project, kernel, expand, wide_gain, gains, wide_shift, shifts = weights
    row_count = stream.shape[0]
    reach = reach_of(encoder)
    first = norm_silu(stream, wide_gain, wide_shift[0]).astype(jnp.bfloat16)
    hidden_in = matmul(first, project) + shifts[2]
    second = norm_silu(hidden_in, gains[0], shifts[0]).astype(jnp.bfloat16)
    if encoder:
        extended = extended_2(second, (("seq", 0),), reach)
    else:
        arrived = from_behind(second[row_count - reach :], "seq", 1)
        extended = jnp.concatenate([arrived, second], axis=0)
    columns = gather_taps(extended, reach, tap_offsets(encoder), fwd_masks, row_count)
    tap_count = kernel.shape[0]
    mixed = (
        matmul(columns, kernel.reshape(tap_count * kernel.shape[1], kernel.shape[2])) + shifts[3]
    )
    third = norm_silu(mixed, gains[1], shifts[1]).astype(jnp.bfloat16)
    branch = matmul(third, expand) + wide_shift[1]
    stored = (stream, first, hidden_in, columns, mixed, third)
    return (stream + branch, stored)


def backward_block(grad_out, stored, weights, back_masks, encoder):
    project, kernel, expand, wide_gain, gains, wide_shift, shifts = weights
    stream, first, hidden_in, columns, mixed, third = stored
    row_count = stream.shape[0]
    reach = reach_of(encoder)
    grad_branch = grad_out.astype(jnp.bfloat16)
    grad_expand = inner_product(third, grad_branch)
    grad_bias_out = jnp.sum(grad_branch.astype(jnp.float32), axis=0)
    grad_third = matmul_back(grad_branch, expand)
    unused, pull_third = jax.vjp(norm_silu, mixed, gains[1], shifts[1])
    grad_mixed, grad_gain_three, grad_shift_three = pull_third(grad_third)
    grad_mixed = grad_mixed.astype(jnp.bfloat16)
    grad_kernel = inner_product(columns, grad_mixed).reshape(kernel.shape)
    grad_bias_conv = jnp.sum(grad_mixed.astype(jnp.float32), axis=0)
    if encoder:
        grad_ext = extended_2(grad_mixed, (("seq", 0),), reach)
        back_front = reach
    else:
        arrived = from_behind(grad_mixed[:reach], "seq", -1)
        grad_ext = jnp.concatenate([grad_mixed, arrived], axis=0)
        back_front = 0
    back_offsets = [-offset for offset in tap_offsets(encoder)]
    back_columns = gather_taps(grad_ext, back_front, back_offsets, back_masks, row_count)
    tap_count = kernel.shape[0]
    kernel_back = jnp.transpose(kernel, (0, 2, 1)).reshape(
        tap_count * kernel.shape[2], kernel.shape[1]
    )
    grad_second = matmul(back_columns, kernel_back)
    unused, pull_second = jax.vjp(norm_silu, hidden_in, gains[0], shifts[0])
    grad_hidden, grad_gain_two, grad_shift_two = pull_second(grad_second)
    grad_hidden = grad_hidden.astype(jnp.bfloat16)
    grad_project = inner_product(first, grad_hidden)
    grad_bias_in = jnp.sum(grad_hidden.astype(jnp.float32), axis=0)
    grad_first = matmul_back(grad_hidden, project)
    unused, pull_first = jax.vjp(norm_silu, stream, wide_gain, wide_shift[0])
    grad_stream, grad_gain_one, grad_shift_one = pull_first(grad_first)
    grads = (
        grad_project,
        grad_kernel,
        grad_expand,
        grad_gain_one,
        jnp.stack([grad_gain_two, grad_gain_three]),
        jnp.stack([grad_shift_one, grad_bias_out]),
        jnp.stack([grad_shift_two, grad_shift_three, grad_bias_in, grad_bias_conv]),
    )
    return (grad_out + grad_stream, grads)


def unpack(gathered, first_index):
    return (
        gathered[first_index],
        gathered[first_index + 1],
        gathered[first_index + 2],
        gathered[first_index + 3].astype(jnp.float32),
        gathered[first_index + 4].astype(jnp.float32),
        gathered[first_index + 5].astype(jnp.float32),
        gathered[first_index + 6].astype(jnp.float32),
    )


def add_arrays(first_arr, second_arr):
    return first_arr + second_arr


def own_share(gradient, axis_dim, own_index, group_size):
    piece_len = gradient.shape[axis_dim] // group_size
    return lax.dynamic_slice_in_dim(gradient, own_index * piece_len, piece_len, axis=axis_dim)


def local(
    characters,
    lengths,
    cotangent,
    encproject,
    enckernel,
    encexpand,
    encwidegain,
    encgains,
    encwideshift,
    encshifts,
    decproject,
    deckernel,
    decexpand,
    decwidegain,
    decgains,
    decwideshift,
    decshifts,
):
    row_count = characters.shape[2]
    stream_len = row_count * lax.axis_size("seq")
    total_rows = characters.shape[0] * stream_len * lax.axis_size("fsdp")
    factor = 1.0 / jnp.sqrt(jnp.float32(total_rows))
    places = lax.axis_index("seq") * row_count + jnp.arange(row_count, dtype=jnp.int32)
    enc_offsets = tap_offsets(True)
    dec_offsets = tap_offsets(False)
    running = None
    outputs = []
    input_grads = []
    for micro_step in range(characters.shape[0]):
        gathered = (
            lax.all_gather(encproject, "fsdp", axis=0, tiled=True),
            lax.all_gather(enckernel, "fsdp", axis=1, tiled=True),
            lax.all_gather(encexpand, "fsdp", axis=0, tiled=True),
            lax.all_gather(encwidegain, "fsdp", axis=0, tiled=True),
            lax.all_gather(encgains, "fsdp", axis=1, tiled=True),
            lax.all_gather(encwideshift, "fsdp", axis=1, tiled=True),
            lax.all_gather(encshifts, "fsdp", axis=1, tiled=True),
            lax.all_gather(decproject, "fsdp", axis=0, tiled=True),
            lax.all_gather(deckernel, "fsdp", axis=1, tiled=True),
            lax.all_gather(decexpand, "fsdp", axis=0, tiled=True),
            lax.all_gather(decwidegain, "fsdp", axis=0, tiled=True),
            lax.all_gather(decgains, "fsdp", axis=1, tiled=True),
            lax.all_gather(decwideshift, "fsdp", axis=1, tiled=True),
            lax.all_gather(decshifts, "fsdp", axis=1, tiled=True),
        )
        doc_ends = jnp.cumsum(lengths[micro_step, 0])
        enc_fwd = build_masks(places, doc_ends, stream_len, enc_offsets)
        dec_fwd = build_masks(places, doc_ends, stream_len, dec_offsets)
        stream = characters[micro_step, 0].astype(jnp.float32)
        middle, enc_stored = forward_block(stream, unpack(gathered, 0), enc_fwd, True)
        final, dec_stored = forward_block(middle, unpack(gathered, 7), dec_fwd, False)
        outputs.append(final.astype(jnp.bfloat16))
        gathered = (
            lax.all_gather(encproject, "fsdp", axis=0, tiled=True),
            lax.all_gather(enckernel, "fsdp", axis=1, tiled=True),
            lax.all_gather(encexpand, "fsdp", axis=0, tiled=True),
            lax.all_gather(encwidegain, "fsdp", axis=0, tiled=True),
            lax.all_gather(encgains, "fsdp", axis=1, tiled=True),
            lax.all_gather(encwideshift, "fsdp", axis=1, tiled=True),
            lax.all_gather(encshifts, "fsdp", axis=1, tiled=True),
            lax.all_gather(decproject, "fsdp", axis=0, tiled=True),
            lax.all_gather(deckernel, "fsdp", axis=1, tiled=True),
            lax.all_gather(decexpand, "fsdp", axis=0, tiled=True),
            lax.all_gather(decwidegain, "fsdp", axis=0, tiled=True),
            lax.all_gather(decgains, "fsdp", axis=1, tiled=True),
            lax.all_gather(decwideshift, "fsdp", axis=1, tiled=True),
            lax.all_gather(decshifts, "fsdp", axis=1, tiled=True),
        )
        enc_back = build_masks(places, doc_ends, stream_len, [-offset for offset in enc_offsets])
        dec_back = build_masks(places, doc_ends, stream_len, [-offset for offset in dec_offsets])
        grad_middle, dec_grads = backward_block(
            cotangent[micro_step, 0].astype(jnp.float32),
            dec_stored,
            unpack(gathered, 7),
            dec_back,
            False,
        )
        grad_stream, enc_grads = backward_block(
            grad_middle, enc_stored, unpack(gathered, 0), enc_back, True
        )
        input_grads.append(grad_stream.astype(jnp.bfloat16))
        step_grads = enc_grads + dec_grads
        if running is None:
            running = step_grads
        else:
            running = jax.tree.map(add_arrays, running, step_grads)
    summed = lax.psum(
        (
            running[0],
            running[1],
            running[2],
            running[3],
            running[4],
            running[5],
            running[6],
            running[7],
            running[8],
            running[9],
            running[10],
            running[11],
            running[12],
            running[13],
        ),
        ("seq", "fsdp"),
    )
    own_index = lax.axis_index("fsdp")
    group_size = lax.axis_size("fsdp")
    shard_dims = (0, 1, 0, 0, 1, 1, 1, 0, 1, 0, 0, 1, 1, 1)
    summed = tuple(
        (
            own_share(gradient, axis_dim, own_index, group_size)
            for gradient, axis_dim in zip(summed, shard_dims)
        )
    )
    summed = tuple((entry * factor for entry in summed))
    output = jnp.stack(outputs)[:, None]
    grad_characters = jnp.stack(input_grads)[:, None]
    return (output, grad_characters) + tuple(summed)


def solution(mesh):
    placed = (
        P(None, "fsdp", "seq", None),
        P(None, "fsdp", None),
        P(None, "fsdp", "seq", None),
        P("fsdp", None),
        P(None, "fsdp", None),
        P("fsdp", None),
        P("fsdp"),
        P(None, "fsdp"),
        P(None, "fsdp"),
        P(None, "fsdp"),
        P("fsdp", None),
        P(None, "fsdp", None),
        P("fsdp", None),
        P("fsdp"),
        P(None, "fsdp"),
        P(None, "fsdp"),
        P(None, "fsdp"),
    )
    return jax.shard_map(
        local,
        mesh=mesh,
        in_specs=placed,
        out_specs=(
            P(None, "fsdp", "seq", None),
            P(None, "fsdp", "seq", None),
            P("fsdp", None),
            P(None, "fsdp", None),
            P("fsdp", None),
            P("fsdp"),
            P(None, "fsdp"),
            P(None, "fsdp"),
            P(None, "fsdp"),
            P("fsdp", None),
            P(None, "fsdp", None),
            P("fsdp", None),
            P("fsdp"),
            P(None, "fsdp"),
            P(None, "fsdp"),
            P(None, "fsdp"),
        ),
        check_vma=False,
    )
```

profile of v0, /device:TPU:0, one launch (start us, length us, event | category | flops | bytes accessed | tf_op | source)
XLA Modules:
  0.0 1773.4 jit_solution(6275527585586401262)
XLA Ops:
  11.3 13.7 all-gather
  25.7 12.2 all-gather.1
  47.1 9.9 all-reduce.4
  57.1 9.2 all-gather.2
  67.4 11.9 all-gather.3
  80.0 14.3 all-gather.4
  94.4 7.9 all-gather.5
  147.5 54.5 %all-gather.15.cloned.1.call-done = bf16[5,800,800]{2,1,0:T(8,128)(2,1)} async-done(((bf16[5,200,800]{2,1,0:T(8,128)(2,1)}), bf16[5,800,800]{2,1,0:T(8,128)(2,1)}) %all-gather.15.cloned.1.call-update) | async-done | bytes 6400016 | tf_op jit(solution)/shard_map/all_gather | solution.py:221
  202.0 10.0 add_reduce_fusion.10
  215.7 8.5 multiply_reduce_fusion.54
  225.0 32.2 %all-gather.17.cloned.1.call-done = bf16[800,1600]{1,0:T(8,128)(2,1)} async-done(((bf16[200,1600]{1,0:T(8,128)(2,1)}), bf16[800,1600]{1,0:T(8,128)(2,1)}) %all-gather.17.cloned.1.call-update) | async-done | bytes 2560016 | tf_op jit(solution)/shard_map/all_gather | solution.py:222
  257.2 4.8 fusion.396
  274.4 41.9 %all-gather.19.cloned.1.call-done = bf16[1600,800]{1,0:T(8,128)(2,1)} async-done(((bf16[400,800]{1,0:T(8,128)(2,1)}), bf16[1600,800]{1,0:T(8,128)(2,1)}) %all-gather.19.cloned.1.call-update) | async-done | bytes 2560016 | tf_op jit(solution)/shard_map/all_gather | solution.py:227
  320.1 4.5 fusion.398
  333.0 4.6 broadcast_select_fusion.4
  342.3 56.7 %all-gather.21.cloned.1.call-done = bf16[3,800,800]{2,1,0:T(8,128)(2,1)} async-done(((bf16[3,200,800]{2,1,0:T(8,128)(2,1)}), bf16[3,800,800]{2,1,0:T(8,128)(2,1)}) %all-gather.21.cloned.1.call-update) | async-done | bytes 3840016 | tf_op jit(solution)/shard_map/all_gather | solution.py:228
  399.0 7.2 copy.99
  415.1 12.7 copy.100
  430.7 5.2 add_reduce_fusion.4
  441.1 6.8 fusion.163
  455.0 6.5 fusion.351
  467.0 5.2 fusion.167
  481.8 5.4 fusion.192
  487.3 5.4 fusion.194
  513.8 5.8 fusion.352
  530.6 14.7 multiply_reduce_fusion.2
  545.4 7.3 fusion.386
  552.7 6.3 convert_reduce_fusion
  573.2 9.0 fusion.412
  582.3 7.0 fusion.411
  589.3 5.2 fusion.343
  594.5 5.3 fusion.342
  599.8 4.5 fusion.415
  612.9 6.2 collective-permute-start.23
  649.5 4.8 fusion.406
  658.0 8.5 fusion.358
  670.1 7.7 fusion.360
  679.3 4.5 fusion.409
  685.3 4.5 fusion.408
  697.3 12.9 fusion.79
  715.3 4.7 collective-permute-start
  740.2 4.9 collective-permute-start.2
  761.9 5.4 fusion.196
  767.4 5.2 fusion.171
  774.1 13.4 add_add_fusion.1
  787.5 8.6 add_add_fusion.4
  796.0 9.9 copy.102
  810.8 5.4 fusion.354
  819.0 4.7 multiply_reduce_fusion.3
  836.4 6.7 fusion.410
  843.1 5.2 fusion.341
  859.5 18.4 %add_add_fusion = f32[4000,800]{0,1:T(8,128)} fusion(f32[4000,800]{0,1:T(8,128)} %fusion.412, f32[4000,800]{0,1:T(8,128)} %fusion.410, f32[4000,800]{0,1:T(8,128)} %fusion.411, bf16[480,4000]{0,1:T(8,128)(2,1)} %copy-done.65, bf16[480,800]{0,1:T(8,128)(2,1)S(1)} %copy-done.2), kind=kOutput, calls=%fused_computation | convolution fusion | flops 3081600000 | bytes 55808000 | tf_op jit(solution)/shard_map/dot_general | solution.py:50
  877.9 9.1 add_add_fusion.5
  889.0 9.4 add_add_fusion.2
  901.9 15.6 copy.101
  922.0 7.5 fusion.362
  932.3 4.5 fusion.407
  937.0 7.0 fusion.42
  950.7 11.6 add_add_fusion.3
  964.3 4.7 fusion.95
  985.5 7.2 fusion.158
  992.8 4.7 fusion.156
  1000.9 74.3 %all-reduce.8.cloned.1.call-done = (f32[1600]{0:T(1024)}, f32[2,800]{1,0:T(2,128)}, f32[2,1600]{1,0:T(2,128)}, f32[4,800]{1,0:T(4,128)}, f32[1600]{0:T(1024)}, /...) async-done(((f32[1600]{0:T(1024)}, f32[2,800]{1,0:T(2,128)}, f32[2,1600]{1,0:T(2,128)}, f32[4,800]{1,0:T(4,128)}, f32[1600]{0:T(1024)}, ...) | async-done | bytes 76816 | tf_op jit(solution)/shard_map/psum | solution.py:276
  1085.9 662.9 %all-reduce.10.cloned.1.call-done = (f32[1600,800]{1,0:T(8,128)}, f32[5,800,800]{2,1,0:T(8,128)}, f32[800,1600]{1,0:T(8,128)}, f32[1600,800]{1,0:T(8,128)}, f32[3,800,800]{2,1,0:T(8,128)}, /*index=5*/f32[800,1600]{1,0:T(8,128)}) async-done(((f32[1600,800]{1,0:T(8,128)}, f32[5,800,800]{2,1,0:T(8,128)}, f32[800,1600]{1,0:T(8,128)}, f32[1600,800]{1,0:T(8,128)}, f32[3,800,800]{2,1,0:T(8,128)}, ...) | async-done | bytes 40960016 | tf_op jit(solution)/shard_map/psum | solution.py:276
  (1219 shorter events, 375.9 us)
Async XLA Ops:
  7.2 102.8 %all-gather.13.cloned.1.call-start = ((), (), s32[]{:S(2)}) async-start(), calls=%async_computation | async-start | bytes 3584000 | tf_op jit(solution)/shard_map/all_gather | solution.py:220
  7.9 194.0 %all-gather.15.cloned.1.call-start = ((), (), s32[]{:S(2)}) async-start(), calls=%async_computation.1 | async-start | bytes 8960000 | tf_op jit(solution)/shard_map/all_gather | solution.py:221
  8.7 248.5 %all-gather.17.cloned.1.call-start = ((), (), s32[]{:S(2)}) async-start(), calls=%async_computation.2 | async-start | bytes 3328000 | tf_op jit(solution)/shard_map/all_gather | solution.py:222
  9.4 306.9 %all-gather.19.cloned.1.call-start = ((), (), s32[]{:S(2)}) async-start(), calls=%async_computation.3 | async-start | bytes 3584000 | tf_op jit(solution)/shard_map/all_gather | solution.py:227
  10.0 389.0 %all-gather.21.cloned.1.call-start = ((), (), s32[]{:S(2)}) async-start(), calls=%async_computation.4 | async-start | bytes 5376000 | tf_op jit(solution)/shard_map/all_gather | solution.py:228
  10.6 444.4 %all-gather.23.cloned.1.call-start = ((), (), s32[]{:S(2)}) async-start(), calls=%async_computation.5 | async-start | bytes 3328000 | tf_op jit(solution)/shard_map/all_gather | solution.py:229
  11.2 1064.0 %all-reduce.8.cloned.1.call-start = ((), (), s32[]{:S(2)}) async-start(), calls=%async_computation.6 | async-start | bytes 172032 | tf_op jit(solution)/shard_map/psum | solution.py:276
  25.7 88.1 %copy-start.141 = (f32[1600]{0:T(1024)}, f32[1600]{0:T(1024)S(1)}, u32[]{:S(2)}) copy-start(f32[1600]{0:T(1024)S(1)} %get-tuple-element.214) | copy-start | bytes 19204
  38.6 82.6 %copy-start.111 = (f32[800]{0:T(1024)}, f32[800]{0:T(1024)S(1)}, u32[]{:S(2)}) copy-start(f32[800]{0:T(1024)S(1)} %get-tuple-element.211) | copy-start | bytes 9604
  38.6 82.6 %copy-start.146 = (f32[800]{0:T(1024)}, f32[800]{0:T(1024)S(1)}, u32[]{:S(2)}) copy-start(f32[800]{0:T(1024)S(1)} %get-tuple-element.210) | copy-start | bytes 9604
  38.6 281.5 %copy-start.126 = (f32[800]{0:T(1024)}, f32[800]{0:T(1024)S(1)}, u32[]{:S(2)}) copy-start(f32[800]{0:T(1024)S(1)} %get-tuple-element.209) | copy-start | bytes 9604
  42.5 71.2 %copy-start.194 = (f32[480]{0:T(512)}, f32[480]{0:T(512)S(1)}, u32[]{:S(2)}) copy-start(f32[480]{0:T(512)S(1)} %broadcast_multiply_fusion.17) | copy-start | bytes 5764
  42.6 60.5 %copy-start.149 = (f32[480]{0:T(512)}, f32[480]{0:T(512)S(1)}, u32[]{:S(2)}) copy-start(f32[480]{0:T(512)S(1)} %get-tuple-element.613) | copy-start | bytes 5764
  42.6 60.5 %copy-start.154 = (f32[480]{0:T(512)}, f32[480]{0:T(512)S(1)}, u32[]{:S(2)}) copy-start(f32[480]{0:T(512)S(1)} %get-tuple-element.614) | copy-start | bytes 5764
  43.4 51.0 %copy-start.349 = (bf16[2,200]{1,0:T(2,128)(2,1)S(1)}, bf16[2,200]{1,0:T(2,128)(2,1)}, u32[]{:S(2)}) copy-start(bf16[2,200]{1,0:T(2,128)(2,1)} %param.31) | copy-start | bytes 2404
  45.3 61.7 %copy-start.157 = (f32[480]{0:T(512)}, f32[480]{0:T(512)S(1)}, u32[]{:S(2)}) copy-start(f32[480]{0:T(512)S(1)} %fusion.297) | copy-start | bytes 5764
  57.0 56.7 %copy-start.118 = (f32[1600]{0:T(1024)}, f32[1600]{0:T(1024)S(1)}, u32[]{:S(2)}) copy-start(f32[1600]{0:T(1024)S(1)} %convert_element_type.480) | copy-start | bytes 19204
  57.0 50.0 %copy-start.197 = (f32[480]{0:T(512)}, f32[480]{0:T(512)S(1)}, u32[]{:S(2)}) copy-start(f32[480]{0:T(512)S(1)} %fusion.291) | copy-start | bytes 5764
  57.1 56.7 %copy-start.299 = (f32[480]{0:T(512)}, f32[480]{0:T(512)S(1)}, u32[]{:S(2)}) copy-start(f32[480]{0:T(512)S(1)} %fusion.303) | copy-start | bytes 5764
  66.4 54.8 %copy-start.123 = (f32[800]{0:T(1024)}, f32[800]{0:T(1024)S(1)}, u32[]{:S(2)}) copy-start(f32[800]{0:T(1024)S(1)} %get-tuple-element.235) | copy-start | bytes 9604
  66.4 253.6 %copy-start.137 = (f32[800]{0:T(1024)}, f32[800]{0:T(1024)S(1)}, u32[]{:S(2)}) copy-start(f32[800]{0:T(1024)S(1)} %get-tuple-element.234) | copy-start | bytes 9604
  80.0 450.6 %copy-start.139 = (f32[1600]{0:T(1024)}, f32[1600]{0:T(1024)S(1)}, u32[]{:S(2)}) copy-start(f32[1600]{0:T(1024)S(1)} %get-tuple-element.212) | copy-start | bytes 19204
  102.4 442.9 %copy-start.121 = (f32[1600]{0:T(1024)}, f32[1600]{0:T(1024)S(1)}, u32[]{:S(2)}) copy-start(f32[1600]{0:T(1024)S(1)} %convert_element_type.491) | copy-start | bytes 19204
  103.1 377.0 %copy-start.114 = (f32[800]{0:T(1024)}, f32[800]{0:T(1024)S(1)}, u32[]{:S(2)}) copy-start(f32[800]{0:T(1024)S(1)} %get-tuple-element.205) | copy-start | bytes 9604
  103.1 377.0 %copy-start.130 = (f32[800]{0:T(1024)}, f32[800]{0:T(1024)S(1)}, u32[]{:S(2)}) copy-start(f32[800]{0:T(1024)S(1)} %get-tuple-element.622) | copy-start | bytes 9604
  103.1 418.0 %copy-start.116 = (f32[800]{0:T(1024)}, f32[800]{0:T(1024)S(1)}, u32[]{:S(2)}) copy-start(f32[800]{0:T(1024)S(1)} %get-tuple-element.207) | copy-start | bytes 9604
  103.1 418.0 %copy-start.128 = (f32[800]{0:T(1024)}, f32[800]{0:T(1024)S(1)}, u32[]{:S(2)}) copy-start(f32[800]{0:T(1024)S(1)} %get-tuple-element.621) | copy-start | bytes 9604
  123.7 7.7 collective-permute-start.9
  125.2 9.3 collective-permute-start.3
  126.9 9.2 collective-permute-start.6
  128.8 11.9 collective-permute-start.4
  130.1 11.5 collective-permute-start.10
  131.4 13.4 collective-permute-start.7
  212.0 50.7 %copy-start.55 = (f32[480,800]{0,1:T(8,128)}, f32[480,800]{0,1:T(8,128)S(1)}, u32[]{:S(2)}) copy-start(f32[480,800]{0,1:T(8,128)S(1)} %get-tuple-element.583) | copy-start | bytes 4608004
  212.0 50.6 %copy-start.241 = (f32[480]{0:T(512)}, f32[480]{0:T(512)S(1)}, u32[]{:S(2)}) copy-start(f32[480]{0:T(512)S(1)} %broadcast_multiply_fusion.10) | copy-start | bytes 5764
  224.3 38.4 %copy-start.306 = (f32[480]{0:T(512)}, f32[480]{0:T(512)S(1)}, u32[]{:S(2)}) copy-start(f32[480]{0:T(512)S(1)} %get-tuple-element.242) | copy-start | bytes 5764
  224.3 95.8 %copy-start.162 = (f32[480]{0:T(512)}, f32[480]{0:T(512)S(1)}, u32[]{:S(2)}) copy-start(f32[480]{0:T(512)S(1)} %broadcast_multiply_fusion.2) | copy-start | bytes 5764
  225.0 95.1 %copy-start.204 = (f32[480]{0:T(512)}, f32[480]{0:T(512)S(1)}, u32[]{:S(2)}) copy-start(f32[480]{0:T(512)S(1)} %fusion.305) | copy-start | bytes 5764
  274.4 45.6 %copy-start.82 = (bf16[480,1600]{1,0:T(8,128)(2,1)}, bf16[480,1600]{1,0:T(8,128)(2,1)S(1)}, u32[]{:S(2)}) copy-start(bf16[480,1600]{1,0:T(8,128)(2,1)S(1)} %get-tuple-element.511) | copy-start | bytes 4608004
  324.6 220.8 %copy-start.5 = (f32[480,1600]{1,0:T(8,128)}, f32[480,1600]{1,0:T(8,128)S(1)}, u32[]{:S(2)}) copy-start(f32[480,1600]{1,0:T(8,128)S(1)} %get-tuple-element.592) | copy-start | bytes 9216004
  324.6 220.8 %copy-start.165 = (f32[480]{0:T(512)}, f32[480]{0:T(512)S(1)}, u32[]{:S(2)}) copy-start(f32[480]{0:T(512)S(1)} %broadcast_multiply_fusion.16) | copy-start | bytes 5764
  327.7 217.7 %copy-start.207 = (f32[480]{0:T(512)}, f32[480]{0:T(512)S(1)}, u32[]{:S(2)}) copy-start(f32[480]{0:T(512)S(1)} %fusion.306) | copy-start | bytes 5764
  339.4 88.5 %collective-permute-start.8 = (bf16[32,800]{0,1:T(8,128)(2,1)}, bf16[32,800]{0,1:T(8,128)(2,1)}, u32[]{:S(2)}, u32[]{:S(2)}) collective-permute-start(bf16[32,800]{0,1:T(8,128)(2,1)} %slice.560), channel_id=1, source_target_pairs={{0,4},{4,8},{8,12},{12,16},{16,20},{20,24},{24,28},{1,5},{5,9},{9,... | collective-permute-start | bytes 153608 | tf_op jit(solution)/shard_map/ppermute | solution.py:35
  408.0 28.3 %collective-permute-start.5 = (bf16[32,800]{0,1:T(8,128)(2,1)}, bf16[32,800]{0,1:T(8,128)(2,1)}, u32[]{:S(2)}, u32[]{:S(2)}) collective-permute-start(bf16[32,800]{0,1:T(8,128)(2,1)} %slice.551), channel_id=1, source_target_pairs={{0,4},{4,8},{8,12},{12,16},{16,20},{20,24},{24,28},{1,5},{5,9},{9,... | collective-permute-start | bytes 153608 | tf_op jit(solution)/shard_map/ppermute | solution.py:35
  412.2 27.4 %collective-permute-start.11 = (bf16[32,800]{0,1:T(8,128)(2,1)}, bf16[32,800]{0,1:T(8,128)(2,1)S(1)}, u32[]{:S(2)}, u32[]{:S(2)}) collective-permute-start(bf16[32,800]{0,1:T(8,128)(2,1)} %slice.569), channel_id=1, source_target_pairs={{0,4},{4,8},{8,12},{12,16},{16,20},{20,24},{24,28},{1,5},{5,9},{9,... | collective-permute-start | bytes 153608 | tf_op jit(solution)/shard_map/ppermute | solution.py:35
  436.0 40.6 %copy-start.235 = (f32[480]{0:T(512)}, f32[480]{0:T(512)S(1)}, u32[]{:S(2)}) copy-start(f32[480]{0:T(512)S(1)} %broadcast_multiply_fusion.4) | copy-start | bytes 5764
  477.9 23.1 %collective-permute-start.21 = (bf16[32,800]{0,1:T(8,128)(2,1)S(1)}, bf16[32,800]{0,1:T(8,128)(2,1)S(1)}, u32[]{:S(2)}, u32[]{:S(2)}) collective-permute-start(bf16[32,800]{0,1:T(8,128)(2,1)S(1)} %slice.599), channel_id=1, source_target_pairs={{4,0},{8,4},{12,8},{16,12},{20,16},{24,20},{28,24},{5,1},{9,5},{13... | collective-permute-start | bytes 153608 | tf_op jit(solution)/shard_map/ppermute | solution.py:35
  492.7 13.4 collective-permute-start.18
  494.0 17.8 %collective-permute-start.15 = (bf16[32,800]{0,1:T(8,128)(2,1)S(1)}, bf16[32,800]{0,1:T(8,128)(2,1)S(1)}, u32[]{:S(2)}, u32[]{:S(2)}) collective-permute-start(bf16[32,800]{0,1:T(8,128)(2,1)S(1)} %slice.581), channel_id=1, source_target_pairs={{4,0},{8,4},{12,8},{16,12},{20,16},{24,20},{28,24},{5,1},{9,5},{13... | collective-permute-start | bytes 153608 | tf_op jit(solution)/shard_map/ppermute | solution.py:35
  571.7 76.7 %copy-start.1 = (bf16[480,800]{0,1:T(8,128)(2,1)}, bf16[480,800]{0,1:T(8,128)(2,1)S(1)}, u32[]{:S(2)}) copy-start(bf16[480,800]{0,1:T(8,128)(2,1)S(1)} %get-tuple-element.532) | copy-start | bytes 2304004
  608.8 30.6 %collective-permute-start.16 = (bf16[16,800]{0,1:T(8,128)(2,1)S(1)}, bf16[16,800]{0,1:T(8,128)(2,1)S(1)}, u32[]{:S(2)}, u32[]{:S(2)}) collective-permute-start(bf16[16,800]{0,1:T(8,128)(2,1)S(1)} %get-tuple-element.488), channel_id=1, source_target_pairs={{4,0},{8,4},{12,8},{16,12},{20,16},{24,20},{28,24},{5,1},{9,5},{13... | collective-permute-start | bytes 76808 | tf_op jit(solution)/shard_map/ppermute | solution.py:25
  610.2 32.7 %collective-permute-start.19 = (bf16[16,800]{0,1:T(8,128)(2,1)S(1)}, bf16[16,800]{0,1:T(8,128)(2,1)S(1)}, u32[]{:S(2)}, u32[]{:S(2)}) collective-permute-start(bf16[16,800]{0,1:T(8,128)(2,1)S(1)} %get-tuple-element.490), channel_id=1, source_target_pairs={{4,0},{8,4},{12,8},{16,12},{20,16},{24,20},{28,24},{5,1},{9,5},{13... | collective-permute-start | bytes 76808 | tf_op jit(solution)/shard_map/ppermute | solution.py:25
  611.6 33.9 %collective-permute-start.22 = (bf16[16,800]{0,1:T(8,128)(2,1)S(1)}, bf16[16,800]{0,1:T(8,128)(2,1)S(1)}, u32[]{:S(2)}, u32[]{:S(2)}) collective-permute-start(bf16[16,800]{0,1:T(8,128)(2,1)S(1)} %get-tuple-element.492), channel_id=1, source_target_pairs={{4,0},{8,4},{12,8},{16,12},{20,16},{24,20},{28,24},{5,1},{9,5},{13... | collective-permute-start | bytes 76808 | tf_op jit(solution)/shard_map/ppermute | solution.py:25
  612.9 34.9 %collective-permute-start.23 = (bf16[16,800]{0,1:T(8,128)(2,1)S(1)}, bf16[16,800]{0,1:T(8,128)(2,1)S(1)}, u32[]{:S(2)}, u32[]{:S(2)}) collective-permute-start(bf16[16,800]{0,1:T(8,128)(2,1)S(1)} %get-tuple-element.491), channel_id=1, source_target_pairs={{0,4},{4,8},{8,12},{12,16},{16,20},{20,24},{24,28},{1,5},{5,9},{9,... | collective-permute-start | bytes 76808 | tf_op jit(solution)/shard_map/ppermute | solution.py:23
  619.1 35.3 %collective-permute-start.20 = (bf16[16,800]{0,1:T(8,128)(2,1)S(1)}, bf16[16,800]{0,1:T(8,128)(2,1)S(1)}, u32[]{:S(2)}, u32[]{:S(2)}) collective-permute-start(bf16[16,800]{0,1:T(8,128)(2,1)S(1)} %get-tuple-element.489), channel_id=1, source_target_pairs={{0,4},{4,8},{8,12},{12,16},{16,20},{20,24},{24,28},{1,5},{5,9},{9,... | collective-permute-start | bytes 76808 | tf_op jit(solution)/shard_map/ppermute | solution.py:23
  639.4 27.2 %collective-permute-start.17 = (bf16[16,800]{0,1:T(8,128)(2,1)S(1)}, bf16[16,800]{0,1:T(8,128)(2,1)S(1)}, u32[]{:S(2)}, u32[]{:S(2)}) collective-permute-start(bf16[16,800]{0,1:T(8,128)(2,1)S(1)} %get-tuple-element.487), channel_id=1, source_target_pairs={{0,4},{4,8},{8,12},{12,16},{16,20},{20,24},{24,28},{1,5},{5,9},{9,... | collective-permute-start | bytes 76808 | tf_op jit(solution)/shard_map/ppermute | solution.py:23
  715.3 7.6 collective-permute-start
  720.0 4.6 collective-permute-start.1
  733.0 90.8 %copy-start.20 = (f32[480,1600]{1,0:T(8,128)}, f32[480,1600]{1,0:T(8,128)S(1)}, u32[]{:S(2)}) copy-start(f32[480,1600]{1,0:T(8,128)S(1)} %get-tuple-element.606) | copy-start | bytes 9216004
  740.2 12.0 collective-permute-start.2
  772.6 35.1 %collective-permute-start.12 = (bf16[32,800]{0,1:T(8,128)(2,1)S(1)}, bf16[32,800]{0,1:T(8,128)(2,1)}, u32[]{:S(2)}, u32[]{:S(2)}) collective-permute-start(bf16[32,800]{0,1:T(8,128)(2,1)S(1)} %slice.572), channel_id=1, source_target_pairs={{4,0},{8,4},{12,8},{16,12},{20,16},{24,20},{28,24},{5,1},{9,5},{13... | collective-permute-start | bytes 153608 | tf_op jit(solution)/shard_map/ppermute | solution.py:35
  852.7 64.9 %collective-permute-start.13 = (bf16[16,800]{0,1:T(8,128)(2,1)}, bf16[16,800]{0,1:T(8,128)(2,1)}, u32[]{:S(2)}, u32[]{:S(2)}) collective-permute-start(bf16[16,800]{0,1:T(8,128)(2,1)} %get-tuple-element.483), channel_id=1, source_target_pairs={{4,0},{8,4},{12,8},{16,12},{20,16},{24,20},{28,24},{5,1},{9,5},{13... | collective-permute-start | bytes 76808 | tf_op jit(solution)/shard_map/ppermute | solution.py:25
  854.0 66.6 %collective-permute-start.14 = (bf16[16,800]{0,1:T(8,128)(2,1)}, bf16[16,800]{0,1:T(8,128)(2,1)S(1)}, u32[]{:S(2)}, u32[]{:S(2)}) collective-permute-start(bf16[16,800]{0,1:T(8,128)(2,1)} %get-tuple-element.482), channel_id=1, source_target_pairs={{0,4},{4,8},{8,12},{12,16},{16,20},{20,24},{24,28},{1,5},{5,9},{9,... | collective-permute-start | bytes 76808 | tf_op jit(solution)/shard_map/ppermute | solution.py:23
  950.5 798.4 %all-reduce.10.cloned.1.call-start = ((), (), s32[]{:S(2)}) async-start(), calls=%async_computation.7 | async-start | bytes 90112000 | tf_op jit(solution)/shard_map/psum | solution.py:276
  (358 other events, 2728.5 us)
Sparse Core Ops, SparseCore 0:
  9.6 62.2 all-gather.12
  73.5 128.4 all-gather.14
  203.5 53.6 all-gather.16
  258.6 57.6 all-gather.18
  317.8 81.1 all-gather.20
  400.5 53.9 all-gather.22
  950.6 124.5 all-reduce.7
  1082.7 666.1 all-reduce.9
where the time goes:
time: 1780 us; the launch traced here: 1770 us
  waiting for transfers between devices  926 us (52%)
  matrix products  396 us (22%)
  other arithmetic  176 us (10%)
  local copies, waits for them, and re-layouts  119 us (7%)
  blocking collectives  79 us (4%)
  starting transfers between devices  55.5 us (3%)
  between operations  21 us (1%)
    psum x2, waiting for transfers between devices, local(): lax.psum((running[0], running[1], running[2], running[3], running[4], run...  737 us
    dot_general x24, matrix products, inner_product(): lax.dot_general(factor, matrix, (((0,), (0,)), ((), ())), preferred_eleme...  169 us
    dot_general x32, matrix products, matmul(): return jnp.dot(factor, matrix, preferred_element_type=jnp.float32)  141 us
    dot_general x16, matrix products, matmul_back(): lax.dot_general(factor, matrix, (((1,), (1,)), ((), ())), preferred_eleme...  85.8 us
    all_gather x1, waiting for transfers between devices, local(): lax.all_gather(deckernel, 'fsdp', axis=1, tiled=True)  56.7 us
    all_gather x1, waiting for transfers between devices, local(): lax.all_gather(enckernel, 'fsdp', axis=1, tiled=True)  54.5 us
    all_gather x1, waiting for transfers between devices, local(): lax.all_gather(decproject, 'fsdp', axis=0, tiled=True)  41.9 us
  transfers between devices with their start and end apart: 32, of which 6 were waited for; matrix products, arithmetic and copies ran while one was open for 21% of the time, Pallas kernels for 0%

commit v1 on v0

v1 whole, which is shorter than its diff:
```python
import jax
import jax.numpy as jnp
from jax import lax
from jax.experimental import pallas as pl
from jax.experimental.pallas import tpu as pltpu
from jax.sharding import PartitionSpec as P

ENC_TAPS = 5
ENC_DILATION = 8
DEC_TAPS = 3
DEC_DILATION = 16
EPSILON = 1e-05
CHUNK = 48
VMEM_LIMIT = 60 * 1024 * 1024

BF16 = jnp.bfloat16
F32 = jnp.float32
NN = (((1,), (0,)), ((), ()))
NT = (((1,), (1,)), ((), ()))
TN = (((0,), (0,)), ((), ()))


def dot(left, right, dims):
    return lax.dot_general(left, right, dims, preferred_element_type=F32)


def tap_offsets(encoder):
    if encoder:
        return [(tap - ENC_TAPS // 2) * ENC_DILATION for tap in range(ENC_TAPS)]
    return [(tap - DEC_TAPS + 1) * DEC_DILATION for tap in range(DEC_TAPS)]


def normalized(values):
    average = jnp.mean(values, axis=-1, keepdims=True)
    centred = values - average
    scale = lax.rsqrt(jnp.mean(centred * centred, axis=-1, keepdims=True) + EPSILON)
    return centred * scale, scale


def logistic(inner):
    return 0.5 * jnp.tanh(0.5 * inner) + 0.5


def norm_silu(values, gain, shift):
    unit, _ = normalized(values)
    inner = unit * gain + shift
    return inner * logistic(inner)


def norm_silu_back(values, gain, shift, grad):
    unit, scale = normalized(values)
    inner = unit * gain + shift
    gate = logistic(inner)
    grad_inner = grad * (gate + inner * gate * (1.0 - gate))
    grad_unit = grad_inner * gain
    along = jnp.mean(grad_unit * unit, axis=-1, keepdims=True)
    level = jnp.mean(grad_unit, axis=-1, keepdims=True)
    grad_values = scale * (grad_unit - level - unit * along)
    return grad_values, grad_inner * unit, grad_inner


def fold_rows(values):
    total = values[0:8]
    for start in range(8, values.shape[0], 8):
        total = total + values[start : start + 8]
    return total


def by_chunks(row_count, body):
    for start in range(0, row_count, CHUNK):
        body(pl.ds(start, CHUNK))


def clear_first(*refs):
    @pl.when(pl.program_id(0) == 0)
    def _():
        for ref in refs:
            ref[...] = jnp.zeros_like(ref)


def at_last(body):
    pl.when(pl.program_id(0) == pl.num_programs(0) - 1)(body)


def fill_columns(columns, extended, masks, offsets, front, row_count):
    width = extended.shape[-1]
    for tap, offset in enumerate(offsets):
        window = extended[front + offset : front + offset + row_count, :]
        if offset != 0:
            window = window * masks[:, tap : tap + 1]
        columns[:, tap * width : (tap + 1) * width] = window


def enter_kernel(stream, project, wide, inner, first, hidden, second):
    row_count = stream.shape[0]

    def make_first(rows):
        values = stream[rows, :].astype(F32)
        first[rows, :] = norm_silu(values, wide[0:1, :], wide[1:2, :]).astype(BF16)

    by_chunks(row_count, make_first)
    hidden[...] = dot(first[...], project[...], NN) + inner[4:5, :]

    def make_second(rows):
        second[rows, :] = norm_silu(hidden[rows, :], inner[0:1, :], inner[2:3, :]).astype(BF16)

    by_chunks(row_count, make_second)


def fetch(sources, spots, target, semaphores):
    copies = [
        pltpu.make_async_copy(source, target.at[spot], semaphores.at[index])
        for index, (source, spot) in enumerate(zip(sources, spots))
    ]
    for copy in copies:
        copy.start()
    for copy in copies:
        copy.wait()


def fetch_shards(place, pieces, fsdp_count, landed, semaphores):
    seq_count = len(pieces) // 2
    half_count = fsdp_count // 2
    sources, spots = [], []
    for index, piece in enumerate(pieces):
        half, differs = index // seq_count, index % seq_count
        for within in range(half_count):
            shard = place[0] ^ (half * half_count + within)
            sources.append(piece.at[within])
            spots.append(shard * seq_count + (place[2] ^ differs))
    fetch(sources, spots, landed, semaphores)


class Shards:
    def __init__(self, landed, fsdp_count):
        self.landed, self.fsdp_count = landed, fsdp_count
        self.seq_count = landed.shape[0] // fsdp_count

    def spread(self, shard, start, rows, write):
        part, done = self.landed.shape[1], 0
        while done < rows:
            owner, local = (start + done) // part, (start + done) % part
            size = min(rows - done, part - local)
            write(done, self.landed[shard * self.seq_count + owner, local : local + size, :])
            done += size


def enter_encoder_kernel(parts, spacing, place, *refs):
    refs = list(refs)
    stream = refs.pop(0)
    pieces = [refs.pop(0) for _ in range(len(refs) - 8)]
    wide, inner, first, hidden, second, project, landed, semaphores = refs
    shard_rows = project.shape[0] * parts // len(pieces)

    @pl.when(pl.program_id(0) == 0)
    def _():
        spots = [
            (place[0] ^ (index // parts)) * parts + (place[1] ^ (index % parts))
            for index in range(len(pieces))
        ]
        fetch(pieces, spots, landed, semaphores)
        for index in range(len(pieces)):
            start = index // parts * shard_rows + index % parts * spacing
            project[start : start + landed.shape[1], :] = landed[index]

    enter_kernel(stream, project, wide, inner, first, hidden, second)


def unpack_kernel(shards, start, taps, kernel, flat):
    width = flat.shape[0]
    part = width // shards.fsdp_count
    for own in range(shards.fsdp_count):
        for tap in range(taps):

            def write(done, block):
                row = own * part + done
                size = block.shape[0]
                kernel[tap * width + row : tap * width + row + size, :] = block
                flat[row : row + size, tap * width : (tap + 1) * width] = block

            shards.spread(own, start + tap * part, part, write)


def unpack_expand(shards, start, expand):
    width = expand.shape[1] // 2
    part = expand.shape[0] // shards.fsdp_count
    for own in range(shards.fsdp_count):
        for half in range(2):

            def write(done, block):
                row = own * part + done
                expand[row : row + block.shape[0], half * width : (half + 1) * width] = block

            shards.spread(own, start + half * part, part, write)


def unpack_rows(shards, start, whole):
    part = whole.shape[0] // shards.fsdp_count
    for own in range(shards.fsdp_count):

        def write(done, block):
            row = own * part + done
            whole[row : row + block.shape[0], :] = block

        shards.spread(own, start, part, write)


def middle_kernel(offsets, fsdp_count, place, second_in, low, high, masks, stream, *refs):
    pieces, refs = refs[:-12], refs[-12:]
    enc_wide, enc_inner, mixed, third, middle, expand, flat = refs[:7]
    extended, columns, kernel, landed, semaphores = refs[7:]
    row_count = stream.shape[0]
    front = low.shape[0]

    @pl.when(pl.program_id(0) == 0)
    def _():
        fetch_shards(place, pieces, fsdp_count, landed, semaphores)
        shards = Shards(landed, fsdp_count)
        unpack_kernel(shards, 0, len(offsets), kernel, flat)
        unpack_expand(shards, kernel.shape[0] // fsdp_count, expand)

    extended[:front, :] = low[...]
    extended[front : front + row_count, :] = second_in[...]
    extended[front + row_count :, :] = high[...]
    fill_columns(columns, extended, masks, offsets, front, row_count)
    mixed[...] = dot(columns[...], kernel[...], NN) + enc_inner[5:6, :]

    def make_third(rows):
        third[rows, :] = norm_silu(mixed[rows, :], enc_inner[1:2, :], enc_inner[3:4, :]).astype(
            BF16
        )

    by_chunks(row_count, make_third)
    middle[...] = dot(third[...], expand[...], NN)

    def make_middle(rows):
        branch = middle[rows, :] + enc_wide[2:3, :]
        middle[rows, :] = stream[rows, :].astype(F32) + branch

    by_chunks(row_count, make_middle)


def enter_decoder_kernel(taps, fsdp_count, place, stream, *refs):
    pieces, refs = refs[:-11], refs[-11:]
    wide, inner, first, hidden, second, project, kernel, flat, expand, landed, semaphores = refs

    @pl.when(pl.program_id(0) == 0)
    def _():
        fetch_shards(place, pieces, fsdp_count, landed, semaphores)
        shards = Shards(landed, fsdp_count)
        start = project.shape[0] // fsdp_count
        unpack_rows(shards, 0, project)
        unpack_kernel(shards, start, taps, kernel, flat)
        unpack_expand(shards, start + kernel.shape[0] // fsdp_count, expand)

    enter_kernel(stream, project, wide, inner, first, hidden, second)


def turn_kernel(
    offsets,
    second,
    low,
    masks,
    cotangent,
    kernel,
    expand,
    inner,
    third,
    grad_mixed,
    grad_expand,
    sums_wide,
    sums_inner,
    extended,
    columns,
    mixed,
    grad_third,
    total,
):
    row_count = cotangent.shape[0]
    front = low.shape[0]
    clear_first(total, sums_wide, sums_inner)
    extended[:front, :] = low[...]
    extended[front : front + row_count, :] = second[...]
    fill_columns(columns, extended, masks, offsets, front, row_count)
    mixed[...] = dot(columns[...], kernel[...], NN) + inner[5:6, :]

    def make_third(rows):
        third[rows, :] = norm_silu(mixed[rows, :], inner[1:2, :], inner[3:4, :]).astype(BF16)

    by_chunks(row_count, make_third)
    grad_third[...] = dot(cotangent[...], expand[...], NT)

    def add_cotangent(rows):
        sums_wide[0] += fold_rows(cotangent[rows, :].astype(F32))

    by_chunks(row_count, add_cotangent)

    def make_grad(rows):
        grad, gain_part, shift_part = norm_silu_back(
            mixed[rows, :], inner[1:2, :], inner[3:4, :], grad_third[rows, :]
        )
        rounded = grad.astype(BF16)
        grad_mixed[rows, :] = rounded
        sums_inner[0] += fold_rows(gain_part)
        sums_inner[1] += fold_rows(shift_part)
        sums_inner[2] += fold_rows(rounded.astype(F32))

    by_chunks(row_count, make_grad)
    total[...] += dot(third[...], cotangent[...], TN)

    @at_last
    def _():
        grad_expand[...] = total[...].astype(BF16)


def routes(seq_count):
    rest = [1 << bit for bit in range(1, seq_count.bit_length() - 1)]
    return rest[::-1], rest


def pack(place, sections, keep, send):
    seq_count, fsdp_count, part = sections.seq_count, sections.fsdp_count, keep.shape[1]
    orders = routes(seq_count)
    cells = keep.shape[0] // 2

    def write(own_core):
        for shard in range(fsdp_count):
            far = place[0] ^ shard
            half = far // (fsdp_count // 2)
            within = far % (fsdp_count // 2)
            for owner in range(seq_count):
                differs = place[2] ^ owner
                spots = []
                for order in orders:
                    spot = 0
                    for bit in order:
                        spot = spot * 2 + (differs // bit) % 2
                    spots.append(spot)
                spot = jnp.where(half == 0, spots[0], spots[1])
                spot = half * cells + spot * (fsdp_count // 2) + within
                target = keep if owner % 2 == own_core else send
                filled = 0
                for start, rows, block in sections.cut(owner * part, part):
                    target[spot, filled : filled + rows, :] = block(shard, start, rows)
                    filled += rows
                if filled < part:
                    target[spot, filled:, :] = jnp.zeros((part - filled, keep.shape[2]), BF16)

    for own_core in range(2):

        @pl.when(place[2] % 2 == own_core)
        def _():
            write(own_core)


class Sections:
    def __init__(self, seq_count, fsdp_count):
        self.seq_count, self.fsdp_count = seq_count, fsdp_count
        self.entries = []

    def add(self, rows, block):
        self.entries.append((rows, block))

    def rows_of(self, total):
        part = total.shape[0] // self.fsdp_count
        self.add(
            part,
            lambda shard, start, rows: total[
                shard * part + start : shard * part + start + rows, :
            ].astype(BF16),
        )

    def kernel(self, total, taps):
        part, width = total.shape[0] // self.fsdp_count, total.shape[1] // taps
        for tap in range(taps):
            self.add(
                part,
                lambda shard, start, rows, tap=tap: total[
                    shard * part + start : shard * part + start + rows,
                    tap * width : (tap + 1) * width,
                ].astype(BF16),
            )

    def cut(self, first, rows):
        found, begin = [], 0
        for length, block in self.entries:
            low, high = max(first, begin), min(first + rows, begin + length)
            if low < high:
                found.append((low - begin, high - low, block))
            begin += length
        return found


def back_columns(offsets, front, back, grad_mixed, low, high, masks, extended, columns):
    row_count = grad_mixed.shape[0]
    if front:
        extended[:front, :] = low[...]
    extended[front : front + row_count, :] = grad_mixed[...]
    if back:
        extended[front + row_count :, :] = high[...]
    fill_columns(columns, extended, masks, offsets, front, row_count)


def hidden_grad(hidden, inner, grad_second, grad_hidden, sums_inner):
    def make_grad(rows):
        grad, gain_part, shift_part = norm_silu_back(
            hidden[rows, :], inner[0:1, :], inner[2:3, :], grad_second[rows, :]
        )
        rounded = grad.astype(BF16)
        grad_hidden[rows, :] = rounded
        sums_inner[0] += fold_rows(gain_part)
        sums_inner[1] += fold_rows(shift_part)
        sums_inner[2] += fold_rows(rounded.astype(F32))

    by_chunks(hidden.shape[0], make_grad)


def decoder_back_kernel(
    offsets,
    back,
    counts,
    place,
    grad_mixed,
    high,
    masks,
    second,
    hidden,
    first,
    flat,
    inner,
    grad_expand,
    grad_hidden,
    keep,
    send,
    sums_inner,
    extended,
    columns,
    grad_second,
    total_kernel,
    total_project,
):
    clear_first(total_kernel, total_project, sums_inner)
    back_columns(offsets, 0, back, grad_mixed, None, high, masks, extended, columns)
    grad_second[...] = dot(columns[...], flat[...], NT)
    hidden_grad(hidden, inner, grad_second, grad_hidden, sums_inner)
    total_kernel[...] += dot(second[...], columns[...], TN)
    total_project[...] += dot(first[...], grad_hidden[...], TN)

    @at_last
    def _():
        sections = Sections(*counts)
        sections.rows_of(total_project)
        sections.kernel(total_kernel, len(offsets))
        sections.kernel(grad_expand, 2)
        pack(place, sections, keep, send)


def encoder_kernel_grad_kernel(
    offsets,
    front,
    back,
    counts,
    place,
    grad_mixed,
    low,
    high,
    masks,
    second,
    grad_expand,
    keep,
    send,
    extended,
    columns,
    total_kernel,
):
    clear_first(total_kernel)
    back_columns(offsets, front, back, grad_mixed, low, high, masks, extended, columns)
    total_kernel[...] += dot(second[...], columns[...], TN)

    @at_last
    def _():
        sections = Sections(*counts)
        sections.kernel(total_kernel, len(offsets))
        sections.kernel(grad_expand, 2)
        pack(place, sections, keep, send)


def encoder_back_kernel(
    offsets,
    front,
    back,
    counts,
    place,
    grad_mixed,
    low,
    high,
    masks,
    hidden,
    first,
    flat,
    inner,
    grad_hidden,
    keep,
    send,
    sums_inner,
    extended,
    columns,
    grad_second,
    total_project,
):
    clear_first(total_project, sums_inner)
    back_columns(offsets, front, back, grad_mixed, low, high, masks, extended, columns)
    grad_second[...] = dot(columns[...], flat[...], NT)
    hidden_grad(hidden, inner, grad_second, grad_hidden, sums_inner)
    total_project[...] += dot(first[...], grad_hidden[...], TN)

    @at_last
    def _():
        sections = Sections(*counts)
        sections.rows_of(total_project)
        pack(place, sections, keep, send)


def link_back_kernel(
    grad_hidden,
    middle,
    cotangent,
    mixed,
    third,
    project,
    dec_wide,
    expand,
    enc_inner,
    grad_middle,
    grad_mixed,
    grad_expand,
    sums_wide,
    sums_inner,
    grad_first,
    branch,
    grad_third,
    total,
):
    row_count = middle.shape[0]
    clear_first(total, sums_wide, sums_inner)
    grad_first[...] = dot(grad_hidden[...], project[...], NT)

    def make_branch(rows):
        grad, gain_part, shift_part = norm_silu_back(
            middle[rows, :], dec_wide[0:1, :], dec_wide[1:2, :], grad_first[rows, :]
        )
        sums_wide[0] += fold_rows(gain_part)
        sums_wide[1] += fold_rows(shift_part)
        grad = cotangent[rows, :].astype(F32) + grad
        grad_middle[rows, :] = grad
        rounded = grad.astype(BF16)
        branch[rows, :] = rounded
        sums_wide[2] += fold_rows(rounded.astype(F32))

    by_chunks(row_count, make_branch)
    grad_third[...] = dot(branch[...], expand[...], NT)

    def make_grad(rows):
        grad, gain_part, shift_part = norm_silu_back(
            mixed[rows, :], enc_inner[1:2, :], enc_inner[3:4, :], grad_third[rows, :]
        )
        rounded = grad.astype(BF16)
        grad_mixed[rows, :] = rounded
        sums_inner[0] += fold_rows(gain_part)
        sums_inner[1] += fold_rows(shift_part)
        sums_inner[2] += fold_rows(rounded.astype(F32))

    by_chunks(row_count, make_grad)
    total[...] += dot(third[...], branch[...], TN)

    @at_last
    def _():
        grad_expand[...] = total[...].astype(BF16)


def output_kernel(third, middle, expand, wide, output, branch):
    branch[...] = dot(third[...], expand[...], NN)

    def make_output(rows):
        values = middle[rows, :] + (branch[rows, :] + wide[2:3, :])
        output[rows, :] = values.astype(BF16)

    by_chunks(middle.shape[0], make_output)


def leave_kernel(
    grad_hidden, stream, grad_middle, project, wide, grad_stream, sums_wide, grad_first
):
    row_count = stream.shape[0]
    clear_first(sums_wide)
    grad_first[...] = dot(grad_hidden[...], project[...], NT)

    def make_grad(rows):
        grad, gain_part, shift_part = norm_silu_back(
            stream[rows, :].astype(F32), wide[0:1, :], wide[1:2, :], grad_first[rows, :]
        )
        sums_wide[0] += fold_rows(gain_part)
        sums_wide[1] += fold_rows(shift_part)
        grad_stream[rows, :] = (grad_middle[rows, :] + grad).astype(BF16)

    by_chunks(row_count, make_grad)


def finish_kernel(layout, factor, place, *refs):
    count = len(refs) - len(layout) - 1
    pieces, outs, landed = refs[:count], refs[count:-1], refs[-1]
    part = landed.shape[1]
    for index, piece in enumerate(pieces):
        landed[place[2] ^ index] = piece[...]

    def write(out, where, columns, start, rows):
        done = 0
        while done < rows:
            owner, local = (start + done) // part, (start + done) % part
            size = min(rows - done, part - local)
            block = landed[owner, local : local + size, :].astype(F32) * factor
            if where is None:
                out[done : done + size, columns] = block
            else:
                out[where, done : done + size, :] = block
            done += size

    for out, (start, halves) in zip(outs, layout):
        width = landed.shape[2]
        if halves:
            for half in range(2):
                columns = slice(half * width, (half + 1) * width)
                write(out, None, columns, start + half * out.shape[0], out.shape[0])
        elif len(out.shape) == 3:
            for tap in range(out.shape[0]):
                write(out, tap, None, start + tap * out.shape[1], out.shape[1])
        else:
            write(out, None, slice(0, width), start, out.shape[0])


def stepped(array):
    rest = (0,) * (array.ndim - 1)
    return pl.BlockSpec((None,) + array.shape[1:], lambda step: (step,) + rest)


def held(array):
    zeros = (0,) * array.ndim
    return pl.BlockSpec(array.shape, lambda step: zeros, pipeline_mode=pl.Buffered(1))


def call(body, steps, moving, fixed, outs, sums, scratch, flops, loose=(), place=None, semaphores=0):
    out_shapes = [jax.ShapeDtypeStruct(shape, kind) for shape, kind in outs]
    sum_shapes = [jax.ShapeDtypeStruct(shape, kind) for shape, kind in sums]
    operands = list(moving) + list(loose) + list(fixed)
    traffic = sum(
        entry.size * entry.dtype.itemsize for entry in operands + out_shapes + sum_shapes
    )
    in_specs = [stepped(entry) for entry in moving]
    in_specs += [pl.BlockSpec(memory_space=pl.ANY) for _ in loose]
    in_specs += [held(entry) for entry in fixed]
    if place is not None:
        operands = [place] + operands
        in_specs = [pl.BlockSpec(memory_space=pltpu.SMEM)] + in_specs
    scratch_shapes = [pltpu.VMEM(shape, kind) for shape, kind in scratch]
    if semaphores:
        scratch_shapes.append(pltpu.SemaphoreType.DMA((semaphores,)))
    return pl.pallas_call(
        body,
        grid=(steps,),
        in_specs=in_specs,
        out_specs=[stepped(entry) for entry in out_shapes] + [held(entry) for entry in sum_shapes],
        out_shape=out_shapes + sum_shapes,
        scratch_shapes=scratch_shapes,
        compiler_params=pltpu.CompilerParams(
            dimension_semantics=("arbitrary",), vmem_limit_bytes=VMEM_LIMIT
        ),
        cost_estimate=pl.CostEstimate(flops=flops, bytes_accessed=traffic, transcendentals=0),
    )(*operands)


def owners(places, doc_ends):
    return jnp.sum((places[..., None] >= doc_ends[:, None, :]).astype(jnp.int32), axis=-1)


def build_masks(places, doc_ends, stream_len, offsets):
    own_doc = owners(places[None, :], doc_ends)
    columns = []
    for offset in offsets:
        partner = places + offset
        inside = (partner >= 0) & (partner < stream_len)
        columns.append(inside[None, :] & (owners(partner[None, :], doc_ends) == own_doc))
    return jnp.stack(columns, axis=-1).astype(BF16)


def to_next(block):
    count = lax.axis_size("seq")
    return lax.ppermute(block, "seq", [(i, i + 1) for i in range(count - 1)])


def to_previous(block):
    count = lax.axis_size("seq")
    return lax.ppermute(block, "seq", [(i + 1, i) for i in range(count - 1)])


def exchanged(block, axis, bit):
    return lax.ppermute(block, axis, [(i, i ^ bit) for i in range(lax.axis_size(axis))])


def round_up(value, unit):
    return -(-value // unit) * unit


def padded(block, rows):
    return jnp.pad(block, ((0, rows - block.shape[0]), (0, 0)))


class Chain:
    def __init__(self, steps):
        self.steps, self.result = steps, None
        self.pending = next(steps)

    def advance(self, arrays=None):
        try:
            self.pending = self.steps.send(self.pending if arrays is None else arrays)
        except StopIteration as stop:
            self.pending, self.result = None, stop.value
        return self

    def finish(self):
        while self.pending is not None:
            self.advance()
        return self.result


def slot(operand, *chains):
    live = [chain for chain in chains if chain.pending is not None]
    operand, arrays = lax.optimization_barrier((operand, [chain.pending for chain in live]))
    for chain, pending in zip(live, arrays):
        chain.advance(pending)
    return operand


PARTS = 4


def half_spacing(rows):
    part = round_up(rows // PARTS, 16)
    return part, (rows - part) // (PARTS - 1)


def gather_half(shard):
    part, spacing = half_spacing(shard.shape[0])
    own = lax.axis_index("seq") & (PARTS - 1)
    piece = lax.dynamic_slice_in_dim(shard, own * spacing, part, axis=0)
    (piece,) = yield [piece]
    columns = [piece]
    for bit in range(1, lax.axis_size("fsdp")):
        columns.append(exchanged(piece, "fsdp", bit))
    columns = yield columns
    others = [exchanged(entry, "seq", 2) for entry in columns]
    columns, others = yield [columns, others]
    pieces = []
    for entry, other in zip(columns, others):
        pieces += [entry, exchanged(entry, "seq", 1), other, exchanged(other, "seq", 1)]
    return pieces


def gather_full(shard):
    seq_count, fsdp_count = lax.axis_size("seq"), lax.axis_size("fsdp")
    part = round_up(shard.shape[0], 16 * seq_count) // seq_count
    piece = lax.dynamic_slice_in_dim(
        padded(shard, part * seq_count), lax.axis_index("seq") * part, part, axis=0
    )
    (piece,) = yield [piece]
    columns = [piece]
    for far in range(1, fsdp_count):
        columns.append(exchanged(piece, "fsdp", far))
    half_count = fsdp_count // 2
    halves = [[jnp.stack(columns[:half_count])], [jnp.stack(columns[half_count:])]]
    indices = [[0], [0]]
    orders = routes(seq_count)
    for step in range(len(orders[0]) + 1):
        halves = yield halves
        for half, order in enumerate(orders):
            bit = (order + [1])[step]
            halves[half] = halves[half] + [exchanged(entry, "seq", bit) for entry in halves[half]]
            indices[half] = indices[half] + [index ^ bit for index in indices[half]]
    pieces = []
    for entries, places in zip(halves, indices):
        pieces += [entry for _, entry in sorted(zip(places, entries), key=lambda pair: pair[0])]
    return pieces


def add_low(*blocks):
    total = blocks[0].astype(F32)
    for block in blocks[1:]:
        total = total + block.astype(F32)
    return total.astype(BF16)


def reduce_pieces(keep, send):
    seq_count, fsdp_count = lax.axis_size("seq"), lax.axis_size("fsdp")
    shape = (2, -1, fsdp_count // 2) + keep.shape[1:]
    (send,) = yield [send]
    parts = (keep.reshape(shape), exchanged(send, "seq", 1).reshape(shape))
    orders = routes(seq_count)
    terms = [[entry[half] for entry in parts] for half in range(2)]
    for step in range(len(orders[0])):
        size = terms[0][0].shape[0] // 2
        leaving = [add_low(*[term[size:] for term in entries]) for entries in terms]
        leaving = yield leaving
        terms = [
            [term[:size] for term in entries] + [exchanged(block, "seq", order[step])]
            for entries, block, order in zip(terms, leaving, orders)
        ]
    columns = []
    for entries in terms:
        columns += [[term[0, within] for term in entries] for within in range(fsdp_count // 2)]
    leaving = yield [add_low(*columns[far]) for far in range(1, fsdp_count)]
    arrived = [exchanged(block, "fsdp", far + 1) for far, block in enumerate(leaving)]
    pieces = [add_low(*columns[0], *arrived)]
    indices = [0]
    for bit in orders[1] + [1]:
        pieces = yield pieces
        pieces = pieces + [exchanged(piece, "seq", bit) for piece in pieces]
        indices = indices + [index ^ bit for index in indices]
    return [piece for _, piece in sorted(zip(indices, pieces), key=lambda pair: pair[0])]


def reduce_vectors(vectors):
    for axis in ("seq", "fsdp"):
        bit = 1
        while bit < lax.axis_size(axis):
            (vectors,) = yield [vectors]
            vectors = vectors + exchanged(vectors, axis, bit)
            bit *= 2
    return vectors


def local(
    characters,
    lengths,
    cotangent,
    encproject,
    enckernel,
    encexpand,
    encwidegain,
    encgains,
    encwideshift,
    encshifts,
    decproject,
    deckernel,
    decexpand,
    decwidegain,
    decgains,
    decwideshift,
    decshifts,
):
    micro, _, rows, width = characters.shape
    inner_width = encproject.shape[1]
    seq_count = lax.axis_size("seq")
    fsdp_count = lax.axis_size("fsdp")
    stream_len = rows * seq_count
    total_rows = micro * stream_len * fsdp_count
    factor = 1.0 / jnp.sqrt(jnp.float32(total_rows))
    stream = characters[:, 0]
    cot = cotangent[:, 0]

    seq_index = lax.axis_index("seq")
    place = jnp.stack([lax.axis_index("fsdp"), seq_index & (PARTS - 1), seq_index])
    place = place.astype(jnp.int32)
    def rows_of(kernel):
        return kernel.reshape(-1, kernel.shape[2])

    def halves(expand):
        return [expand[:, :inner_width], expand[:, inner_width:]]

    wide_local = [encwidegain[None], encwideshift, decwidegain[None], decwideshift]
    wide_local = jnp.concatenate(wide_local, axis=0)
    inner_local = jnp.concatenate([encgains, encshifts, decgains, decshifts], axis=0)
    vector_local = jnp.concatenate([wide_local.reshape(-1), inner_local.reshape(-1)])
    vector_shards = jnp.stack(
        [vector_local] + [exchanged(vector_local, "fsdp", far) for far in range(1, fsdp_count)]
    )
    own = lax.axis_index("fsdp")
    vector_shards = jnp.stack(
        [
            lax.dynamic_index_in_dim(vector_shards, own ^ shard, 0, keepdims=False)
            for shard in range(fsdp_count)
        ]
    ).astype(F32)

    def whole_vectors(shards, like):
        cut = shards.reshape((fsdp_count,) + like.shape)
        return jnp.transpose(cut, (1, 0, 2)).reshape(like.shape[0], -1)

    wides = whole_vectors(vector_shards[:, : wide_local.size], wide_local)
    inners = whole_vectors(vector_shards[:, wide_local.size :], inner_local)
    enc_wide, dec_wide = wides[:3], wides[3:]
    enc_inner, dec_inner = inners[:6], inners[6:]

    enc_rows = jnp.concatenate([rows_of(enckernel)] + halves(encexpand), axis=0)
    dec_rows = jnp.concatenate([decproject, rows_of(deckernel)] + halves(decexpand), axis=0)
    entry = Chain(gather_half(encproject)).advance()
    enc_gather = Chain(gather_full(enc_rows)).advance()
    dec_gather = Chain(gather_full(dec_rows)).advance()
    _, spacing = half_spacing(encproject.shape[0])

    def landing(pieces):
        count = len(pieces) * pieces[0].shape[0]
        return ((count,) + pieces[0].shape[1:], BF16), count

    places = lax.axis_index("seq") * rows + jnp.arange(rows, dtype=jnp.int32)
    doc_ends = jnp.cumsum(lengths[:, 0], axis=1)
    enc_offsets = tap_offsets(True)
    dec_offsets = tap_offsets(False)
    enc_back = [-offset for offset in enc_offsets]
    dec_back = [-offset for offset in dec_offsets]
    enc_masks = build_masks(places, doc_ends, stream_len, enc_offsets)
    dec_masks = build_masks(places, doc_ends, stream_len, dec_offsets)
    enc_back_masks = build_masks(places, doc_ends, stream_len, enc_back)
    dec_back_masks = build_masks(places, doc_ends, stream_len, dec_back)
    enc_reach = max(enc_offsets)
    dec_reach = -min(dec_offsets)

    wide_shape = (micro, rows, width)
    inner_shape = (micro, rows, inner_width)
    unit = 2 * micro * rows * width * inner_width
    tap_unit = 2 * micro * rows * inner_width * inner_width

    def enter_body(*refs):
        enter_encoder_kernel(PARTS, spacing, *refs)

    project_pieces = entry.finish()
    enc_gather.advance()
    enc_wide = slot(enc_wide, enc_gather)
    first_e, hidden_e, second_e, enc_project = call(
        enter_body,
        micro,
        [stream],
        [enc_wide, enc_inner],
        [(wide_shape, BF16), (inner_shape, F32), (inner_shape, BF16)],
        [((width, inner_width), BF16)],
        [((len(project_pieces),) + project_pieces[0].shape, BF16)],
        unit,
        project_pieces,
        place,
        len(project_pieces),
    )
    low = to_next(second_e[:, rows - enc_reach :])
    high = to_previous(second_e[:, :enc_reach])

    def middle_body(*refs):
        middle_kernel(enc_offsets, fsdp_count, *refs)

    enc_pieces = enc_gather.finish()
    dec_gather.advance()
    enc_inner = slot(enc_inner, dec_gather)
    landed, copies = landing(enc_pieces)
    mixed_e, third_e, middle, enc_expand, enc_flat = call(
        middle_body,
        micro,
        [second_e, low, high, enc_masks, stream],
        [enc_wide, enc_inner],
        [(inner_shape, F32), (inner_shape, BF16), (wide_shape, F32)],
        [((inner_width, width), BF16), ((inner_width, ENC_TAPS * inner_width), BF16)],
        [
            ((rows + 2 * enc_reach, inner_width), BF16),
            ((rows, ENC_TAPS * inner_width), BF16),
            ((ENC_TAPS * inner_width, inner_width), BF16),
            landed,
        ],
        unit + ENC_TAPS * tap_unit,
        enc_pieces,
        place,
        copies,
    )

    def enter_decoder_body(*refs):
        enter_decoder_kernel(DEC_TAPS, fsdp_count, *refs)

    dec_pieces = dec_gather.finish()
    landed, copies = landing(dec_pieces)
    first_d, hidden_d, second_d, dec_project, dec_stacked, dec_flat, dec_expand = call(
        enter_decoder_body,
        micro,
        [middle],
        [dec_wide, dec_inner],
        [(wide_shape, BF16), (inner_shape, F32), (inner_shape, BF16)],
        [
            ((width, inner_width), BF16),
            ((DEC_TAPS * inner_width, inner_width), BF16),
            ((inner_width, DEC_TAPS * inner_width), BF16),
            ((inner_width, width), BF16),
        ],
        [landed],
        unit,
        dec_pieces,
        place,
        copies,
    )
    low = to_next(second_d[:, rows - dec_reach :])

    def turn_body(*refs):
        turn_kernel(dec_offsets, *refs)

    third_d, gmixed_d, gexpand_d, turn_wide, turn_inner = call(
        turn_body,
        micro,
        [second_d, low, dec_masks, cot],
        [dec_stacked, dec_expand, dec_inner],
        [(inner_shape, BF16), (inner_shape, BF16)],
        [
            ((inner_width, width), BF16),
            ((1, 8, width), F32),
            ((3, 8, inner_width), F32),
        ],
        [
            ((rows + dec_reach, inner_width), BF16),
            ((rows, DEC_TAPS * inner_width), BF16),
            ((rows, inner_width), F32),
            ((rows, inner_width), F32),
            ((inner_width, width), F32),
        ],
        2 * unit + DEC_TAPS * tap_unit,
    )
    high = to_previous(gmixed_d[:, :dec_reach])

    counts = (seq_count, fsdp_count)

    def packed_pair(row_total):
        part = round_up(row_total, 8 * seq_count) // seq_count
        return [((seq_count * fsdp_count // 2, part, inner_width), BF16)] * 2

    shard_part = inner_width // fsdp_count

    def decoder_back_body(*refs):
        decoder_back_kernel(dec_back, dec_reach, counts, *refs)

    ghidden_d, keep_d, send_d, conv_inner_d = call(
        decoder_back_body,
        micro,
        [gmixed_d, high, dec_back_masks, second_d, hidden_d, first_d],
        [dec_flat, dec_inner, gexpand_d],
        [(inner_shape, BF16)],
        packed_pair((DEC_TAPS + 2) * shard_part + width // fsdp_count)
        + [((3, 8, inner_width), F32)],
        [
            ((rows + dec_reach, inner_width), BF16),
            ((rows, DEC_TAPS * inner_width), BF16),
            ((rows, inner_width), F32),
            ((inner_width, DEC_TAPS * inner_width), F32),
            ((width, inner_width), F32),
        ],
        unit + 2 * DEC_TAPS * tap_unit,
        place=place,
    )

    dec_reduce = Chain(reduce_pieces(keep_d, send_d))
    dec_wide = slot(dec_wide, dec_reduce)
    gmiddle, gmixed_e, gexpand_e, link_wide, link_inner = call(
        link_back_kernel,
        micro,
        [ghidden_d, middle, cot, mixed_e, third_e],
        [dec_project, dec_wide, enc_expand, enc_inner],
        [(wide_shape, F32), (inner_shape, BF16)],
        [
            ((inner_width, width), BF16),
            ((3, 8, width), F32),
            ((3, 8, inner_width), F32),
        ],
        [
            ((rows, width), F32),
            ((rows, width), BF16),
            ((rows, inner_width), F32),
            ((inner_width, width), F32),
        ],
        3 * unit,
    )
    low = to_next(gmixed_e[:, rows - enc_reach :])
    high = to_previous(gmixed_e[:, :enc_reach])
    extended_scratch = [
        ((rows + 2 * enc_reach, inner_width), BF16),
        ((rows, ENC_TAPS * inner_width), BF16),
    ]

    def kernel_grad_body(*refs):
        encoder_kernel_grad_kernel(enc_back, enc_reach, enc_reach, counts, *refs)

    gexpand_e = slot(gexpand_e, dec_reduce)
    keep_e, send_e = call(
        kernel_grad_body,
        micro,
        [gmixed_e, low, high, enc_back_masks, second_e],
        [gexpand_e],
        [],
        packed_pair((ENC_TAPS + 2) * shard_part),
        extended_scratch + [((inner_width, ENC_TAPS * inner_width), F32)],
        ENC_TAPS * tap_unit,
        place=place,
    )

    def encoder_back_body(*refs):
        encoder_back_kernel(enc_back, enc_reach, enc_reach, counts, *refs)

    enc_reduce = Chain(reduce_pieces(keep_e, send_e))
    enc_inner = slot(enc_inner, dec_reduce, enc_reduce)
    ghidden_e, keep_p, send_p, conv_inner_e = call(
        encoder_back_body,
        micro,
        [gmixed_e, low, high, enc_back_masks, hidden_e, first_e],
        [enc_flat, enc_inner],
        [(inner_shape, BF16)],
        packed_pair(width // fsdp_count) + [((3, 8, inner_width), F32)],
        extended_scratch + [((rows, inner_width), F32), ((width, inner_width), F32)],
        unit + ENC_TAPS * tap_unit,
        place=place,
    )
    entry_reduce = Chain(reduce_pieces(keep_p, send_p))
    enc_wide = slot(enc_wide, dec_reduce, enc_reduce, entry_reduce)
    gstream, leave_wide = call(
        leave_kernel,
        micro,
        [ghidden_e, stream, gmiddle],
        [enc_project, enc_wide],
        [(wide_shape, BF16)],
        [((2, 8, width), F32)],
        [((rows, width), F32)],
        unit,
    )

    sums = [leave_wide, link_wide, turn_wide, conv_inner_e, link_inner, conv_inner_d, turn_inner]
    sums = [jnp.sum(entry, axis=1).reshape(-1, inner_width) for entry in sums]
    vector_reduce = Chain(reduce_vectors(jnp.concatenate(sums, axis=0)))
    dec_wide = slot(dec_wide, dec_reduce, enc_reduce, entry_reduce, vector_reduce)
    (output,) = call(
        output_kernel,
        micro,
        [third_d, middle],
        [dec_expand, dec_wide],
        [(wide_shape, BF16)],
        [],
        [((rows, width), F32)],
        unit,
    )

    def own_columns(vectors):
        part = vectors.shape[1] // fsdp_count
        return lax.dynamic_slice_in_dim(vectors, own * part, part, axis=1)

    sums = vector_reduce.finish() * factor
    wide_sums = sums[:12].reshape(6, width)
    order = [wide_sums[:2], wide_sums[4:5], wide_sums[2:4], wide_sums[5:]]
    wide_own = own_columns(jnp.concatenate(order))
    inner_own = own_columns(sums[12:])

    def vectors(wide_rows, inner_rows):
        widegain = wide_rows[0]
        wideshift = wide_rows[1:3]
        gains = jnp.stack([inner_rows[0], inner_rows[3]])
        shifts = jnp.stack([inner_rows[1], inner_rows[4], inner_rows[2], inner_rows[5]])
        return widegain, gains, wideshift, shifts

    project_rows = width // fsdp_count
    scale = total_rows**-0.5
    shapes = {
        "project": (project_rows, inner_width),
        "expand": (shard_part, width),
    }

    def finish(chain, names):
        pieces = chain.finish()
        layout, outs, start = [], [], 0
        for name in names:
            shape = shapes.get(name, (name, shard_part, inner_width))
            layout.append((start, name == "expand"))
            outs.append(jax.ShapeDtypeStruct(shape, F32))
            size = 1
            for extent in shape:
                size *= extent
            start += size // inner_width

        def body(*refs):
            finish_kernel(layout, scale, *refs)

        whole = pl.BlockSpec(memory_space=pltpu.VMEM)
        return pl.pallas_call(
            body,
            in_specs=[pl.BlockSpec(memory_space=pltpu.SMEM)] + [whole] * len(pieces),
            out_specs=[whole] * len(outs),
            out_shape=outs,
            scratch_shapes=[pltpu.VMEM((len(pieces),) + pieces[0].shape, BF16)],
            compiler_params=pltpu.CompilerParams(vmem_limit_bytes=VMEM_LIMIT),
        )(place, *pieces)

    gproject_d, gkernel_d, gexpand_d = finish(dec_reduce, ["project", DEC_TAPS, "expand"])
    gkernel_e, gexpand_e = finish(enc_reduce, [ENC_TAPS, "expand"])
    (gproject_e,) = finish(entry_reduce, ["project"])
    return (
        output[:, None],
        gstream[:, None],
        gproject_e,
        gkernel_e,
        gexpand_e,
        *vectors(wide_own[:3], inner_own[:6]),
        gproject_d,
        gkernel_d,
        gexpand_d,
        *vectors(wide_own[3:], inner_own[6:]),
    )


def solution(mesh):
    tokens = P(None, "fsdp", "seq", None)
    weights = (
        P("fsdp", None),
        P(None, "fsdp", None),
        P("fsdp", None),
        P("fsdp"),
        P(None, "fsdp"),
        P(None, "fsdp"),
        P(None, "fsdp"),
    )
    return jax.shard_map(
        local,
        mesh=mesh,
        in_specs=(tokens, P(None, "fsdp", None), tokens) + weights + weights,
        out_specs=(tokens, tokens) + weights + weights,
        check_vma=False,
    )
```

time: 1780 us -> 683 us (0.38)
  waiting for transfers between devices: 926 us -> 138 us
  matrix products: 396 us -> 0 us
  Pallas kernels: 0 us -> 318 us
  other arithmetic: 176 us -> 48.3 us
  blocking collectives: 79 us -> 0 us
  local copies, waits for them, and re-layouts: 119 us -> 41.9 us
  starting transfers between devices: 55.5 us -> 126 us
  between operations: 21 us -> 2.37 us
    psum x2 -> x0, waiting for transfers between devices: 737 us -> none  [local(): lax.psum((running[0], running[1], running[2], running[3], running[4], run...]
    dot_general x72 -> x0, matrix products: 396 us -> none  [the longest x24 169 us: inner_product(): lax.dot_general(factor, matrix, (((0,), (0,)), ((), ())), preferred_eleme...]
    pallas_call x0 -> x13, Pallas kernels: none -> 318 us  [the longest x10 306 us: call(): pl.pallas_call(body, grid=(steps,), in_specs=in_specs, out_specs=[stepped...]
    all_gather x6 -> x0, waiting for transfers between devices: 185 us -> none  [the longest x1 56.7 us: local(): lax.all_gather(deckernel, 'fsdp', axis=1, tiled=True)]
    ppermute x24 -> x108, waiting for transfers between devices: 0.06 us -> 138 us  [the longest x102 130 us: exchanged(): lax.ppermute(block, axis, [(i, i ^ bit) for i in range(lax.axis_size(axis...]
    ppermute x24 -> x108, starting transfers between devices: 55 us -> 126 us  [the longest x102 117 us: exchanged(): lax.ppermute(block, axis, [(i, i ^ bit) for i in range(lax.axis_size(axis...]
    all_gather x6 -> x0, blocking collectives: 69.1 us -> none  [the longest x1 14.3 us: local(): lax.all_gather(decshifts, 'fsdp', axis=1, tiled=True)]
    reduce_sum x38 -> x8, other arithmetic: 51.9 us -> 3.82 us  [the longest x7 3.55 us: local(): sums = [jnp.sum(entry, axis=1).reshape(-1, inner_width) for entry in sums]]
  transfers between devices with their start and end apart: 32 -> 108, of which waited for: 6 -> 27; matrix products, arithmetic and copies ran while one was open for 21% -> 10% of each run, Pallas kernels for 0% -> 31%
where the time goes in v1:
time: 683 us; the launch traced here: 675 us
  Pallas kernels  318 us (47%)
  waiting for transfers between devices  138 us (20%)
  starting transfers between devices  126 us (18%)
  other arithmetic  48.3 us (7%)
  local copies, waits for them, and re-layouts  41.9 us (6%)
    pallas_call x10, Pallas kernels, call(): pl.pallas_call(body, grid=(steps,), in_specs=in_specs, out_specs=[stepped...  306 us
    ppermute x102, waiting for transfers between devices, exchanged(): lax.ppermute(block, axis, [(i, i ^ bit) for i in range(lax.axis_size(axis...  130 us
    ppermute x102, starting transfers between devices, exchanged(): lax.ppermute(block, axis, [(i, i ^ bit) for i in range(lax.axis_size(axis...  117 us
    convert_element_type x9, other arithmetic, add_low(): return total.astype(BF16)  25.1 us
  transfers between devices with their start and end apart: 108, of which 27 were waited for; matrix products, arithmetic and copies ran while one was open for 10% of the time, Pallas kernels for 31%

profile of v1, /device:TPU:0, one launch (start us, length us, event | category | flops | bytes accessed | tf_op | source)
XLA Modules:
  0.0 674.8 jit_solution(1514205754091576389)
XLA Ops:
  3.9 3.0 collective-permute-start.15
  7.0 2.6 collective-permute-start.16
  9.6 2.0 collective-permute-start.7
  11.6 2.0 collective-permute-start.11
  13.6 2.0 fusion.53
  22.1 2.0 collective-permute-start.20
  24.3 4.3 collective-permute-done.7.refs_10_
  28.6 9.8 %collective-permute-start.21 = (bf16[176,800]{1,0:T(8,128)(2,1)S(1)}, bf16[176,800]{1,0:T(8,128)(2,1)S(1)}, u32[]{:S(2)}, u32[]{:S(2)}) collective-permute-start(bf16[176,800]{1,0:T(8,128)(2,1)S(1)} %fusion.20), channel_id=1, source_target_pairs={{0,3},{1,2},{2,1},{3,0},{4,7},{5,6},{6,5},{7,4},{8,11},{9,10},{10,... | collective-permute-start | bytes 844808 | tf_op jit(solution)/shard_map/ppermute | solution.py:706
  38.4 6.7 collective-permute-start.18
  45.1 2.4 collective-permute-start.40
  47.5 14.5 %collective-permute-done.20 = bf16[176,800]{1,0:T(8,128)(2,1)S(1)} collective-permute-done((bf16[176,800]{1,0:T(8,128)(2,1)S(1)}, bf16[176,800]{1,0:T(8,128)(2,1)S(1)}, u32[]{:S(2)}, u32[]{:S(2)}) %collective-permute-start.20) | collective-permute-done | bytes 281632 | tf_op jit(solution)/shard_map/ppermute | solution.py:706
  64.1 2.0 collective-permute-start.13
  66.1 12.0 %collective-permute-done.39 = bf16[176,800]{1,0:T(8,128)(2,1)S(1)} collective-permute-done((bf16[176,800]{1,0:T(8,128)(2,1)S(1)}, bf16[176,800]{1,0:T(8,128)(2,1)S(1)}, u32[]{:S(2)}, u32[]{:S(2)}) %collective-permute-start.39) | collective-permute-done | bytes 281632 | tf_op jit(solution)/shard_map/ppermute | solution.py:706
  82.3 3.8 collective-permute-done.5.refs_8_
  88.3 11.3 %collective-permute-done.22.refs_16_ = bf16[2,176,800]{2,1,0:T(8,128)(2,1)} collective-permute-done((bf16[2,176,800]{2,1,0:T(8,128)(2,1)}, bf16[2,176,800]{2,1,0:T(8,128)(2,1)}, u32[]{:S(2)}, u32[]{:S(2)}) %collective-permute-start.22) | collective-permute-done | bytes 563232 | tf_op jit(solution)/shard_map/ppermute | solution.py:706
  105.9 7.1 %collective-permute-done.41.refs_12_ = bf16[2,176,800]{2,1,0:T(8,128)(2,1)S(1)} collective-permute-done((bf16[2,176,800]{2,1,0:T(8,128)(2,1)S(1)}, bf16[2,176,800]{2,1,0:T(8,128)(2,1)S(1)}, u32[]{:S(2)}, u32[]{:S(2)}) %collective-permute-start.41) | collective-permute-done | bytes 563232 | tf_op jit(solution)/shard_map/ppermute | solution.py:706
  114.5 20.0 %shard_map.288 = (bf16[4,480,1600]{2,1,0:T(8,128)(2,1)}, f32[4,480,800]{2,1,0:T(8,128)}, bf16[4,480,800]{2,1,0:T(8,128)(2,1)}, bf16[1600,800]{1,0:T(8,128)(2,1)}) custom-call(s32[3]{0:T(128)} %pad_add_fusion.2.refs_0_, bf16[4,480,1600]{2,1,0:T(8,128)(2,1)} %bitcast.138, bf16[112,800]{1,0:T(8,128)(2,1)} %copy-done.35, bf16[112,800]{1,0:T(8,128)(2,1)} %copy-done.52, ...), custom_call_target="tpu_custom_call" | custom-call | flops 4915200000 | bytes 26969600 | tf_op jit(solution)/shard_map/pallas_call | solution.py:667
  137.8 1.8 collective-permute-start.24
  139.6 3.9 collective-permute-done.24.refs_3_
  143.6 4.1 collective-permute-start.25
  154.1 11.5 %collective-permute-done.43.refs_4_ = bf16[2,176,800]{2,1,0:T(8,128)(2,1)S(1)} collective-permute-done((bf16[2,176,800]{2,1,0:T(8,128)(2,1)S(1)}, bf16[2,176,800]{2,1,0:T(8,128)(2,1)S(1)}, u32[]{:S(2)}, u32[]{:S(2)}) %collective-permute-start.43) | collective-permute-done | bytes 563232 | tf_op jit(solution)/shard_map/ppermute | solution.py:706
  166.3 12.0 %collective-permute-done.46.refs_8_ = bf16[2,176,800]{2,1,0:T(8,128)(2,1)S(1)} collective-permute-done((bf16[2,176,800]{2,1,0:T(8,128)(2,1)S(1)}, bf16[2,176,800]{2,1,0:T(8,128)(2,1)S(1)}, u32[]{:S(2)}, u32[]{:S(2)}) %collective-permute-start.46) | collective-permute-done | bytes 563232 | tf_op jit(solution)/shard_map/ppermute | solution.py:706
  178.9 4.4 collective-permute-done.52.refs_16_
  189.1 40.2 %shard_map.289 = (f32[4,480,800]{2,1,0:T(8,128)}, bf16[4,480,800]{2,1,0:T(8,128)(2,1)}, f32[4,480,1600]{2,1,0:T(8,128)}, bf16[800,1600]{1,0:T(8,128)(2,1)}, bf16[800,4000]{1,0:T(8,128)(2,1)}) custom-call(s32[3]{0:T(128)} %pad_add_fusion.2.refs_0_, bf16[4,480,800]{2,1,0:T(8,128)(2,1)} %get-tuple-element.93.refs_1_.refs_5_, bf16[4,16,800]{2,1,0:T(8,128)(2,1)} %copy-done.58, ...), custom_call_target="tpu_custom_call" | custom-call | flops 17203200000 | bytes 48953600 | tf_op jit(solution)/shard_map/pallas_call | solution.py:667
  230.3 26.1 %shard_map.290 = (bf16[4,480,1600]{2,1,0:T(8,128)(2,1)}, f32[4,480,800]{2,1,0:T(8,128)}, bf16[4,480,800]{2,1,0:T(8,128)(2,1)}, bf16[1600,800]{1,0:T(8,128)(2,1)}...) custom-call(s32[3]{0:T(128)} %pad_add_fusion.2.refs_0_, ...), custom_call_target="tpu_custom_call" | custom-call | flops 4915200000 | bytes 49497600 | tf_op jit(solution)/shard_map/pallas_call | solution.py:667
  257.4 2.2 collective-permute-start.54
  261.5 36.9 %shard_map.291 = (bf16[4,480,800]{2,1,0:T(8,128)(2,1)}, bf16[4,480,800]{2,1,0:T(8,128)(2,1)}, bf16[800,1600]{1,0:T(8,128)(2,1)}, f32[1,8,1600]{2,1,0:T(8,128)}, f32[3,8,800]{2,1,0:T(8,128)}) custom-call(bf16[4,480,800]{2,1,0:T(8,128)(2,1)} %get-tuple-element.104.refs_0_.refs_4_, bf16[4,32,800]{2,1,0:T(8,128)(2,1)} %copy-done.48, ...), custom_call_target="tpu_custom_call" | custom-call | flops 17203200000 | bytes 24683520 | tf_op jit(solution)/shard_map/pallas_call | solution.py:667
  301.7 3.7 collective-permute-done.55.refs_2_
  306.1 42.3 %shard_map.292 = (bf16[4,480,800]{2,1,0:T(8,128)(2,1)}, bf16[16,176,800]{2,1,0:T(8,128)(2,1)}, bf16[16,176,800]{2,1,0:T(8,128)(2,1)}, f32[3,8,800]{2,1,0:T(8,128)}) custom-call(s32[3]{0:T(128)} %pad_add_fusion.2.refs_0_, bf16[4,480,800]{2,1,0:T(8,128)(2,1)} %get-tuple-element.108.refs_1_, bf16[4,32,800]{2,1,0:T(8,128)(2,1)} %copy-done.49, ...), custom_call_target="tpu_custom_call" | custom-call | flops 19660800000 | bytes 37227520 | tf_op jit(solution)/shard_map/pallas_call | solution.py:667
  348.4 5.3 collective-permute-start.56
  355.0 44.2 %shard_map.293 = (f32[4,480,1600]{2,1,0:T(8,128)}, bf16[4,480,800]{2,1,0:T(8,128)(2,1)}, bf16[800,1600]{1,0:T(8,128)(2,1)}, f32[3,8,1600]{2,1,0:T(8,128)}, f32[3,8,800]{2,1,0:T(8,128)}) custom-call(bf16[4,480,800]{2,1,0:T(8,128)(2,1)} %get-tuple-element.117.grad_hidden, f32[4,480,1600]{2,1,0:T(8,128)} %get-tuple-element.99.refs_1_.middle, ...), custom_call_target="tpu_custom_call" | custom-call | flops 14745600000 | bytes 54028800 | tf_op jit(solution)/shard_map/pallas_call | solution.py:667
  400.2 1.9 collective-permute-start.59
  403.5 4.5 add_convert_fusion.2
  408.0 3.6 collective-permute-start.57
  413.2 24.6 %shard_map.294 = (bf16[16,176,800]{2,1,0:T(8,128)(2,1)}, bf16[16,176,800]{2,1,0:T(8,128)(2,1)}) custom-call(s32[3]{0:T(128)} %pad_add_fusion.2.refs_0_, bf16[4,480,800]{2,1,0:T(8,128)(2,1)} %get-tuple-element.125.refs_1_, bf16[4,16,800]{2,1,0:T(8,128)(2,1)} %copy-done.60, bf16[4,16,800]{2,1,0:T(8,128)(2,1)} %copy-done.61, ...), custom_call_target="tpu_custom_call" | custom-call | flops 12288000000 | bytes 17939200 | tf_op jit(solution)/shard_map/pallas_call | solution.py:667
  437.8 2.3 collective-permute-done.57
  440.1 4.1 fusion.2
  448.7 36.6 %shard_map.295 = (bf16[4,480,800]{2,1,0:T(8,128)(2,1)}, bf16[16,56,800]{2,1,0:T(8,128)(2,1)}, bf16[16,56,800]{2,1,0:T(8,128)(2,1)}, f32[3,8,800]{2,1,0:T(8,128)}) custom-call(s32[3]{0:T(128)} %pad_add_fusion.2.refs_0_, bf16[4,480,800]{2,1,0:T(8,128)(2,1)} %get-tuple-element.125.refs_1_, bf16[4,16,800]{2,1,0:T(8,128)(2,1)} %copy-done.60, ...), custom_call_target="tpu_custom_call" | custom-call | flops 17203200000 | bytes 28019200 | tf_op jit(solution)/shard_map/pallas_call | solution.py:667
  485.4 1.9 fusion.24
  487.2 2.3 fusion.26
  489.6 4.5 add_convert_fusion
  494.9 1.6 collective-permute-start.68
  496.5 6.4 collective-permute-start.64
  509.1 2.2 collective-permute-done.64
  511.3 2.3 collective-permute-start.66
  513.6 22.0 %shard_map.296 = (bf16[4,480,1600]{2,1,0:T(8,128)(2,1)}, f32[2,8,1600]{2,1,0:T(8,128)}) custom-call(bf16[4,480,800]{2,1,0:T(8,128)(2,1)} %get-tuple-element.144.grad_hidden, bf16[4,480,1600]{2,1,0:T(8,128)(2,1)} %bitcast.140, f32[4,480,1600]{2,1,0:T(8,128)} %get-tuple-element.145.grad_middle, bf16[1600,800]{1,0:T(8,128)(2,1)} %get-tuple-element.146.project, ...), custom_call_target="tpu_custom_call" | custom-call | flops 4915200000 | bytes 30329600 | tf_op jit(solution)/shard_map/pallas_call | solution.py:667
  537.2 3.9 concatenate.26
  542.8 3.7 fusion
  546.4 2.1 add_convert_fusion.4
  551.7 1.7 collective-permute-start.102
  555.1 1.6 collective-permute-start.73
  557.5 13.3 %shard_map.297 = bf16[4,480,1600]{2,1,0:T(8,128)(2,1)} custom-call(bf16[4,480,800]{2,1,0:T(8,128)(2,1)} %get-tuple-element.107.third, f32[4,480,1600]{2,1,0:T(8,128)} %get-tuple-element.99.refs_1_.middle, bf16[800,1600]{1,0:T(8,128)(2,1)} %get-tuple-element.106.refs_5_.expand, f32[3,1600]{1,0:T(4,128)} %slice.617.refs_18_.dec_wide.wide), custom_call_target="tpu_custom_call" | custom-call | flops 4915200000 | bytes 24083200 | tf_op jit(solution)/shard_map/pallas_call | solution.py:667
  572.1 1.7 slice_bitcast_fusion.9
  578.0 5.4 collective-permute-done.73
  583.5 2.2 fusion.18
  598.3 2.3 collective-permute-start.88
  603.7 2.7 collective-permute-done.85
  607.2 14.4 %collective-permute-done.87 = bf16[176,800]{1,0:T(8,128)(2,1)S(1)} collective-permute-done((bf16[176,800]{1,0:T(8,128)(2,1)S(1)}, bf16[176,800]{1,0:T(8,128)(2,1)S(1)}, u32[]{:S(2)}, u32[]{:S(2)}) %collective-permute-start.87) | collective-permute-done | bytes 281632 | tf_op jit(solution)/shard_map/ppermute | solution.py:706
  621.6 5.3 collective-permute-start.75
  628.3 3.2 collective-permute-start.76
  642.6 13.6 %collective-permute-done.80.refs_5_ = bf16[56,800]{1,0:T(8,128)(2,1)S(1)} collective-permute-done((bf16[56,800]{1,0:T(8,128)(2,1)S(1)}, bf16[56,800]{1,0:T(8,128)(2,1)S(1)}, u32[]{:S(2)}, u32[]{:S(2)}) %collective-permute-start.80) | collective-permute-done | bytes 89632 | tf_op jit(solution)/shard_map/ppermute | solution.py:706
  661.7 4.6 shard_map.300
  666.3 2.5 shard_map.298
  669.7 4.6 shard_map.299
  (410 shorter events, 116.5 us)
Async XLA Ops:
  3.9 16.0 %collective-permute-start.15 = (bf16[4800]{0:T(1024)(128)(2,1)S(1)}, bf16[4800]{0:T(1024)(128)(2,1)S(1)}, u32[]{:S(2)}, u32[]{:S(2)}) collective-permute-start(bf16[4800]{0:T(1024)(128)(2,1)S(1)} %pad_maximum_fusion.5), channel_id=1, source_target_pairs={{0,1},{1,0},{2,3},{3,2},{4,5},{5,4},{6,7},{7,6},{8,9},{9,8},{10,11... | collective-permute-start | bytes 28808 | tf_op jit(solution)/shard_map/ppermute | solution.py:706
  7.0 13.5 %collective-permute-start.16 = (bf16[4800]{0:T(1024)(128)(2,1)S(1)}, bf16[4800]{0:T(1024)(128)(2,1)S(1)}, u32[]{:S(2)}, u32[]{:S(2)}) collective-permute-start(bf16[4800]{0:T(1024)(128)(2,1)S(1)} %pad_maximum_fusion.5), channel_id=1, source_target_pairs={{0,2},{1,3},{2,0},{3,1},{4,6},{5,7},{6,4},{7,5},{8,10},{9,11},{10,... | collective-permute-start | bytes 28808 | tf_op jit(solution)/shard_map/ppermute | solution.py:706
  9.6 19.0 %collective-permute-start.7 = (bf16[112,800]{1,0:T(8,128)(2,1)S(1)}, bf16[112,800]{1,0:T(8,128)(2,1)}, u32[]{:S(2)}, u32[]{:S(2)}) collective-permute-start(bf16[112,800]{1,0:T(8,128)(2,1)S(1)} %constant_dynamic-slice_fusion.5.refs_2_), channel_id=1, source_target_pairs={{0,2},{1,3},{2,0},{3,1},{4,6},{5,7},{6,4},{7,5},{8,10},{9,11},{10,... | collective-permute-start | bytes 537608 | tf_op jit(solution)/shard_map/ppermute | solution.py:706
  11.6 26.9 %collective-permute-start.11 = (bf16[112,800]{1,0:T(8,128)(2,1)S(1)}, bf16[112,800]{1,0:T(8,128)(2,1)}, u32[]{:S(2)}, u32[]{:S(2)}) collective-permute-start(bf16[112,800]{1,0:T(8,128)(2,1)S(1)} %constant_dynamic-slice_fusion.5.refs_2_), channel_id=1, source_target_pairs={{0,3},{1,2},{2,1},{3,0},{4,7},{5,6},{6,5},{7,4},{8,11},{9,10},{10,... | collective-permute-start | bytes 537608 | tf_op jit(solution)/shard_map/ppermute | solution.py:706
  20.0 25.1 %collective-permute-start.3 = (bf16[112,800]{1,0:T(8,128)(2,1)S(1)}, bf16[112,800]{1,0:T(8,128)(2,1)S(1)}, u32[]{:S(2)}, u32[]{:S(2)}) collective-permute-start(bf16[112,800]{1,0:T(8,128)(2,1)S(1)} %constant_dynamic-slice_fusion.5.refs_2_), channel_id=1, source_target_pairs={{0,1},{1,0},{2,3},{3,2},{4,5},{5,4},{6,7},{7,6},{8,9},{9,8},{10,11... | collective-permute-start | bytes 537608 | tf_op jit(solution)/shard_map/ppermute | solution.py:706
  20.5 24.6 %collective-permute-start.1 = (bf16[112,800]{1,0:T(8,128)(2,1)S(1)}, bf16[112,800]{1,0:T(8,128)(2,1)S(1)}, u32[]{:S(2)}, u32[]{:S(2)}) collective-permute-start(bf16[112,800]{1,0:T(8,128)(2,1)S(1)} %constant_dynamic-slice_fusion.5.refs_2_), channel_id=1, source_target_pairs={{0,8},{4,12},{8,0},{12,4},{16,24},{20,28},{24,16},{28,20},{1,9},{5... | collective-permute-start | bytes 537608 | tf_op jit(solution)/shard_map/ppermute | solution.py:706
  22.1 39.9 %collective-permute-start.20 = (bf16[176,800]{1,0:T(8,128)(2,1)S(1)}, bf16[176,800]{1,0:T(8,128)(2,1)S(1)}, u32[]{:S(2)}, u32[]{:S(2)}) collective-permute-start(bf16[176,800]{1,0:T(8,128)(2,1)S(1)} %fusion.20), channel_id=1, source_target_pairs={{0,2},{1,3},{2,0},{3,1},{4,6},{5,7},{6,4},{7,5},{8,10},{9,11},{10,... | collective-permute-start | bytes 844808 | tf_op jit(solution)/shard_map/ppermute | solution.py:706
  28.6 33.5 %collective-permute-start.21 = (bf16[176,800]{1,0:T(8,128)(2,1)S(1)}, bf16[176,800]{1,0:T(8,128)(2,1)S(1)}, u32[]{:S(2)}, u32[]{:S(2)}) collective-permute-start(bf16[176,800]{1,0:T(8,128)(2,1)S(1)} %fusion.20), channel_id=1, source_target_pairs={{0,3},{1,2},{2,1},{3,0},{4,7},{5,6},{6,5},{7,4},{8,11},{9,10},{10,... | collective-permute-start | bytes 844808 | tf_op jit(solution)/shard_map/ppermute | solution.py:706
  38.4 23.8 %collective-permute-start.18 = (bf16[176,800]{1,0:T(8,128)(2,1)S(1)}, bf16[176,800]{1,0:T(8,128)(2,1)S(1)}, u32[]{:S(2)}, u32[]{:S(2)}) collective-permute-start(bf16[176,800]{1,0:T(8,128)(2,1)S(1)} %fusion.20), channel_id=1, source_target_pairs={{0,1},{1,0},{2,3},{3,2},{4,5},{5,4},{6,7},{7,6},{8,9},{9,8},{10,11... | collective-permute-start | bytes 844808 | tf_op jit(solution)/shard_map/ppermute | solution.py:706
  45.1 33.1 %collective-permute-start.39 = (bf16[176,800]{1,0:T(8,128)(2,1)S(1)}, bf16[176,800]{1,0:T(8,128)(2,1)S(1)}, u32[]{:S(2)}, u32[]{:S(2)}) collective-permute-start(bf16[176,800]{1,0:T(8,128)(2,1)S(1)} %fusion.23), channel_id=1, source_target_pairs={{0,2},{1,3},{2,0},{3,1},{4,6},{5,7},{6,4},{7,5},{8,10},{9,11},{10,... | collective-permute-start | bytes 844808 | tf_op jit(solution)/shard_map/ppermute | solution.py:706
  45.1 33.1 %collective-permute-start.40 = (bf16[176,800]{1,0:T(8,128)(2,1)S(1)}, bf16[176,800]{1,0:T(8,128)(2,1)S(1)}, u32[]{:S(2)}, u32[]{:S(2)}) collective-permute-start(bf16[176,800]{1,0:T(8,128)(2,1)S(1)} %fusion.23), channel_id=1, source_target_pairs={{0,3},{1,2},{2,1},{3,0},{4,7},{5,6},{6,5},{7,4},{8,11},{9,10},{10,... | collective-permute-start | bytes 844808 | tf_op jit(solution)/shard_map/ppermute | solution.py:706
  62.0 17.7 %collective-permute-start.37 = (bf16[176,800]{1,0:T(8,128)(2,1)S(1)}, bf16[176,800]{1,0:T(8,128)(2,1)S(1)}, u32[]{:S(2)}, u32[]{:S(2)}) collective-permute-start(bf16[176,800]{1,0:T(8,128)(2,1)S(1)} %fusion.23), channel_id=1, source_target_pairs={{0,1},{1,0},{2,3},{3,2},{4,5},{5,4},{6,7},{7,6},{8,9},{9,8},{10,11... | collective-permute-start | bytes 844808 | tf_op jit(solution)/shard_map/ppermute | solution.py:706
  62.2 18.0 %collective-permute-start.9 = (bf16[112,800]{1,0:T(8,128)(2,1)}, bf16[112,800]{1,0:T(8,128)(2,1)S(1)}, u32[]{:S(2)}, u32[]{:S(2)}) collective-permute-start(bf16[112,800]{1,0:T(8,128)(2,1)} %collective-permute-done.7.refs_10_), channel_id=1, source_target_pairs={{0,8},{4,12},{8,0},{12,4},{16,24},{20,28},{24,16},{28,20},{1,9},{5... | collective-permute-start | bytes 537608 | tf_op jit(solution)/shard_map/ppermute | solution.py:706
  64.1 18.0 %collective-permute-start.13 = (bf16[112,800]{1,0:T(8,128)(2,1)}, bf16[112,800]{1,0:T(8,128)(2,1)S(1)}, u32[]{:S(2)}, u32[]{:S(2)}) collective-permute-start(bf16[112,800]{1,0:T(8,128)(2,1)} %collective-permute-done.11.refs_14_), channel_id=1, source_target_pairs={{0,8},{4,12},{8,0},{12,4},{16,24},{20,28},{24,16},{28,20},{1,9},{5... | collective-permute-start | bytes 537608 | tf_op jit(solution)/shard_map/ppermute | solution.py:706
  79.7 19.9 %collective-permute-start.22 = (bf16[2,176,800]{2,1,0:T(8,128)(2,1)}, bf16[2,176,800]{2,1,0:T(8,128)(2,1)}, u32[]{:S(2)}, u32[]{:S(2)}) collective-permute-start(bf16[2,176,800]{2,1,0:T(8,128)(2,1)} %pad_maximum_fusion.1.refs_14_), channel_id=1, source_target_pairs={{0,8},{4,12},{8,0},{12,4},{16,24},{20,28},{24,16},{28,20},{1,9},{5... | collective-permute-start | bytes 1689608 | tf_op jit(solution)/shard_map/ppermute | solution.py:706
  80.2 19.4 %collective-permute-start.19 = (bf16[2,176,800]{2,1,0:T(8,128)(2,1)}, bf16[2,176,800]{2,1,0:T(8,128)(2,1)}, u32[]{:S(2)}, u32[]{:S(2)}) collective-permute-start(bf16[2,176,800]{2,1,0:T(8,128)(2,1)} %pad_maximum_fusion.refs_6_), channel_id=1, source_target_pairs={{0,16},{4,20},{8,24},{12,28},{16,0},{20,4},{24,8},{28,12},{1,17},{... | collective-permute-start | bytes 1689608 | tf_op jit(solution)/shard_map/ppermute | solution.py:706
  86.1 26.9 %collective-permute-start.41 = (bf16[2,176,800]{2,1,0:T(8,128)(2,1)S(1)}, bf16[2,176,800]{2,1,0:T(8,128)(2,1)S(1)}, u32[]{:S(2)}, u32[]{:S(2)}) collective-permute-start(bf16[2,176,800]{2,1,0:T(8,128)(2,1)S(1)} %pad_maximum_fusion.3.refs_10_), channel_id=1, source_target_pairs={{0,8},{4,12},{8,0},{12,4},{16,24},{20,28},{24,16},{28,20},{1,9},{5... | collective-permute-start | bytes 1689608 | tf_op jit(solution)/shard_map/ppermute | solution.py:706
  87.7 14.0 %collective-permute-start.2 = (bf16[112,800]{1,0:T(8,128)(2,1)S(1)}, bf16[112,800]{1,0:T(8,128)(2,1)}, u32[]{:S(2)}, u32[]{:S(2)}) collective-permute-start(bf16[112,800]{1,0:T(8,128)(2,1)S(1)} %collective-permute-done.1.refs_4_), channel_id=1, source_target_pairs={{0,4},{4,0},{8,12},{12,8},{16,20},{20,16},{24,28},{28,24},{1,5},{5... | collective-permute-start | bytes 537608 | tf_op jit(solution)/shard_map/ppermute | solution.py:706
  87.9 15.4 %collective-permute-start.10 = (bf16[112,800]{1,0:T(8,128)(2,1)S(1)}, bf16[112,800]{1,0:T(8,128)(2,1)}, u32[]{:S(2)}, u32[]{:S(2)}) collective-permute-start(bf16[112,800]{1,0:T(8,128)(2,1)S(1)} %collective-permute-done.9.refs_12_), channel_id=1, source_target_pairs={{0,4},{4,0},{8,12},{12,8},{16,20},{20,16},{24,28},{28,24},{1,5},{5... | collective-permute-start | bytes 537608 | tf_op jit(solution)/shard_map/ppermute | solution.py:706
  101.7 33.9 %collective-permute-start.38 = (bf16[2,176,800]{2,1,0:T(8,128)(2,1)S(1)}, bf16[2,176,800]{2,1,0:T(8,128)(2,1)S(1)}, u32[]{:S(2)}, u32[]{:S(2)}) collective-permute-start(bf16[2,176,800]{2,1,0:T(8,128)(2,1)S(1)} %pad_maximum_fusion.2.refs_2_), channel_id=1, source_target_pairs={{0,16},{4,20},{8,24},{12,28},{16,0},{20,4},{24,8},{28,12},{1,17},{... | collective-permute-start | bytes 1689608 | tf_op jit(solution)/shard_map/ppermute | solution.py:706
  103.3 44.4 %collective-permute-start.26 = (bf16[2,176,800]{2,1,0:T(8,128)(2,1)}, bf16[2,176,800]{2,1,0:T(8,128)(2,1)S(1)}, u32[]{:S(2)}, u32[]{:S(2)}) collective-permute-start(bf16[2,176,800]{2,1,0:T(8,128)(2,1)} %pad_maximum_fusion.refs_6_), channel_id=1, source_target_pairs={{0,8},{4,12},{8,0},{12,4},{16,24},{20,28},{24,16},{28,20},{1,9},{5... | collective-permute-start | bytes 1689608 | tf_op jit(solution)/shard_map/ppermute | solution.py:706
  104.9 42.9 %collective-permute-start.29 = (bf16[2,176,800]{2,1,0:T(8,128)(2,1)}, bf16[2,176,800]{2,1,0:T(8,128)(2,1)}, u32[]{:S(2)}, u32[]{:S(2)}) collective-permute-start(bf16[2,176,800]{2,1,0:T(8,128)(2,1)} %collective-permute-done.19.refs_10_), channel_id=1, source_target_pairs={{0,8},{4,12},{8,0},{12,4},{16,24},{20,28},{24,16},{28,20},{1,9},{5... | collective-permute-start | bytes 1689608 | tf_op jit(solution)/shard_map/ppermute | solution.py:706
  105.4 42.8 %collective-permute-start.33 = (bf16[2,176,800]{2,1,0:T(8,128)(2,1)}, bf16[2,176,800]{2,1,0:T(8,128)(2,1)}, u32[]{:S(2)}, u32[]{:S(2)}) collective-permute-start(bf16[2,176,800]{2,1,0:T(8,128)(2,1)} %pad_maximum_fusion.1.refs_14_), channel_id=1, source_target_pairs={{0,16},{4,20},{8,24},{12,28},{16,0},{20,4},{24,8},{28,12},{1,17},{... | collective-permute-start | bytes 1689608 | tf_op jit(solution)/shard_map/ppermute | solution.py:706
  113.0 35.5 %collective-permute-start.35 = (bf16[2,176,800]{2,1,0:T(8,128)(2,1)}, bf16[2,176,800]{2,1,0:T(8,128)(2,1)}, u32[]{:S(2)}, u32[]{:S(2)}) collective-permute-start(bf16[2,176,800]{2,1,0:T(8,128)(2,1)} %collective-permute-done.22.refs_16_), channel_id=1, source_target_pairs={{0,16},{4,20},{8,24},{12,28},{16,0},{20,4},{24,8},{28,12},{1,17},{... | collective-permute-start | bytes 1689608 | tf_op jit(solution)/shard_map/ppermute | solution.py:706
  148.5 17.0 %collective-permute-start.43 = (bf16[2,176,800]{2,1,0:T(8,128)(2,1)S(1)}, bf16[2,176,800]{2,1,0:T(8,128)(2,1)S(1)}, u32[]{:S(2)}, u32[]{:S(2)}) collective-permute-start(bf16[2,176,800]{2,1,0:T(8,128)(2,1)S(1)} %pad_maximum_fusion.2.refs_2_), channel_id=1, source_target_pairs={{0,8},{4,12},{8,0},{12,4},{16,24},{20,28},{24,16},{28,20},{1,9},{5... | collective-permute-start | bytes 1689608 | tf_op jit(solution)/shard_map/ppermute | solution.py:706
  150.1 33.2 %collective-permute-start.42 = (bf16[2,176,800]{2,1,0:T(8,128)(2,1)S(1)}, bf16[2,176,800]{2,1,0:T(8,128)(2,1)S(1)}, u32[]{:S(2)}, u32[]{:S(2)}) collective-permute-start(bf16[2,176,800]{2,1,0:T(8,128)(2,1)S(1)} %pad_maximum_fusion.2.refs_2_), channel_id=1, source_target_pairs={{0,4},{4,0},{8,12},{12,8},{16,20},{20,16},{24,28},{28,24},{1,5},{5... | collective-permute-start | bytes 1689608 | tf_op jit(solution)/shard_map/ppermute | solution.py:706
  150.6 27.7 %collective-permute-start.46 = (bf16[2,176,800]{2,1,0:T(8,128)(2,1)S(1)}, bf16[2,176,800]{2,1,0:T(8,128)(2,1)S(1)}, u32[]{:S(2)}, u32[]{:S(2)}) collective-permute-start(bf16[2,176,800]{2,1,0:T(8,128)(2,1)S(1)} %collective-permute-done.38.refs_6_), channel_id=1, source_target_pairs={{0,8},{4,12},{8,0},{12,4},{16,24},{20,28},{24,16},{28,20},{1,9},{5... | collective-permute-start | bytes 1689608 | tf_op jit(solution)/shard_map/ppermute | solution.py:706
  152.1 31.7 %collective-permute-start.45 = (bf16[2,176,800]{2,1,0:T(8,128)(2,1)S(1)}, bf16[2,176,800]{2,1,0:T(8,128)(2,1)S(1)}, u32[]{:S(2)}, u32[]{:S(2)}) collective-permute-start(bf16[2,176,800]{2,1,0:T(8,128)(2,1)S(1)} %collective-permute-done.38.refs_6_), channel_id=1, source_target_pairs={{0,4},{4,0},{8,12},{12,8},{16,20},{20,16},{24,28},{28,24},{1,5},{5... | collective-permute-start | bytes 1689608 | tf_op jit(solution)/shard_map/ppermute | solution.py:706
  153.3 25.0 %collective-permute-start.50 = (bf16[2,176,800]{2,1,0:T(8,128)(2,1)S(1)}, bf16[2,176,800]{2,1,0:T(8,128)(2,1)S(1)}, u32[]{:S(2)}, u32[]{:S(2)}) collective-permute-start(bf16[2,176,800]{2,1,0:T(8,128)(2,1)S(1)} %pad_maximum_fusion.3.refs_10_), channel_id=1, source_target_pairs={{0,16},{4,20},{8,24},{12,28},{16,0},{20,4},{24,8},{28,12},{1,17},{... | collective-permute-start | bytes 1689608 | tf_op jit(solution)/shard_map/ppermute | solution.py:706
  165.5 17.8 %collective-permute-start.52 = (bf16[2,176,800]{2,1,0:T(8,128)(2,1)S(1)}, bf16[2,176,800]{2,1,0:T(8,128)(2,1)S(1)}, u32[]{:S(2)}, u32[]{:S(2)}) collective-permute-start(bf16[2,176,800]{2,1,0:T(8,128)(2,1)S(1)} %collective-permute-done.41.refs_12_), channel_id=1, source_target_pairs={{0,16},{4,20},{8,24},{12,28},{16,0},{20,4},{24,8},{28,12},{1,17},{... | collective-permute-start | bytes 1689608 | tf_op jit(solution)/shard_map/ppermute | solution.py:706
  187.7 41.5 %collective-permute-start.49 = (bf16[2,176,800]{2,1,0:T(8,128)(2,1)S(1)}, bf16[2,176,800]{2,1,0:T(8,128)(2,1)S(1)}, u32[]{:S(2)}, u32[]{:S(2)}) collective-permute-start(bf16[2,176,800]{2,1,0:T(8,128)(2,1)S(1)} %collective-permute-done.41.refs_12_), channel_id=1, source_target_pairs={{0,4},{4,0},{8,12},{12,8},{16,20},{20,16},{24,28},{28,24},{1,5},{5... | collective-permute-start | bytes 1689608 | tf_op jit(solution)/shard_map/ppermute | solution.py:706
  188.1 41.2 %collective-permute-start.44 = (bf16[2,176,800]{2,1,0:T(8,128)(2,1)S(1)}, bf16[2,176,800]{2,1,0:T(8,128)(2,1)S(1)}, u32[]{:S(2)}, u32[]{:S(2)}) collective-permute-start(bf16[2,176,800]{2,1,0:T(8,128)(2,1)S(1)} %collective-permute-done.43.refs_4_), channel_id=1, source_target_pairs={{0,4},{4,0},{8,12},{12,8},{16,20},{20,16},{24,28},{28,24},{1,5},{5... | collective-permute-start | bytes 1689608 | tf_op jit(solution)/shard_map/ppermute | solution.py:706
  188.3 41.1 %collective-permute-start.47 = (bf16[2,176,800]{2,1,0:T(8,128)(2,1)}, bf16[2,176,800]{2,1,0:T(8,128)(2,1)}, u32[]{:S(2)}, u32[]{:S(2)}) collective-permute-start(bf16[2,176,800]{2,1,0:T(8,128)(2,1)} %copy-done.17), channel_id=1, source_target_pairs={{0,4},{4,0},{8,12},{12,8},{16,20},{20,16},{24,28},{28,24},{1,5},{5... | collective-permute-start | bytes 1689608 | tf_op jit(solution)/shard_map/ppermute | solution.py:706
  188.6 40.8 %collective-permute-start.51 = (bf16[2,176,800]{2,1,0:T(8,128)(2,1)}, bf16[2,176,800]{2,1,0:T(8,128)(2,1)}, u32[]{:S(2)}, u32[]{:S(2)}) collective-permute-start(bf16[2,176,800]{2,1,0:T(8,128)(2,1)} %copy-done.19), channel_id=1, source_target_pairs={{0,4},{4,0},{8,12},{12,8},{16,20},{20,16},{24,28},{28,24},{1,5},{5... | collective-permute-start | bytes 1689608 | tf_op jit(solution)/shard_map/ppermute | solution.py:706
  188.8 40.6 %collective-permute-start.53 = (bf16[2,176,800]{2,1,0:T(8,128)(2,1)}, bf16[2,176,800]{2,1,0:T(8,128)(2,1)}, u32[]{:S(2)}, u32[]{:S(2)}) collective-permute-start(bf16[2,176,800]{2,1,0:T(8,128)(2,1)} %copy-done.20), channel_id=1, source_target_pairs={{0,4},{4,0},{8,12},{12,8},{16,20},{20,16},{24,28},{28,24},{1,5},{5... | collective-permute-start | bytes 1689608 | tf_op jit(solution)/shard_map/ppermute | solution.py:706
  348.4 55.1 %collective-permute-start.56 = (bf16[16,176,800]{2,1,0:T(8,128)(2,1)}, bf16[16,176,800]{2,1,0:T(8,128)(2,1)}, u32[]{:S(2)}, u32[]{:S(2)}) collective-permute-start(bf16[16,176,800]{2,1,0:T(8,128)(2,1)} %get-tuple-element.116), channel_id=1, source_target_pairs={{0,4},{4,0},{8,12},{12,8},{16,20},{20,16},{24,28},{28,24},{1,5},{5... | collective-permute-start | bytes 13516808 | tf_op jit(solution)/shard_map/ppermute | solution.py:706
  408.0 32.2 %collective-permute-start.57 = (bf16[2,2,176,800]{3,2,1,0:T(8,128)(2,1)}, bf16[2,2,176,800]{3,2,1,0:T(8,128)(2,1)S(1)}, u32[]{:S(2)}, u32[]{:S(2)}) collective-permute-start(bf16[2,2,176,800]{3,2,1,0:T(8,128)(2,1)} %bitcast.26), channel_id=1, source_target_pairs={{0,16},{4,20},{8,24},{12,28},{16,0},{20,4},{24,8},{28,12},{1,17},{... | collective-permute-start | bytes 3379208 | tf_op jit(solution)/shard_map/ppermute | solution.py:706
  411.5 28.6 %collective-permute-start.58 = (bf16[2,2,176,800]{3,2,1,0:T(8,128)(2,1)}, bf16[2,2,176,800]{3,2,1,0:T(8,128)(2,1)S(1)}, u32[]{:S(2)}, u32[]{:S(2)}) collective-permute-start(bf16[2,2,176,800]{3,2,1,0:T(8,128)(2,1)} %bitcast.27), channel_id=1, source_target_pairs={{0,8},{4,12},{8,0},{12,4},{16,24},{20,28},{24,16},{28,20},{1,9},{5... | collective-permute-start | bytes 3379208 | tf_op jit(solution)/shard_map/ppermute | solution.py:706
  444.2 45.3 %collective-permute-start.63 = (bf16[16,176,800]{2,1,0:T(8,128)(2,1)}, bf16[16,176,800]{2,1,0:T(8,128)(2,1)}, u32[]{:S(2)}, u32[]{:S(2)}) collective-permute-start(bf16[16,176,800]{2,1,0:T(8,128)(2,1)} %get-tuple-element.131), channel_id=1, source_target_pairs={{0,4},{4,0},{8,12},{12,8},{16,20},{20,16},{24,28},{28,24},{1,5},{5... | collective-permute-start | bytes 13516808 | tf_op jit(solution)/shard_map/ppermute | solution.py:706
  447.0 40.2 %collective-permute-start.62 = (bf16[1,2,176,800]{3,2,1,0:T(8,128)(2,1)}, bf16[1,2,176,800]{3,2,1,0:T(8,128)(2,1)}, u32[]{:S(2)}, u32[]{:S(2)}) collective-permute-start(bf16[1,2,176,800]{3,2,1,0:T(8,128)(2,1)} %get-tuple-element.129), channel_id=1, source_target_pairs={{0,16},{4,20},{8,24},{12,28},{16,0},{20,4},{24,8},{28,12},{1,17},{... | collective-permute-start | bytes 1689608 | tf_op jit(solution)/shard_map/ppermute | solution.py:706
  448.3 37.0 %collective-permute-start.61 = (bf16[1,2,176,800]{3,2,1,0:T(8,128)(2,1)}, bf16[1,2,176,800]{3,2,1,0:T(8,128)(2,1)S(1)}, u32[]{:S(2)}, u32[]{:S(2)}) collective-permute-start(bf16[1,2,176,800]{3,2,1,0:T(8,128)(2,1)} %get-tuple-element.128), channel_id=1, source_target_pairs={{0,8},{4,12},{8,0},{12,4},{16,24},{20,28},{24,16},{28,20},{1,9},{5... | collective-permute-start | bytes 1689608 | tf_op jit(solution)/shard_map/ppermute | solution.py:706
  494.1 48.6 %collective-permute-start.67 = (bf16[2,2,176,800]{3,2,1,0:T(8,128)(2,1)}, bf16[2,2,176,800]{3,2,1,0:T(8,128)(2,1)}, u32[]{:S(2)}, u32[]{:S(2)}) collective-permute-start(bf16[2,2,176,800]{3,2,1,0:T(8,128)(2,1)} %bitcast.36), channel_id=1, source_target_pairs={{0,16},{4,20},{8,24},{12,28},{16,0},{20,4},{24,8},{28,12},{1,17},{... | collective-permute-start | bytes 3379208 | tf_op jit(solution)/shard_map/ppermute | solution.py:706
  494.9 47.9 %collective-permute-start.68 = (bf16[2,2,176,800]{3,2,1,0:T(8,128)(2,1)}, bf16[2,2,176,800]{3,2,1,0:T(8,128)(2,1)}, u32[]{:S(2)}, u32[]{:S(2)}) collective-permute-start(bf16[2,2,176,800]{3,2,1,0:T(8,128)(2,1)} %bitcast.37), channel_id=1, source_target_pairs={{0,8},{4,12},{8,0},{12,4},{16,24},{20,28},{24,16},{28,20},{1,9},{5... | collective-permute-start | bytes 3379208 | tf_op jit(solution)/shard_map/ppermute | solution.py:706
  496.5 49.9 %collective-permute-start.69 = (bf16[16,56,800]{2,1,0:T(8,128)(2,1)}, bf16[16,56,800]{2,1,0:T(8,128)(2,1)}, u32[]{:S(2)}, u32[]{:S(2)}) collective-permute-start(bf16[16,56,800]{2,1,0:T(8,128)(2,1)} %get-tuple-element.143), channel_id=1, source_target_pairs={{0,4},{4,0},{8,12},{12,8},{16,20},{20,16},{24,28},{28,24},{1,5},{5... | collective-permute-start | bytes 4300808 | tf_op jit(solution)/shard_map/ppermute | solution.py:706
  496.5 14.8 %collective-permute-start.64 = (bf16[176,800]{1,0:T(8,128)(2,1)}, bf16[176,800]{1,0:T(8,128)(2,1)}, u32[]{:S(2)}, u32[]{:S(2)}) collective-permute-start(bf16[176,800]{1,0:T(8,128)(2,1)} %fusion.24), channel_id=1, source_target_pairs={{0,1},{1,0},{2,3},{3,2},{4,5},{5,4},{6,7},{7,6},{8,9},{9,8},{10,11... | collective-permute-start | bytes 844808 | tf_op jit(solution)/shard_map/ppermute | solution.py:706
  508.3 32.9 %collective-permute-start.65 = (bf16[176,800]{1,0:T(8,128)(2,1)}, bf16[176,800]{1,0:T(8,128)(2,1)}, u32[]{:S(2)}, u32[]{:S(2)}) collective-permute-start(bf16[176,800]{1,0:T(8,128)(2,1)} %get-tuple-element.138), channel_id=1, source_target_pairs={{0,2},{1,3},{2,0},{3,1},{4,6},{5,7},{6,4},{7,5},{8,10},{9,11},{10,... | collective-permute-start | bytes 844808 | tf_op jit(solution)/shard_map/ppermute | solution.py:706
  511.3 29.9 %collective-permute-start.66 = (bf16[176,800]{1,0:T(8,128)(2,1)S(1)}, bf16[176,800]{1,0:T(8,128)(2,1)}, u32[]{:S(2)}, u32[]{:S(2)}) collective-permute-start(bf16[176,800]{1,0:T(8,128)(2,1)S(1)} %get-tuple-element.139), channel_id=1, source_target_pairs={{0,3},{1,2},{2,1},{3,0},{4,7},{5,6},{6,5},{7,4},{8,11},{9,10},{10,... | collective-permute-start | bytes 844808 | tf_op jit(solution)/shard_map/ppermute | solution.py:706
  551.7 52.0 %collective-permute-start.102 = (bf16[176,800]{1,0:T(8,128)(2,1)S(1)}, bf16[176,800]{1,0:T(8,128)(2,1)}, u32[]{:S(2)}, u32[]{:S(2)}) collective-permute-start(bf16[176,800]{1,0:T(8,128)(2,1)S(1)} %fusion.16.refs_1_), channel_id=1, source_target_pairs={{0,8},{4,12},{8,0},{12,4},{16,24},{20,28},{24,16},{28,20},{1,9},{5... | collective-permute-start | bytes 844808 | tf_op jit(solution)/shard_map/ppermute | solution.py:706
  553.4 39.9 %collective-permute-start.84 = (bf16[1,2,176,800]{3,2,1,0:T(8,128)(2,1)}, bf16[1,2,176,800]{3,2,1,0:T(8,128)(2,1)}, u32[]{:S(2)}, u32[]{:S(2)}) collective-permute-start(bf16[1,2,176,800]{3,2,1,0:T(8,128)(2,1)} %get-tuple-element.159), channel_id=1, source_target_pairs={{0,8},{4,12},{8,0},{12,4},{16,24},{20,28},{24,16},{28,20},{1,9},{5... | collective-permute-start | bytes 1689608 | tf_op jit(solution)/shard_map/ppermute | solution.py:706
  553.8 22.9 %collective-permute-start.70 = (bf16[2,2,56,800]{3,2,1,0:T(8,128)(2,1)}, bf16[2,2,56,800]{3,2,1,0:T(8,128)(2,1)}, u32[]{:S(2)}, u32[]{:S(2)}) collective-permute-start(bf16[2,2,56,800]{3,2,1,0:T(8,128)(2,1)} %bitcast.40), channel_id=1, source_target_pairs={{0,16},{4,20},{8,24},{12,28},{16,0},{20,4},{24,8},{28,12},{1,17},{... | collective-permute-start | bytes 1075208 | tf_op jit(solution)/shard_map/ppermute | solution.py:706
  555.1 28.4 %collective-permute-start.73 = (bf16[2,2,56,800]{3,2,1,0:T(8,128)(2,1)S(1)}, bf16[2,2,56,800]{3,2,1,0:T(8,128)(2,1)}, u32[]{:S(2)}, u32[]{:S(2)}) collective-permute-start(bf16[2,2,56,800]{3,2,1,0:T(8,128)(2,1)S(1)} %bitcast.146), channel_id=1, source_target_pairs={{0,8},{4,12},{8,0},{12,4},{16,24},{20,28},{24,16},{28,20},{1,9},{5... | collective-permute-start | bytes 1075208 | tf_op jit(solution)/shard_map/ppermute | solution.py:706
  556.7 14.1 %collective-permute-start.98 = (f32[24,800]{1,0:T(8,128)S(1)}, f32[24,800]{1,0:T(8,128)S(1)}, u32[]{:S(2)}, u32[]{:S(2)}) collective-permute-start(f32[24,800]{1,0:T(8,128)S(1)} %add.544), channel_id=1, source_target_pairs={{0,16},{4,20},{8,24},{12,28},{16,0},{20,4},{24,8},{28,12},{1,17},{... | collective-permute-start | bytes 230408 | tf_op jit(solution)/shard_map/ppermute | solution.py:706
  575.4 20.5 %collective-permute-start.86 = (bf16[1,2,176,800]{3,2,1,0:T(8,128)(2,1)}, bf16[1,2,176,800]{3,2,1,0:T(8,128)(2,1)}, u32[]{:S(2)}, u32[]{:S(2)}) collective-permute-start(bf16[1,2,176,800]{3,2,1,0:T(8,128)(2,1)} %get-tuple-element.160), channel_id=1, source_target_pairs={{0,16},{4,20},{8,24},{12,28},{16,0},{20,4},{24,8},{28,12},{1,17},{... | collective-permute-start | bytes 1689608 | tf_op jit(solution)/shard_map/ppermute | solution.py:706
  587.1 14.6 %collective-permute-start.74 = (bf16[1,2,56,800]{3,2,1,0:T(8,128)(2,1)}, bf16[1,2,56,800]{3,2,1,0:T(8,128)(2,1)}, u32[]{:S(2)}, u32[]{:S(2)}) collective-permute-start(bf16[1,2,56,800]{3,2,1,0:T(8,128)(2,1)} %get-tuple-element.364), channel_id=1, source_target_pairs={{0,16},{4,20},{8,24},{12,28},{16,0},{20,4},{24,8},{28,12},{1,17},{... | collective-permute-start | bytes 537608 | tf_op jit(solution)/shard_map/ppermute | solution.py:706
  597.4 24.2 %collective-permute-start.87 = (bf16[176,800]{1,0:T(8,128)(2,1)S(1)}, bf16[176,800]{1,0:T(8,128)(2,1)S(1)}, u32[]{:S(2)}, u32[]{:S(2)}) collective-permute-start(bf16[176,800]{1,0:T(8,128)(2,1)S(1)} %get-tuple-element.367), channel_id=1, source_target_pairs={{0,2},{1,3},{2,0},{3,1},{4,6},{5,7},{6,4},{7,5},{8,10},{9,11},{10,... | collective-permute-start | bytes 844808 | tf_op jit(solution)/shard_map/ppermute | solution.py:706
  598.3 23.3 %collective-permute-start.88 = (bf16[176,800]{1,0:T(8,128)(2,1)S(1)}, bf16[176,800]{1,0:T(8,128)(2,1)S(1)}, u32[]{:S(2)}, u32[]{:S(2)}) collective-permute-start(bf16[176,800]{1,0:T(8,128)(2,1)S(1)} %get-tuple-element.368), channel_id=1, source_target_pairs={{0,3},{1,2},{2,1},{3,0},{4,7},{5,6},{6,5},{7,4},{8,11},{9,10},{10,... | collective-permute-start | bytes 844808 | tf_op jit(solution)/shard_map/ppermute | solution.py:706
  601.7 26.6 %collective-permute-start.104 = (bf16[176,800]{1,0:T(8,128)(2,1)S(1)}, bf16[176,800]{1,0:T(8,128)(2,1)S(1)}, u32[]{:S(2)}, u32[]{:S(2)}) collective-permute-start(bf16[176,800]{1,0:T(8,128)(2,1)S(1)} %fusion.16.refs_1_), channel_id=1, source_target_pairs={{0,16},{4,20},{8,24},{12,28},{16,0},{20,4},{24,8},{28,12},{1,17},{... | collective-permute-start | bytes 844808 | tf_op jit(solution)/shard_map/ppermute | solution.py:706
  603.6 32.3 %collective-permute-start.101 = (bf16[176,800]{1,0:T(8,128)(2,1)S(1)}, bf16[176,800]{1,0:T(8,128)(2,1)S(1)}, u32[]{:S(2)}, u32[]{:S(2)}) collective-permute-start(bf16[176,800]{1,0:T(8,128)(2,1)S(1)} %fusion.16.refs_1_), channel_id=1, source_target_pairs={{0,4},{4,0},{8,12},{12,8},{16,20},{20,16},{24,28},{28,24},{1,5},{5... | collective-permute-start | bytes 844808 | tf_op jit(solution)/shard_map/ppermute | solution.py:706
  606.4 30.6 %collective-permute-start.106 = (bf16[176,800]{1,0:T(8,128)(2,1)}, bf16[176,800]{1,0:T(8,128)(2,1)S(1)}, u32[]{:S(2)}, u32[]{:S(2)}) collective-permute-start(bf16[176,800]{1,0:T(8,128)(2,1)} %collective-permute-done.102.refs_3_), channel_id=1, source_target_pairs={{0,16},{4,20},{8,24},{12,28},{16,0},{20,4},{24,8},{28,12},{1,17},{... | collective-permute-start | bytes 844808 | tf_op jit(solution)/shard_map/ppermute | solution.py:706
  637.0 22.2 %collective-permute-start.92 = (bf16[176,800]{1,0:T(8,128)(2,1)S(1)}, bf16[176,800]{1,0:T(8,128)(2,1)S(1)}, u32[]{:S(2)}, u32[]{:S(2)}) collective-permute-start(bf16[176,800]{1,0:T(8,128)(2,1)S(1)} %fusion.13.refs_1_), channel_id=1, source_target_pairs={{0,16},{4,20},{8,24},{12,28},{16,0},{20,4},{24,8},{28,12},{1,17},{... | collective-permute-start | bytes 844808 | tf_op jit(solution)/shard_map/ppermute | solution.py:706
  638.5 21.1 %collective-permute-start.94 = (bf16[176,800]{1,0:T(8,128)(2,1)S(1)}, bf16[176,800]{1,0:T(8,128)(2,1)S(1)}, u32[]{:S(2)}, u32[]{:S(2)}) collective-permute-start(bf16[176,800]{1,0:T(8,128)(2,1)S(1)} %collective-permute-done.90.refs_3_), channel_id=1, source_target_pairs={{0,16},{4,20},{8,24},{12,28},{16,0},{20,4},{24,8},{28,12},{1,17},{... | collective-permute-start | bytes 844808 | tf_op jit(solution)/shard_map/ppermute | solution.py:706
  639.8 16.4 %collective-permute-start.80 = (bf16[56,800]{1,0:T(8,128)(2,1)S(1)}, bf16[56,800]{1,0:T(8,128)(2,1)S(1)}, u32[]{:S(2)}, u32[]{:S(2)}) collective-permute-start(bf16[56,800]{1,0:T(8,128)(2,1)S(1)} %fusion.32.refs_1_), channel_id=1, source_target_pairs={{0,16},{4,20},{8,24},{12,28},{16,0},{20,4},{24,8},{28,12},{1,17},{... | collective-permute-start | bytes 268808 | tf_op jit(solution)/shard_map/ppermute | solution.py:706
  641.1 15.1 %collective-permute-start.77 = (bf16[56,800]{1,0:T(8,128)(2,1)S(1)}, bf16[56,800]{1,0:T(8,128)(2,1)S(1)}, u32[]{:S(2)}, u32[]{:S(2)}) collective-permute-start(bf16[56,800]{1,0:T(8,128)(2,1)S(1)} %fusion.32.refs_1_), channel_id=1, source_target_pairs={{0,4},{4,0},{8,12},{12,8},{16,20},{20,16},{24,28},{28,24},{1,5},{5... | collective-permute-start | bytes 268808 | tf_op jit(solution)/shard_map/ppermute | solution.py:706
  641.3 16.4 %collective-permute-start.82 = (bf16[56,800]{1,0:T(8,128)(2,1)S(1)}, bf16[56,800]{1,0:T(8,128)(2,1)S(1)}, u32[]{:S(2)}, u32[]{:S(2)}) collective-permute-start(bf16[56,800]{1,0:T(8,128)(2,1)S(1)} %collective-permute-done.78.refs_3_), channel_id=1, source_target_pairs={{0,16},{4,20},{8,24},{12,28},{16,0},{20,4},{24,8},{28,12},{1,17},{... | collective-permute-start | bytes 268808 | tf_op jit(solution)/shard_map/ppermute | solution.py:706
  (106 other events, 1615.6 us)

commit v2 on v1

--- a/solution.py
+++ b/solution.py
@@ -118,16 +118,12 @@
         copy.wait()
 
 
-def fetch_shards(place, pieces, fsdp_count, landed, semaphores):
-    seq_count = len(pieces) // 2
-    half_count = fsdp_count // 2
+def fetch_shards(place, own, parts, pieces, origins, landed, semaphores):
     sources, spots = [], []
-    for index, piece in enumerate(pieces):
-        half, differs = index // seq_count, index % seq_count
-        for within in range(half_count):
-            shard = place[0] ^ (half * half_count + within)
-            sources.append(piece.at[within])
-            spots.append(shard * seq_count + (place[2] ^ differs))
+    for piece, entries in zip(pieces, origins):
+        for index, (far, differs) in enumerate(entries):
+            sources.append(piece.at[index])
+            spots.append((place[0] ^ far) * parts + (own ^ differs))
     fetch(sources, spots, landed, semaphores)
 
 
@@ -145,23 +141,18 @@
             done += size
 
 
-def enter_encoder_kernel(parts, spacing, place, *refs):
-    refs = list(refs)
-    stream = refs.pop(0)
-    pieces = [refs.pop(0) for _ in range(len(refs) - 8)]
+def enter_encoder_kernel(origins, spacing, place, stream, *refs):
+    pieces, refs = refs[:-8], refs[-8:]
     wide, inner, first, hidden, second, project, landed, semaphores = refs
-    shard_rows = project.shape[0] * parts // len(pieces)
 
     @pl.when(pl.program_id(0) == 0)
     def _():
-        spots = [
-            (place[0] ^ (index // parts)) * parts + (place[1] ^ (index % parts))
-            for index in range(len(pieces))
-        ]
-        fetch(pieces, spots, landed, semaphores)
-        for index in range(len(pieces)):
-            start = index // parts * shard_rows + index % parts * spacing
-            project[start : start + landed.shape[1], :] = landed[index]
+        fetch_shards(place, place[1], PARTS, pieces, origins, landed, semaphores)
+        shard_rows = project.shape[0] * PARTS // landed.shape[0]
+        part = shard_rows - (PARTS - 1) * spacing
+        for index in range(landed.shape[0]):
+            start = index // PARTS * shard_rows + index % PARTS * spacing
+            project[start : start + part, :] = landed[index, :part, :]
 
     enter_kernel(stream, project, wide, inner, first, hidden, second)
 
@@ -205,19 +196,22 @@
         shards.spread(own, start, part, write)
 
 
-def middle_kernel(offsets, fsdp_count, place, second_in, low, high, masks, stream, *refs):
-    pieces, refs = refs[:-12], refs[-12:]
-    enc_wide, enc_inner, mixed, third, middle, expand, flat = refs[:7]
-    extended, columns, kernel, landed, semaphores = refs[7:]
+def middle_kernel(offsets, counts, origins, place, second_in, low, high, masks, stream, *refs):
+    pieces, refs = refs[:-13], refs[-13:]
+    enc_wide, enc_inner, mixed, third, middle, expand, flat, project = refs[:8]
+    extended, columns, kernel, landed, semaphores = refs[8:]
     row_count = stream.shape[0]
     front = low.shape[0]
 
     @pl.when(pl.program_id(0) == 0)
     def _():
-        fetch_shards(place, pieces, fsdp_count, landed, semaphores)
+        seq_count, fsdp_count = counts
+        fetch_shards(place, place[2], seq_count, pieces, origins, landed, semaphores)
         shards = Shards(landed, fsdp_count)
         unpack_kernel(shards, 0, len(offsets), kernel, flat)
-        unpack_expand(shards, kernel.shape[0] // fsdp_count, expand)
+        start = kernel.shape[0] // fsdp_count
+        unpack_expand(shards, start, expand)
+        unpack_rows(shards, start + expand.shape[0] * 2 // fsdp_count, project)
 
     extended[:front, :] = low[...]
     extended[front : front + row_count, :] = second_in[...]
@@ -240,45 +234,22 @@
     by_chunks(row_count, make_middle)
 
 
-def enter_decoder_kernel(taps, fsdp_count, place, stream, *refs):
-    pieces, refs = refs[:-11], refs[-11:]
-    wide, inner, first, hidden, second, project, kernel, flat, expand, landed, semaphores = refs
-
-    @pl.when(pl.program_id(0) == 0)
-    def _():
-        fetch_shards(place, pieces, fsdp_count, landed, semaphores)
-        shards = Shards(landed, fsdp_count)
-        start = project.shape[0] // fsdp_count
-        unpack_rows(shards, 0, project)
-        unpack_kernel(shards, start, taps, kernel, flat)
-        unpack_expand(shards, start + kernel.shape[0] // fsdp_count, expand)
-
-    enter_kernel(stream, project, wide, inner, first, hidden, second)
-
-
-def turn_kernel(
-    offsets,
-    second,
-    low,
-    masks,
-    cotangent,
-    kernel,
-    expand,
-    inner,
-    third,
-    grad_mixed,
-    grad_expand,
-    sums_wide,
-    sums_inner,
-    extended,
-    columns,
-    mixed,
-    grad_third,
-    total,
-):
+def turn_kernel(offsets, counts, origins, place, second, low, masks, cotangent, *refs):
+    pieces, refs = refs[:-16], refs[-16:]
+    inner, third, grad_mixed, grad_expand, flat, expand, sums_wide, sums_inner = refs[:8]
+    extended, columns, mixed, grad_third, total, kernel, landed, semaphores = refs[8:]
     row_count = cotangent.shape[0]
     front = low.shape[0]
     clear_first(total, sums_wide, sums_inner)
+
+    @pl.when(pl.program_id(0) == 0)
+    def _():
+        seq_count, fsdp_count = counts
+        fetch_shards(place, place[2], seq_count, pieces, origins, landed, semaphores)
+        shards = Shards(landed, fsdp_count)
+        unpack_kernel(shards, 0, len(offsets), kernel, flat)
+        unpack_expand(shards, kernel.shape[0] // fsdp_count, expand)
+
     extended[:front, :] = low[...]
     extended[front : front + row_count, :] = second[...]
     fill_columns(columns, extended, masks, offsets, front, row_count)
@@ -489,35 +460,33 @@
     offsets,
     front,
     back,
-    counts,
-    place,
     grad_mixed,
     low,
     high,
     masks,
     hidden,
-    first,
     flat,
     inner,
     grad_hidden,
-    keep,
-    send,
     sums_inner,
     extended,
     columns,
     grad_second,
-    total_project,
 ):
-    clear_first(total_project, sums_inner)
+    clear_first(sums_inner)
     back_columns(offsets, front, back, grad_mixed, low, high, masks, extended, columns)
     grad_second[...] = dot(columns[...], flat[...], NT)
     hidden_grad(hidden, inner, grad_second, grad_hidden, sums_inner)
-    total_project[...] += dot(first[...], grad_hidden[...], TN)
+
+
+def project_grad_kernel(counts, place, first, grad_hidden, keep, send, total):
+    clear_first(total)
+    total[...] += dot(first[...], grad_hidden[...], TN)
 
     @at_last
     def _():
         sections = Sections(*counts)
-        sections.rows_of(total_project)
+        sections.rows_of(total)
         pack(place, sections, keep, send)
 
 
@@ -606,12 +575,13 @@
     by_chunks(row_count, make_grad)
 
 
-def finish_kernel(layout, factor, place, *refs):
-    count = len(refs) - len(layout) - 1
+def finish_kernel(layout, factor, indices, place, *refs):
+    count = len(indices)
     pieces, outs, landed = refs[:count], refs[count:-1], refs[-1]
     part = landed.shape[1]
-    for index, piece in enumerate(pieces):
-        landed[place[2] ^ index] = piece[...]
+    for piece, entries in zip(pieces, indices):
+        for spot, index in enumerate(entries):
+            landed[place[2] ^ index] = piece[spot]
 
     def write(out, where, columns, start, rows):
         done = 0
@@ -638,9 +608,9 @@
             write(out, None, slice(0, width), start, out.shape[0])
 
 
-def stepped(array):
+def stepped(array, offset):
     rest = (0,) * (array.ndim - 1)
-    return pl.BlockSpec((None,) + array.shape[1:], lambda step: (step,) + rest)
+    return pl.BlockSpec((None,) + array.shape[1:], lambda step: (step + offset,) + rest)
 
 
 def held(array):
@@ -648,29 +618,52 @@
     return pl.BlockSpec(array.shape, lambda step: zeros, pipeline_mode=pl.Buffered(1))
 
 
-def call(body, steps, moving, fixed, outs, sums, scratch, flops, loose=(), place=None, semaphores=0):
+def call(
+    body,
+    steps,
+    moving,
+    fixed,
+    outs,
+    sums,
+    scratch,
+    flops,
+    loose=(),
+    place=None,
+    semaphores=0,
+    offset=0,
+    carried=(),
+):
     out_shapes = [jax.ShapeDtypeStruct(shape, kind) for shape, kind in outs]
     sum_shapes = [jax.ShapeDtypeStruct(shape, kind) for shape, kind in sums]
     operands = list(moving) + list(loose) + list(fixed)
     traffic = sum(
         entry.size * entry.dtype.itemsize for entry in operands + out_shapes + sum_shapes
     )
-    in_specs = [stepped(entry) for entry in moving]
+    in_specs = [stepped(entry, offset) for entry in moving]
     in_specs += [pl.BlockSpec(memory_space=pl.ANY) for _ in loose]
     in_specs += [held(entry) for entry in fixed]
     if place is not None:
         operands = [place] + operands
         in_specs = [pl.BlockSpec(memory_space=pltpu.SMEM)] + in_specs
+    count = len(operands)
+    operands += list(carried)
+    in_specs += [pl.BlockSpec(memory_space=pl.ANY) for _ in carried]
     scratch_shapes = [pltpu.VMEM(shape, kind) for shape, kind in scratch]
     if semaphores:
         scratch_shapes.append(pltpu.SemaphoreType.DMA((semaphores,)))
+
+    def kernel(*refs):
+        body(*refs[:count], *refs[count + len(carried) :])
+
     return pl.pallas_call(
-        body,
+        kernel,
         grid=(steps,),
         in_specs=in_specs,
-        out_specs=[stepped(entry) for entry in out_shapes] + [held(entry) for entry in sum_shapes],
+        out_specs=[stepped(entry, offset) for entry in out_shapes]
+        + [held(entry) for entry in sum_shapes],
         out_shape=out_shapes + sum_shapes,
         scratch_shapes=scratch_shapes,
+        input_output_aliases={count + index: index for index in range(len(carried))},
         compiler_params=pltpu.CompilerParams(
             dimension_semantics=("arbitrary",), vmem_limit_bytes=VMEM_LIMIT
         ),
@@ -748,47 +741,92 @@
     return part, (rows - part) // (PARTS - 1)
 
 
-def gather_half(shard):
+def tiled(block):
+    return block.reshape(block.shape[0] // 8, 8, block.shape[1])
+
+
+class Spread:
+    def __init__(self, columns, fars, bits):
+        self.parts = [jnp.stack(columns)]
+        self.bits, self.step = bits, 0
+        self.origins = [(far, 0) for far in fars]
+        self.arrays, self.all_origins = [], []
+
+    def moved(self, entries, bit):
+        return [(far, differs ^ bit) for far, differs in entries]
+
+    def advance(self, block):
+        bit = self.bits[self.step]
+        other = exchanged(block, "seq", bit)
+        more = self.moved(self.origins, bit)
+        self.step += 1
+        if self.step < len(self.bits):
+            self.parts = [block, other]
+            self.origins = self.origins + more
+        else:
+            self.arrays = [other, block, exchanged(block, "seq", 1)]
+            self.all_origins = [more, self.origins, self.moved(self.origins, 1)]
+
+    def cross(self, arrays):
+        self.arrays = arrays + [exchanged(arrays[0], "seq", 1)]
+        self.all_origins.append(self.moved(self.all_origins[0], 1))
+
+
+def move(spreads, crossing, before=(), after=()):
+    parts, arrays, after = lax.optimization_barrier(
+        ([entry.parts for entry in spreads], [entry.arrays for entry in crossing], after)
+    )
+    blocks = [jnp.concatenate(pair, axis=0) if len(pair) > 1 else pair[0] for pair in parts]
+    blocks, arrays, before = lax.optimization_barrier((blocks, arrays, before))
+    for entry, block in zip(spreads, blocks):
+        entry.advance(block)
+    for entry, own in zip(crossing, arrays):
+        entry.cross(own)
+    return tuple(before) + tuple(after)
+
+
+def in_progress(spreads):
+    return spreads[0].step < len(spreads[0].bits) - 1
+
+
+def received(spreads):
+    arrays = [
+        array.reshape(array.shape[0], -1, array.shape[-1])
+        for entry in spreads
+        for array in entry.arrays
+    ]
+    origins = [entries for entry in spreads for entries in entry.all_origins]
+    return arrays, origins
+
+
+def along_fsdp(block, fars=None):
+    fars = range(1, lax.axis_size("fsdp")) if fars is None else fars
+    return [block] + [exchanged(block, "fsdp", far) for far in fars]
+
+
+def spread_pair(columns):
+    orders = routes(lax.axis_size("seq"))
+    middle = len(columns) // 2
+    return [
+        Spread(columns[:middle], range(middle), orders[0]),
+        Spread(columns[middle:], range(middle, len(columns)), orders[1]),
+    ]
+
+
+def half_piece(shard):
     part, spacing = half_spacing(shard.shape[0])
     own = lax.axis_index("seq") & (PARTS - 1)
-    piece = lax.dynamic_slice_in_dim(shard, own * spacing, part, axis=0)
-    (piece,) = yield [piece]
-    columns = [piece]
-    for bit in range(1, lax.axis_size("fsdp")):
-        columns.append(exchanged(piece, "fsdp", bit))
-    columns = yield columns
-    others = [exchanged(entry, "seq", 2) for entry in columns]
-    columns, others = yield [columns, others]
-    pieces = []
-    for entry, other in zip(columns, others):
-        pieces += [entry, exchanged(entry, "seq", 1), other, exchanged(other, "seq", 1)]
-    return pieces
-
-
-def gather_full(shard):
-    seq_count, fsdp_count = lax.axis_size("seq"), lax.axis_size("fsdp")
-    part = round_up(shard.shape[0], 16 * seq_count) // seq_count
-    piece = lax.dynamic_slice_in_dim(
-        padded(shard, part * seq_count), lax.axis_index("seq") * part, part, axis=0
-    )
-    (piece,) = yield [piece]
-    columns = [piece]
-    for far in range(1, fsdp_count):
-        columns.append(exchanged(piece, "fsdp", far))
-    half_count = fsdp_count // 2
-    halves = [[jnp.stack(columns[:half_count])], [jnp.stack(columns[half_count:])]]
-    indices = [[0], [0]]
-    orders = routes(seq_count)
-    for step in range(len(orders[0]) + 1):
-        halves = yield halves
-        for half, order in enumerate(orders):
-            bit = (order + [1])[step]
-            halves[half] = halves[half] + [exchanged(entry, "seq", bit) for entry in halves[half]]
-            indices[half] = indices[half] + [index ^ bit for index in indices[half]]
-    pieces = []
-    for entries, places in zip(halves, indices):
-        pieces += [entry for _, entry in sorted(zip(places, entries), key=lambda pair: pair[0])]
-    return pieces
+    return lax.dynamic_slice_in_dim(shard, own * spacing, part, axis=0)
+
+
+def full_piece(shard):
+    seq_count = lax.axis_size("seq")
+    part = round_up(shard.shape[0], 8 * seq_count) // seq_count
+    return tiled(
+        lax.dynamic_slice_in_dim(
+            padded(shard, part * seq_count), lax.axis_index("seq") * part, part, axis=0
+        )
+    )
 
 
 def add_low(*blocks):
@@ -818,13 +856,13 @@
         columns += [[term[0, within] for term in entries] for within in range(fsdp_count // 2)]
     leaving = yield [add_low(*columns[far]) for far in range(1, fsdp_count)]
     arrived = [exchanged(block, "fsdp", far + 1) for far, block in enumerate(leaving)]
-    pieces = [add_low(*columns[0], *arrived)]
-    indices = [0]
-    for bit in orders[1] + [1]:
-        pieces = yield pieces
-        pieces = pieces + [exchanged(piece, "seq", bit) for piece in pieces]
+    block, indices = add_low(*columns[0], *arrived)[None], [0]
+    for bit in orders[1]:
+        (block,) = yield [block]
+        block = jnp.concatenate([block, exchanged(block, "seq", bit)], axis=0)
         indices = indices + [index ^ bit for index in indices]
-    return [piece for _, piece in sorted(zip(indices, pieces), key=lambda pair: pair[0])]
+    (block,) = yield [block]
+    return [block, exchanged(block, "seq", 1)], [indices, [index ^ 1 for index in indices]]
 
 
 def reduce_vectors(vectors):
@@ -879,8 +917,21 @@
     wide_local = jnp.concatenate(wide_local, axis=0)
     inner_local = jnp.concatenate([encgains, encshifts, decgains, decshifts], axis=0)
     vector_local = jnp.concatenate([wide_local.reshape(-1), inner_local.reshape(-1)])
+    enc_rows = jnp.concatenate([rows_of(enckernel)] + halves(encexpand) + [decproject], axis=0)
+    dec_rows = jnp.concatenate([rows_of(deckernel)] + halves(decexpand), axis=0)
+    _, spacing = half_spacing(encproject.shape[0])
+    counts = (seq_count, fsdp_count)
+    enc_own, dec_own = full_piece(enc_rows), full_piece(dec_rows)
+    vector_rows = round_up(vector_local.size, 8 * inner_width) // inner_width
+    vector_piece = jnp.pad(vector_local, (0, vector_rows * inner_width - vector_local.size))
+    vector_piece = vector_piece.reshape(vector_rows, inner_width)
+    entry_piece = jnp.concatenate([half_piece(encproject), vector_piece], axis=0)
+    entry_columns = along_fsdp(tiled(entry_piece))
+    entry_spread = Spread(entry_columns, range(fsdp_count), [2])
+    (enc_own,) = move([entry_spread], [], (enc_own,))
+    enc_spreads = spread_pair(along_fsdp(enc_own))
     vector_shards = jnp.stack(
-        [vector_local] + [exchanged(vector_local, "fsdp", far) for far in range(1, fsdp_count)]
+        [column[-vector_rows // 8 :].reshape(-1)[: vector_local.size] for column in entry_columns]
     )
     own = lax.axis_index("fsdp")
     vector_shards = jnp.stack(
@@ -899,15 +950,15 @@
     enc_wide, dec_wide = wides[:3], wides[3:]
     enc_inner, dec_inner = inners[:6], inners[6:]
 
-    enc_rows = jnp.concatenate([rows_of(enckernel)] + halves(encexpand), axis=0)
-    dec_rows = jnp.concatenate([decproject, rows_of(deckernel)] + halves(decexpand), axis=0)
-    entry = Chain(gather_half(encproject)).advance()
-    enc_gather = Chain(gather_full(enc_rows)).advance()
-    dec_gather = Chain(gather_full(dec_rows)).advance()
-    _, spacing = half_spacing(encproject.shape[0])
+    far_half = fsdp_count // 2 + 1
+    (dec_own,) = move(enc_spreads, [entry_spread], (dec_own,))
+    dec_columns = along_fsdp(dec_own, range(1, far_half))
+    project_pieces, entry_origins = received([entry_spread])
+    while in_progress(enc_spreads):
+        move(enc_spreads, [])
 
     def landing(pieces):
-        count = len(pieces) * pieces[0].shape[0]
+        count = sum(piece.shape[0] for piece in pieces)
         return ((count,) + pieces[0].shape[1:], BF16), count
 
     places = lax.axis_index("seq") * rows + jnp.arange(rows, dtype=jnp.int32)
@@ -929,41 +980,48 @@
     tap_unit = 2 * micro * rows * inner_width * inner_width
 
     def enter_body(*refs):
-        enter_encoder_kernel(PARTS, spacing, *refs)
-
-    project_pieces = entry.finish()
-    enc_gather.advance()
-    enc_wide = slot(enc_wide, enc_gather)
+        enter_encoder_kernel(entry_origins, spacing, *refs)
+
+    landed, copies = landing(project_pieces)
+    enc_wide, dec_columns = move(enc_spreads, [], (enc_wide, dec_columns))
+    dec_columns += along_fsdp(dec_columns[0], range(far_half, fsdp_count))[1:]
+    dec_spreads = spread_pair(dec_columns)
+    entered_shapes = [(wide_shape, BF16), (inner_shape, F32), (inner_shape, BF16)]
     first_e, hidden_e, second_e, enc_project = call(
         enter_body,
         micro,
         [stream],
         [enc_wide, enc_inner],
-        [(wide_shape, BF16), (inner_shape, F32), (inner_shape, BF16)],
+        entered_shapes,
         [((width, inner_width), BF16)],
-        [((len(project_pieces),) + project_pieces[0].shape, BF16)],
+        [landed],
         unit,
         project_pieces,
         place,
-        len(project_pieces),
-    )
-    low = to_next(second_e[:, rows - enc_reach :])
-    high = to_previous(second_e[:, :enc_reach])
+        copies,
+    )
+    tail, head = second_e[:, rows - enc_reach :], second_e[:, :enc_reach]
+    while dec_spreads[0].step < len(dec_spreads[0].bits) - 2:
+        move(dec_spreads, [])
+    tail, head = move(dec_spreads, enc_spreads, after=(tail, head))
+    low, high = to_next(tail), to_previous(head)
+    enc_pieces, enc_origins = received(enc_spreads)
 
     def middle_body(*refs):
-        middle_kernel(enc_offsets, fsdp_count, *refs)
-
-    enc_pieces = enc_gather.finish()
-    dec_gather.advance()
-    enc_inner = slot(enc_inner, dec_gather)
+        middle_kernel(enc_offsets, counts, enc_origins, *refs)
+
     landed, copies = landing(enc_pieces)
-    mixed_e, third_e, middle, enc_expand, enc_flat = call(
+    mixed_e, third_e, middle, enc_expand, enc_flat, dec_project = call(
         middle_body,
         micro,
         [second_e, low, high, enc_masks, stream],
         [enc_wide, enc_inner],
         [(inner_shape, F32), (inner_shape, BF16), (wide_shape, F32)],
-        [((inner_width, width), BF16), ((inner_width, ENC_TAPS * inner_width), BF16)],
+        [
+            ((inner_width, width), BF16),
+            ((inner_width, ENC_TAPS * inner_width), BF16),
+            ((width, inner_width), BF16),
+        ],
         [
             ((rows + 2 * enc_reach, inner_width), BF16),
             ((rows, ENC_TAPS * inner_width), BF16),
@@ -976,41 +1034,37 @@
         copies,
     )
 
-    def enter_decoder_body(*refs):
-        enter_decoder_kernel(DEC_TAPS, fsdp_count, *refs)
-
-    dec_pieces = dec_gather.finish()
-    landed, copies = landing(dec_pieces)
-    first_d, hidden_d, second_d, dec_project, dec_stacked, dec_flat, dec_expand = call(
+    def enter_decoder_body(stream_in, wide, inner, project, *refs):
+        enter_kernel(stream_in, project, wide, inner, *refs)
+
+    dec_inner, enc_expand = move(dec_spreads, [], (dec_inner,), (enc_expand,))
+    first_d, hidden_d, second_d = call(
         enter_decoder_body,
         micro,
         [middle],
-        [dec_wide, dec_inner],
+        [dec_wide, dec_inner, dec_project],
         [(wide_shape, BF16), (inner_shape, F32), (inner_shape, BF16)],
-        [
-            ((width, inner_width), BF16),
-            ((DEC_TAPS * inner_width, inner_width), BF16),
-            ((inner_width, DEC_TAPS * inner_width), BF16),
-            ((inner_width, width), BF16),
-        ],
-        [landed],
+        [],
+        [],
         unit,
-        dec_pieces,
-        place,
-        copies,
-    )
-    low = to_next(second_d[:, rows - dec_reach :])
+    )
+    (tail,) = move([], dec_spreads, after=(second_d[:, rows - dec_reach :],))
+    dec_pieces, dec_origins = received(dec_spreads)
+    low = to_next(tail)
 
     def turn_body(*refs):
-        turn_kernel(dec_offsets, *refs)
-
-    third_d, gmixed_d, gexpand_d, turn_wide, turn_inner = call(
+        turn_kernel(dec_offsets, counts, dec_origins, *refs)
+
+    landed, copies = landing(dec_pieces)
+    third_d, gmixed_d, gexpand_d, dec_flat, dec_expand, turn_wide, turn_inner = call(
         turn_body,
         micro,
         [second_d, low, dec_masks, cot],
-        [dec_stacked, dec_expand, dec_inner],
+        [dec_inner],
         [(inner_shape, BF16), (inner_shape, BF16)],
         [
+            ((inner_width, width), BF16),
+            ((inner_width, DEC_TAPS * inner_width), BF16),
             ((inner_width, width), BF16),
             ((1, 8, width), F32),
             ((3, 8, inner_width), F32),
@@ -1021,12 +1075,15 @@
             ((rows, inner_width), F32),
             ((rows, inner_width), F32),
             ((inner_width, width), F32),
+            ((DEC_TAPS * inner_width, inner_width), BF16),
+            landed,
         ],
         2 * unit + DEC_TAPS * tap_unit,
+        dec_pieces,
+        place,
+        copies,
     )
     high = to_previous(gmixed_d[:, :dec_reach])
-
-    counts = (seq_count, fsdp_count)
 
     def packed_pair(row_total):
         part = round_up(row_total, 8 * seq_count) // seq_count
@@ -1104,62 +1161,89 @@
         encoder_back_kernel(enc_back, enc_reach, enc_reach, counts, *refs)
 
     enc_reduce = Chain(reduce_pieces(keep_e, send_e))
-    enc_inner = slot(enc_inner, dec_reduce, enc_reduce)
-    ghidden_e, keep_p, send_p, conv_inner_e = call(
-        encoder_back_body,
+    def encoder_back_body(*refs):
+        encoder_back_kernel(enc_back, enc_reach, enc_reach, *refs)
+
+    chains = [dec_reduce, enc_reduce]
+    early = (micro + 1) // 2
+    spans = [(0, early)] + ([(early, micro - early)] if micro > early else [])
+    ghidden, conv_sums = (), []
+    for offset, count in spans:
+        enc_inner, ghidden, conv_sums = slot((enc_inner, ghidden, conv_sums), *chains)
+        *ghidden, conv_part = call(
+            encoder_back_body,
+            count,
+            [gmixed_e, low, high, enc_back_masks, hidden_e],
+            [enc_flat, enc_inner],
+            [(inner_shape, BF16)],
+            [((3, 8, inner_width), F32)],
+            extended_scratch + [((rows, inner_width), F32)],
+            ENC_TAPS * tap_unit * count // micro,
+            offset=offset,
+            carried=ghidden,
+        )
+        conv_sums.append(conv_part)
+    (ghidden_e,), conv_inner_e = ghidden, sum(conv_sums)
+
+    def project_grad_body(*refs):
+        project_grad_kernel(counts, *refs)
+
+    keep_p, send_p = call(
+        project_grad_body,
         micro,
-        [gmixed_e, low, high, enc_back_masks, hidden_e, first_e],
-        [enc_flat, enc_inner],
-        [(inner_shape, BF16)],
-        packed_pair(width // fsdp_count) + [((3, 8, inner_width), F32)],
-        extended_scratch + [((rows, inner_width), F32), ((width, inner_width), F32)],
-        unit + ENC_TAPS * tap_unit,
+        [first_e, ghidden_e],
+        [],
+        [],
+        packed_pair(width // fsdp_count),
+        [((width, inner_width), F32)],
+        unit,
         place=place,
     )
     entry_reduce = Chain(reduce_pieces(keep_p, send_p))
-    enc_wide = slot(enc_wide, dec_reduce, enc_reduce, entry_reduce)
-    gstream, leave_wide = call(
-        leave_kernel,
-        micro,
-        [ghidden_e, stream, gmiddle],
-        [enc_project, enc_wide],
-        [(wide_shape, BF16)],
-        [((2, 8, width), F32)],
-        [((rows, width), F32)],
-        unit,
-    )
-
-    sums = [leave_wide, link_wide, turn_wide, conv_inner_e, link_inner, conv_inner_d, turn_inner]
-    sums = [jnp.sum(entry, axis=1).reshape(-1, inner_width) for entry in sums]
-    vector_reduce = Chain(reduce_vectors(jnp.concatenate(sums, axis=0)))
-    dec_wide = slot(dec_wide, dec_reduce, enc_reduce, entry_reduce, vector_reduce)
-    (output,) = call(
-        output_kernel,
-        micro,
-        [third_d, middle],
-        [dec_expand, dec_wide],
-        [(wide_shape, BF16)],
-        [],
-        [((rows, width), F32)],
-        unit,
-    )
-
+    chains.append(entry_reduce)
+    gstream, leave_sums = (), []
+    for offset, count in spans:
+        enc_wide, gstream, leave_sums = slot((enc_wide, gstream, leave_sums), *chains)
+        *gstream, leave_wide = call(
+            leave_kernel,
+            count,
+            [ghidden_e, stream, gmiddle],
+            [enc_project, enc_wide],
+            [(wide_shape, BF16)],
+            [((2, 8, width), F32)],
+            [((rows, width), F32)],
+            unit * count // micro,
+            offset=offset,
+            carried=gstream,
+        )
+        leave_sums.append(leave_wide)
+
+    def row_sums(entry):
+        sums = jnp.sum(entry, axis=1)
+        return jnp.pad(sums, ((0, 0), (0, width - sums.shape[1])))
+
+    sums = [sum(leave_sums), link_wide, turn_wide]
+    sums += [conv_inner_e, link_inner, conv_inner_d, turn_inner]
+    vector_reduce = Chain(reduce_vectors(jnp.concatenate([row_sums(entry) for entry in sums])))
+    chains.append(vector_reduce)
+    output = ()
+    for offset, count in spans:
+        dec_wide, gstream, output = slot((dec_wide, gstream, output), *chains)
+        output = call(
+            output_kernel,
+            count,
+            [third_d, middle],
+            [dec_expand, dec_wide],
+            [(wide_shape, BF16)],
+            [],
+            [((rows, width), F32)],
+            unit * count // micro,
+            offset=offset,
+            carried=output,
+        )
     def own_columns(vectors):
         part = vectors.shape[1] // fsdp_count
         return lax.dynamic_slice_in_dim(vectors, own * part, part, axis=1)
-
-    sums = vector_reduce.finish() * factor
-    wide_sums = sums[:12].reshape(6, width)
-    order = [wide_sums[:2], wide_sums[4:5], wide_sums[2:4], wide_sums[5:]]
-    wide_own = own_columns(jnp.concatenate(order))
-    inner_own = own_columns(sums[12:])
-
-    def vectors(wide_rows, inner_rows):
-        widegain = wide_rows[0]
-        wideshift = wide_rows[1:3]
-        gains = jnp.stack([inner_rows[0], inner_rows[3]])
-        shifts = jnp.stack([inner_rows[1], inner_rows[4], inner_rows[2], inner_rows[5]])
-        return widegain, gains, wideshift, shifts
 
     project_rows = width // fsdp_count
     scale = total_rows**-0.5
@@ -1169,7 +1253,7 @@
     }
 
     def finish(chain, names):
-        pieces = chain.finish()
+        pieces, indices = chain.finish()
         layout, outs, start = [], [], 0
         for name in names:
             shape = shapes.get(name, (name, shard_part, inner_width))
@@ -1181,7 +1265,7 @@
             start += size // inner_width
 
         def body(*refs):
-            finish_kernel(layout, scale, *refs)
+            finish_kernel(layout, scale, indices, *refs)
 
         whole = pl.BlockSpec(memory_space=pltpu.VMEM)
         return pl.pallas_call(
@@ -1189,16 +1273,35 @@
             in_specs=[pl.BlockSpec(memory_space=pltpu.SMEM)] + [whole] * len(pieces),
             out_specs=[whole] * len(outs),
             out_shape=outs,
-            scratch_shapes=[pltpu.VMEM((len(pieces),) + pieces[0].shape, BF16)],
+            scratch_shapes=[pltpu.VMEM((seq_count,) + pieces[0].shape[1:], BF16)],
             compiler_params=pltpu.CompilerParams(vmem_limit_bytes=VMEM_LIMIT),
         )(place, *pieces)
 
-    gproject_d, gkernel_d, gexpand_d = finish(dec_reduce, ["project", DEC_TAPS, "expand"])
-    gkernel_e, gexpand_e = finish(enc_reduce, [ENC_TAPS, "expand"])
-    (gproject_e,) = finish(entry_reduce, ["project"])
+    names = [["project", DEC_TAPS, "expand"], [ENC_TAPS, "expand"], ["project"]]
+    finished = [None] * len(names)
+    while any(chain.pending is not None for chain in chains):
+        for index, entry in enumerate(names):
+            if finished[index] is None and chains[index].pending is None:
+                finished[index] = finish(chains[index], entry)
+        output, finished = slot((output, finished), *chains)
+    finished = [entry or finish(chain, kinds) for entry, chain, kinds in zip(finished, chains, names)]
+    sums = vector_reduce.finish() * factor
+    wide_sums = sums[:6]
+    order = [wide_sums[:2], wide_sums[4:5], wide_sums[2:4], wide_sums[5:]]
+    wide_own = own_columns(jnp.concatenate(order))
+    inner_own = own_columns(sums[6:, :inner_width])
+
+    def vectors(wide_rows, inner_rows):
+        widegain = wide_rows[0]
+        wideshift = wide_rows[1:3]
+        gains = jnp.stack([inner_rows[0], inner_rows[3]])
+        shifts = jnp.stack([inner_rows[1], inner_rows[4], inner_rows[2], inner_rows[5]])
+        return widegain, gains, wideshift, shifts
+
+    (gproject_d, gkernel_d, gexpand_d), (gkernel_e, gexpand_e), (gproject_e,) = finished
     return (
-        output[:, None],
-        gstream[:, None],
+        output[0][:, None],
+        gstream[0][:, None],
         gproject_e,
         gkernel_e,
         gexpand_e,

time: 683 us -> 624 us (0.914)
  waiting for transfers between devices: 138 us -> 101 us
  starting transfers between devices: 126 us -> 92.9 us
  Pallas kernels: 318 us -> 329 us
  local copies, waits for them, and re-layouts: 41.9 us -> 32.2 us
  other arithmetic: 48.3 us -> 57.4 us
    ppermute x102 -> x66, starting transfers between devices: 117 us -> 83.2 us  [exchanged(): lax.ppermute(block, axis, [(i, i ^ bit) for i in range(lax.axis_size(axis...]
    ppermute x102 -> x66, waiting for transfers between devices: 130 us -> 97.8 us  [exchanged(): lax.ppermute(block, axis, [(i, i ^ bit) for i in range(lax.axis_size(axis...]
    pallas_call x10 -> x14, Pallas kernels: 306 us -> 317 us  [call(): pl.pallas_call(kernel, grid=(steps,), in_specs=in_specs, out_specs=[stepp...]
    convert_element_type x9 -> x6, other arithmetic: 25.1 us -> 20.3 us  [add_low(): return total.astype(BF16)]
  transfers between devices with their start and end apart: 108 -> 72, of which waited for: 27 -> 25; matrix products, arithmetic and copies ran while one was open for 10% -> 10% of each run, Pallas kernels for 31% -> 38%
where the time goes in v2:
time: 624 us; the launch traced here: 615 us
  Pallas kernels  329 us (53%)
  waiting for transfers between devices  101 us (16%)
  starting transfers between devices  92.9 us (15%)
  other arithmetic  57.4 us (9%)
  local copies, waits for them, and re-layouts  32.2 us (5%)
    pallas_call x14, Pallas kernels, call(): pl.pallas_call(kernel, grid=(steps,), in_specs=in_specs, out_specs=[stepp...  317 us
    ppermute x66, waiting for transfers between devices, exchanged(): lax.ppermute(block, axis, [(i, i ^ bit) for i in range(lax.axis_size(axis...  97.8 us
    ppermute x66, starting transfers between devices, exchanged(): lax.ppermute(block, axis, [(i, i ^ bit) for i in range(lax.axis_size(axis...  83.2 us
    convert_element_type x6, other arithmetic, add_low(): return total.astype(BF16)  20.3 us
  transfers between devices with their start and end apart: 72, of which 25 were waited for; matrix products, arithmetic and copies ran while one was open for 10% of the time, Pallas kernels for 38%

profile of v2, /device:TPU:0, one launch (start us, length us, event | category | flops | bytes accessed | tf_op | source)
XLA Modules:
  0.0 615.1 jit_solution(10253314977239126324)
XLA Ops:
  4.8 3.0 collective-permute-start
  7.8 2.6 collective-permute-start.1
  10.7 2.1 fusion.59
  17.2 9.2 %collective-permute-done.1 = bf16[15,8,800]{2,1,0:T(8,128)(2,1)} collective-permute-done((bf16[15,8,800]{2,1,0:T(8,128)(2,1)}, bf16[15,8,800]{2,1,0:T(8,128)(2,1)}, u32[]{:S(2)}, u32[]{:S(2)}) %collective-permute-start.1) | collective-permute-done | bytes 192032 | tf_op jit(solution)/shard_map/ppermute | solution.py:699
  26.5 2.2 pad_maximum_fusion.6
  28.7 4.8 collective-permute-start.4
  39.0 21.9 %collective-permute-done.4 = bf16[29,8,800]{2,1,0:T(8,128)(2,1)S(1)} collective-permute-done((bf16[29,8,800]{2,1,0:T(8,128)(2,1)S(1)}, bf16[29,8,800]{2,1,0:T(8,128)(2,1)S(1)}, u32[]{:S(2)}, u32[]{:S(2)}) %collective-permute-start.4) | collective-permute-done | bytes 371232 | tf_op jit(solution)/shard_map/ppermute | solution.py:699
  61.3 1.6 collective-permute-start.10
  62.8 1.5 collective-permute-start.9
  64.5 8.3 %collective-permute-start.11 = (bf16[16,8,800]{2,1,0:T(8,128)(2,1)S(1)}, bf16[16,8,800]{2,1,0:T(8,128)(2,1)S(1)}, u32[]{:S(2)}, u32[]{:S(2)}) collective-permute-start(bf16[16,8,800]{2,1,0:T(8,128)(2,1)S(1)} %fusion.33), channel_id=1, source_target_pairs={{0,1},{1,0},{2,3},{3,2},{4,5},{5,4},{6,7},{7,6},{8,9},{9,8},{10,11... | collective-permute-start | bytes 614408 | tf_op jit(solution)/shard_map/ppermute | solution.py:699
  73.5 5.8 collective-permute-done.10
  80.6 3.3 pad_maximum_fusion
  89.5 19.4 %shard_map.288 = (bf16[4,480,1600]{2,1,0:T(8,128)(2,1)}, f32[4,480,800]{2,1,0:T(8,128)}, bf16[4,480,800]{2,1,0:T(8,128)(2,1)}, bf16[1600,800]{1,0:T(8,128)(2,1)}) custom-call(s32[3]{0:T(128)} %pad_add_fusion.2.refs_0_, bf16[4,480,1600]{2,1,0:T(8,128)(2,1)} %bitcast.182, bf16[4,120,800]{2,1,0:T(8,128)(2,1)} %bitcast.17.refs_2_, ...), custom_call_target="tpu_custom_call" | custom-call | flops 4915200000 | bytes 27174400 | tf_op jit(solution)/shard_map/pallas_call | solution.py:658
  110.0 11.6 %collective-permute-done.14 = bf16[4,29,8,800]{3,2,1,0:T(8,128)(2,1)} collective-permute-done((bf16[4,29,8,800]{3,2,1,0:T(8,128)(2,1)}, bf16[4,29,8,800]{3,2,1,0:T(8,128)(2,1)}, u32[]{:S(2)}, u32[]{:S(2)}) %collective-permute-start.14) | collective-permute-done | bytes 1484832 | tf_op jit(solution)/shard_map/ppermute | solution.py:699
  121.6 2.2 collective-permute-done.16
  124.4 1.9 collective-permute-start.18
  129.4 4.6 collective-permute-start.22
  135.2 39.4 %shard_map.289 = (f32[4,480,800]{2,1,0:T(8,128)}, bf16[4,480,800]{2,1,0:T(8,128)(2,1)}, f32[4,480,1600]{2,1,0:T(8,128)}, bf16[800,1600]{1,0:T(8,128)(2,1)}, bf16...) custom-call(s32[3]{0:T(128)} %pad_add_fusion.2.refs_0_, bf16[4,480,800]{2,1,0:T(8,128)(2,1)} %get-tuple-element.211.refs_1_.refs_5_, ...), custom_call_target="tpu_custom_call" | custom-call | flops 17203200000 | bytes 54380800 | tf_op jit(solution)/shard_map/pallas_call | solution.py:658
  177.7 18.2 %shard_map.290 = (bf16[4,480,1600]{2,1,0:T(8,128)(2,1)}, f32[4,480,800]{2,1,0:T(8,128)}, bf16[4,480,800]{2,1,0:T(8,128)(2,1)}) custom-call(f32[4,480,1600]{2,1,0:T(8,128)} %get-tuple-element.233.refs_0_.refs_1_, f32[3,1600]{1,0:T(4,128)} %slice.631.refs_1_.refs_6_.refs_3_, f32[6,800]{1,0:T(8,128)} %slice.633.refs_2_.refs_13_.refs_8_, ...), custom_call_target="tpu_custom_call" | custom-call | flops 4915200000 | bytes 30246400 | tf_op jit(solution)/shard_map/pallas_call | solution.py:658
  197.4 1.9 collective-permute-done.26
  199.9 1.9 collective-permute-start.28
  204.4 42.4 %shard_map.291 = (bf16[4,480,800]{2,1,0:T(8,128)(2,1)}, bf16[4,480,800]{2,1,0:T(8,128)(2,1)}, bf16[800,1600]{1,0:T(8,128)(2,1)}, bf16[800,2400]{1,0:T(8,128)(2,1...) custom-call(s32[3]{0:T(128)} %pad_add_fusion.2.refs_0_, ...), custom_call_target="tpu_custom_call" | custom-call | flops 17203200000 | bytes 31237120 | tf_op jit(solution)/shard_map/pallas_call | solution.py:658
  250.1 2.9 collective-permute-done.31.refs_2_
  253.6 42.2 %shard_map.292 = (bf16[4,480,800]{2,1,0:T(8,128)(2,1)}, bf16[16,176,800]{2,1,0:T(8,128)(2,1)}, bf16[16,176,800]{2,1,0:T(8,128)(2,1)}, f32[3,8,800]{2,1,0:T(8,128)}) custom-call(s32[3]{0:T(128)} %pad_add_fusion.2.refs_0_, bf16[4,480,800]{2,1,0:T(8,128)(2,1)} %get-tuple-element.261.refs_1_, bf16[4,32,800]{2,1,0:T(8,128)(2,1)} %copy-done.32, ...), custom_call_target="tpu_custom_call" | custom-call | flops 19660800000 | bytes 37227520 | tf_op jit(solution)/shard_map/pallas_call | solution.py:658
  295.8 5.3 collective-permute-start.34
  302.4 44.5 %shard_map.293 = (f32[4,480,1600]{2,1,0:T(8,128)}, bf16[4,480,800]{2,1,0:T(8,128)(2,1)}, bf16[800,1600]{1,0:T(8,128)(2,1)}, f32[3,8,1600]{2,1,0:T(8,128)}, f32[3,8,800]{2,1,0:T(8,128)}) custom-call(bf16[4,480,800]{2,1,0:T(8,128)(2,1)} %get-tuple-element.268.refs_0_, f32[4,480,1600]{2,1,0:T(8,128)} %get-tuple-element.233.refs_0_.refs_1_, ...), custom_call_target="tpu_custom_call" | custom-call | flops 14745600000 | bytes 54028800 | tf_op jit(solution)/shard_map/pallas_call | solution.py:658
  347.9 1.9 collective-permute-start.32
  351.2 4.5 add_convert_fusion.2
  355.7 3.9 collective-permute-start.35
  361.3 24.8 %shard_map.294 = (bf16[16,176,800]{2,1,0:T(8,128)(2,1)}, bf16[16,176,800]{2,1,0:T(8,128)(2,1)}) custom-call(s32[3]{0:T(128)} %pad_add_fusion.2.refs_0_, bf16[4,480,800]{2,1,0:T(8,128)(2,1)} %get-tuple-element.272.refs_1_.refs_0_, bf16[4,16,800]{2,1,0:T(8,128)(2,1)} %copy-done.33, bf16[4,16,800]{2,1,0:T(8,128)(2,1)} %copy-done.34, ...), custom_call_target="tpu_custom_call" | custom-call | flops 12288000000 | bytes 17939200 | tf_op jit(solution)/shard_map/pallas_call | solution.py:658
  386.2 2.1 collective-permute-done.35
  388.2 4.1 fusion.2
  398.5 15.2 %shard_map.295 = (bf16[4,480,800]{2,1,0:T(8,128)(2,1)}, f32[3,8,800]{2,1,0:T(8,128)}) custom-call(bf16[4,480,800]{2,1,0:T(8,128)(2,1)} %get-tuple-element.272.refs_1_.refs_0_, bf16[4,16,800]{2,1,0:T(8,128)(2,1)} %copy-done.33, bf16[4,16,800]{2,1,0:T(8,128)(2,1)} %copy-done.34, bf16[4,480,5]{2,1,0:T(8,128)(2,1)} %convert_element_type.476.refs_4_.refs_3_, ...), custom_call_target="tpu_custom_call" | custom-call | flops 6144000000 | bytes 19008000 | tf_op jit(solution)/shard_map/pallas_call | solution.py:658
  414.8 2.0 fusion.23
  416.8 2.2 fusion.25
  419.0 4.5 add_convert_fusion
  425.0 9.5 %collective-permute-start.40 = (bf16[176,800]{1,0:T(8,128)(2,1)}, bf16[176,800]{1,0:T(8,128)(2,1)S(1)}, u32[]{:S(2)}, u32[]{:S(2)}) collective-permute-start(bf16[176,800]{1,0:T(8,128)(2,1)} %fusion.23), channel_id=1, source_target_pairs={{0,1},{1,0},{2,3},{3,2},{4,5},{5,4},{6,7},{7,6},{8,9},{9,8},{10,11... | collective-permute-start | bytes 844808 | tf_op jit(solution)/shard_map/ppermute | solution.py:699
  434.5 2.4 collective-permute-start.42
  436.8 15.1 %shard_map.296 = (bf16[4,480,800]{2,1,0:T(8,128)(2,1)}, f32[3,8,800]{2,1,0:T(8,128)}) custom-call(bf16[4,480,800]{2,1,0:T(8,128)(2,1)} %get-tuple-element.272.refs_1_.refs_0_, bf16[4,16,800]{2,1,0:T(8,128)(2,1)} %copy-done.33, bf16[4,16,800]{2,1,0:T(8,128)(2,1)} %copy-done.34, ...), custom_call_target="tpu_custom_call", output_to_operand_aliasing={{0}: (7, {})} | custom-call | flops 6144000000 | bytes 19008000 | tf_op jit(solution)/shard_map/pallas_call | solution.py:658
  451.9 12.3 %shard_map.297 = (bf16[16,56,800]{2,1,0:T(8,128)(2,1)}, bf16[16,56,800]{2,1,0:T(8,128)(2,1)}) custom-call(s32[3]{0:T(128)} %pad_add_fusion.2.refs_0_, bf16[4,480,1600]{2,1,0:T(8,128)(2,1)} %get-tuple-element.299.refs_1_, bf16[4,480,800]{2,1,0:T(8,128)(2,1)} %get-tuple-element.291.refs_2_.refs_0_), custom_call_target="tpu_custom_call" | custom-call | flops 4915200000 | bytes 12083200 | tf_op jit(solution)/shard_map/pallas_call | solution.py:658
  465.6 3.5 fusion
  475.2 13.7 %shard_map.298 = (bf16[4,480,1600]{2,1,0:T(8,128)(2,1)}, f32[2,8,1600]{2,1,0:T(8,128)}) custom-call(bf16[4,480,800]{2,1,0:T(8,128)(2,1)} %get-tuple-element.291.refs_2_.refs_0_, bf16[4,480,1600]{2,1,0:T(8,128)(2,1)} %bitcast.184, f32[4,480,1600]{2,1,0:T(8,128)} %get-tuple-element.292.refs_2_, bf16[1600,800]{1,0:T(8,128)(2,1)} %get-tuple-element.293.refs_3_, ...), custom_call_target="tpu_custom_call" | custom-call | flops 2457600000 | bytes 30329600 | tf_op jit(solution)/shard_map/pallas_call | solution.py:658
  488.8 5.4 collective-permute-done.45
  495.3 1.9 fusion.26
  497.3 2.5 fusion.28
  499.8 2.2 add_convert_fusion.4
  506.6 2.4 collective-permute-start.52
  510.0 13.7 %shard_map.299 = (bf16[4,480,1600]{2,1,0:T(8,128)(2,1)}, f32[2,8,1600]{2,1,0:T(8,128)}) custom-call(bf16[4,480,800]{2,1,0:T(8,128)(2,1)} %get-tuple-element.291.refs_2_.refs_0_, bf16[4,480,1600]{2,1,0:T(8,128)(2,1)} %bitcast.185, f32[4,480,1600]{2,1,0:T(8,128)} %get-tuple-element.292.refs_2_, ...), custom_call_target="tpu_custom_call", output_to_operand_aliasing={{0}: (5, {})} | custom-call | flops 2457600000 | bytes 30329600 | tf_op jit(solution)/shard_map/pallas_call | solution.py:658
  525.7 5.1 collective-permute-done.51
  530.8 1.6 fusion.30
  534.0 4.3 collective-permute-done.49
  542.3 8.1 %shard_map.300.refs_4_ = bf16[4,480,1600]{2,1,0:T(8,128)(2,1)} custom-call(bf16[4,480,800]{2,1,0:T(8,128)(2,1)} %get-tuple-element.259.refs_0_, f32[4,480,1600]{2,1,0:T(8,128)} %get-tuple-element.233.refs_0_.refs_1_, bf16[800,1600]{1,0:T(8,128)(2,1)} %get-tuple-element.260.refs_2_, f32[3,1600]{1,0:T(4,128)} %slice.631.refs_1_.refs_6_.refs_3_), custom_call_target="tpu_custom_call" | custom-call | flops 2457600000 | bytes 24083200 | tf_op jit(solution)/shard_map/pallas_call | solution.py:658
  551.5 1.8 fusion.41
  554.2 1.5 collective-permute-start.60
  557.7 2.4 collective-permute-start.63
  560.1 8.4 %shard_map.301 = bf16[4,480,1600]{2,1,0:T(8,128)(2,1)} custom-call(bf16[4,480,800]{2,1,0:T(8,128)(2,1)} %get-tuple-element.259.refs_0_, f32[4,480,1600]{2,1,0:T(8,128)} %get-tuple-element.233.refs_0_.refs_1_, bf16[800,1600]{1,0:T(8,128)(2,1)} %get-tuple-element.260.refs_2_, ...), custom_call_target="tpu_custom_call", output_to_operand_aliasing={{}: (4, {})} | custom-call | flops 2457600000 | bytes 24083200 | tf_op jit(solution)/shard_map/pallas_call | solution.py:658
  570.3 3.5 collective-permute-done.64
  575.1 5.0 shard_map.302
  581.6 3.8 collective-permute-done.66
  585.4 1.7 collective-permute-done.67
  588.2 4.7 shard_map.303
  593.6 5.3 collective-permute-done.69
  599.4 8.1 %collective-permute-done.71 = f32[18,1600]{1,0:T(8,128)S(1)} collective-permute-done((f32[18,1600]{1,0:T(8,128)S(1)}, f32[18,1600]{1,0:T(8,128)S(1)}, u32[]{:S(2)}, u32[]{:S(2)}) %collective-permute-start.71) | collective-permute-done | bytes 115232 | tf_op jit(solution)/shard_map/ppermute | solution.py:699
  612.2 2.4 shard_map.304
  (306 shorter events, 90.8 us)
Async XLA Ops:
  4.8 12.5 %collective-permute-start = (bf16[15,8,800]{2,1,0:T(8,128)(2,1)}, bf16[15,8,800]{2,1,0:T(8,128)(2,1)}, u32[]{:S(2)}, u32[]{:S(2)}) collective-permute-start(bf16[15,8,800]{2,1,0:T(8,128)(2,1)} %get-tuple-element.584), channel_id=1, source_target_pairs={{0,1},{1,0},{2,3},{3,2},{4,5},{5,4},{6,7},{7,6},{8,9},{9,8},{10,11... | collective-permute-start | bytes 576008 | tf_op jit(solution)/shard_map/ppermute | solution.py:699
  7.8 18.7 %collective-permute-start.1 = (bf16[15,8,800]{2,1,0:T(8,128)(2,1)}, bf16[15,8,800]{2,1,0:T(8,128)(2,1)}, u32[]{:S(2)}, u32[]{:S(2)}) collective-permute-start(bf16[15,8,800]{2,1,0:T(8,128)(2,1)} %get-tuple-element.584), channel_id=1, source_target_pairs={{0,2},{1,3},{2,0},{3,1},{4,6},{5,7},{6,4},{7,5},{8,10},{9,11},{10,... | collective-permute-start | bytes 576008 | tf_op jit(solution)/shard_map/ppermute | solution.py:699
  10.4 16.1 %collective-permute-start.2 = (bf16[15,8,800]{2,1,0:T(8,128)(2,1)}, bf16[15,8,800]{2,1,0:T(8,128)(2,1)}, u32[]{:S(2)}, u32[]{:S(2)}) collective-permute-start(bf16[15,8,800]{2,1,0:T(8,128)(2,1)} %get-tuple-element.584), channel_id=1, source_target_pairs={{0,3},{1,2},{2,1},{3,0},{4,7},{5,6},{6,5},{7,4},{8,11},{9,10},{10,... | collective-permute-start | bytes 576008 | tf_op jit(solution)/shard_map/ppermute | solution.py:699
  28.7 32.3 %collective-permute-start.4 = (bf16[29,8,800]{2,1,0:T(8,128)(2,1)S(1)}, bf16[29,8,800]{2,1,0:T(8,128)(2,1)S(1)}, u32[]{:S(2)}, u32[]{:S(2)}) collective-permute-start(bf16[29,8,800]{2,1,0:T(8,128)(2,1)S(1)} %fusion.20), channel_id=1, source_target_pairs={{0,2},{1,3},{2,0},{3,1},{4,6},{5,7},{6,4},{7,5},{8,10},{9,11},{10,... | collective-permute-start | bytes 1113608 | tf_op jit(solution)/shard_map/ppermute | solution.py:699
  33.4 27.6 %collective-permute-start.5 = (bf16[29,8,800]{2,1,0:T(8,128)(2,1)S(1)}, bf16[29,8,800]{2,1,0:T(8,128)(2,1)S(1)}, u32[]{:S(2)}, u32[]{:S(2)}) collective-permute-start(bf16[29,8,800]{2,1,0:T(8,128)(2,1)S(1)} %fusion.20), channel_id=1, source_target_pairs={{0,3},{1,2},{2,1},{3,0},{4,7},{5,6},{6,5},{7,4},{8,11},{9,10},{10,... | collective-permute-start | bytes 1113608 | tf_op jit(solution)/shard_map/ppermute | solution.py:699
  34.8 26.3 %collective-permute-start.3 = (bf16[29,8,800]{2,1,0:T(8,128)(2,1)S(1)}, bf16[29,8,800]{2,1,0:T(8,128)(2,1)S(1)}, u32[]{:S(2)}, u32[]{:S(2)}) collective-permute-start(bf16[29,8,800]{2,1,0:T(8,128)(2,1)S(1)} %fusion.20), channel_id=1, source_target_pairs={{0,1},{1,0},{2,3},{3,2},{4,5},{5,4},{6,7},{7,6},{8,9},{9,8},{10,11... | collective-permute-start | bytes 1113608 | tf_op jit(solution)/shard_map/ppermute | solution.py:699
  34.8 26.5 %collective-permute-start.6 = (bf16[4,15,8,800]{3,2,1,0:T(8,128)(2,1)}, bf16[4,15,8,800]{3,2,1,0:T(8,128)(2,1)}, u32[]{:S(2)}, u32[]{:S(2)}) collective-permute-start(bf16[4,15,8,800]{3,2,1,0:T(8,128)(2,1)} %pad_maximum_fusion.6), channel_id=1, source_target_pairs={{0,8},{4,12},{8,0},{12,4},{16,24},{20,28},{24,16},{28,20},{1,9},{5... | collective-permute-start | bytes 2304008 | tf_op jit(solution)/shard_map/ppermute | solution.py:699
  36.3 25.0 %collective-permute-start.7 = (bf16[4,15,8,800]{3,2,1,0:T(8,128)(2,1)}, bf16[4,15,8,800]{3,2,1,0:T(8,128)(2,1)}, u32[]{:S(2)}, u32[]{:S(2)}) collective-permute-start(bf16[4,15,8,800]{3,2,1,0:T(8,128)(2,1)} %pad_maximum_fusion.6), channel_id=1, source_target_pairs={{0,4},{4,0},{8,12},{12,8},{16,20},{20,16},{24,28},{28,24},{1,5},{5... | collective-permute-start | bytes 2304008 | tf_op jit(solution)/shard_map/ppermute | solution.py:699
  61.3 18.1 %collective-permute-start.10 = (bf16[2,29,8,800]{3,2,1,0:T(8,128)(2,1)S(1)}, bf16[2,29,8,800]{3,2,1,0:T(8,128)(2,1)S(1)}, u32[]{:S(2)}, u32[]{:S(2)}) collective-permute-start(bf16[2,29,8,800]{3,2,1,0:T(8,128)(2,1)S(1)} %pad_maximum_fusion.8), channel_id=1, source_target_pairs={{0,8},{4,12},{8,0},{12,4},{16,24},{20,28},{24,16},{28,20},{1,9},{5... | collective-permute-start | bytes 2227208 | tf_op jit(solution)/shard_map/ppermute | solution.py:699
  62.8 17.8 %collective-permute-start.9 = (bf16[2,29,8,800]{3,2,1,0:T(8,128)(2,1)S(1)}, bf16[2,29,8,800]{3,2,1,0:T(8,128)(2,1)}, u32[]{:S(2)}, u32[]{:S(2)}) collective-permute-start(bf16[2,29,8,800]{3,2,1,0:T(8,128)(2,1)S(1)} %pad_maximum_fusion.7), channel_id=1, source_target_pairs={{0,16},{4,20},{8,24},{12,28},{16,0},{20,4},{24,8},{28,12},{1,17},{... | collective-permute-start | bytes 2227208 | tf_op jit(solution)/shard_map/ppermute | solution.py:699
  64.5 19.4 %collective-permute-start.11 = (bf16[16,8,800]{2,1,0:T(8,128)(2,1)S(1)}, bf16[16,8,800]{2,1,0:T(8,128)(2,1)S(1)}, u32[]{:S(2)}, u32[]{:S(2)}) collective-permute-start(bf16[16,8,800]{2,1,0:T(8,128)(2,1)S(1)} %fusion.33), channel_id=1, source_target_pairs={{0,1},{1,0},{2,3},{3,2},{4,5},{5,4},{6,7},{7,6},{8,9},{9,8},{10,11... | collective-permute-start | bytes 614408 | tf_op jit(solution)/shard_map/ppermute | solution.py:699
  72.8 11.4 %collective-permute-start.12 = (bf16[16,8,800]{2,1,0:T(8,128)(2,1)S(1)}, bf16[16,8,800]{2,1,0:T(8,128)(2,1)S(1)}, u32[]{:S(2)}, u32[]{:S(2)}) collective-permute-start(bf16[16,8,800]{2,1,0:T(8,128)(2,1)S(1)} %fusion.33), channel_id=1, source_target_pairs={{0,2},{1,3},{2,0},{3,1},{4,6},{5,7},{6,4},{7,5},{8,10},{9,11},{10,... | collective-permute-start | bytes 614408 | tf_op jit(solution)/shard_map/ppermute | solution.py:699
  73.5 15.3 %collective-permute-start.8 = (bf16[4,15,8,800]{3,2,1,0:T(8,128)(2,1)}, bf16[4,15,8,800]{3,2,1,0:T(8,128)(2,1)}, u32[]{:S(2)}, u32[]{:S(2)}) collective-permute-start(bf16[4,15,8,800]{3,2,1,0:T(8,128)(2,1)} %collective-permute-done.6), channel_id=1, source_target_pairs={{0,4},{4,0},{8,12},{12,8},{16,20},{20,16},{24,28},{28,24},{1,5},{5... | collective-permute-start | bytes 2304008 | tf_op jit(solution)/shard_map/ppermute | solution.py:699
  84.2 37.4 %collective-permute-start.14 = (bf16[4,29,8,800]{3,2,1,0:T(8,128)(2,1)}, bf16[4,29,8,800]{3,2,1,0:T(8,128)(2,1)}, u32[]{:S(2)}, u32[]{:S(2)}) collective-permute-start(bf16[4,29,8,800]{3,2,1,0:T(8,128)(2,1)} %get-tuple-element.228), channel_id=1, source_target_pairs={{0,8},{4,12},{8,0},{12,4},{16,24},{20,28},{24,16},{28,20},{1,9},{5... | collective-permute-start | bytes 4454408 | tf_op jit(solution)/shard_map/ppermute | solution.py:699
  84.7 36.9 %collective-permute-start.15 = (bf16[4,29,8,800]{3,2,1,0:T(8,128)(2,1)}, bf16[4,29,8,800]{3,2,1,0:T(8,128)(2,1)}, u32[]{:S(2)}, u32[]{:S(2)}) collective-permute-start(bf16[4,29,8,800]{3,2,1,0:T(8,128)(2,1)} %get-tuple-element.228), channel_id=1, source_target_pairs={{0,4},{4,0},{8,12},{12,8},{16,20},{20,16},{24,28},{28,24},{1,5},{5... | collective-permute-start | bytes 4454408 | tf_op jit(solution)/shard_map/ppermute | solution.py:699
  84.7 39.1 %collective-permute-start.16 = (bf16[4,29,8,800]{3,2,1,0:T(8,128)(2,1)}, bf16[4,29,8,800]{3,2,1,0:T(8,128)(2,1)}, u32[]{:S(2)}, u32[]{:S(2)}) collective-permute-start(bf16[4,29,8,800]{3,2,1,0:T(8,128)(2,1)} %get-tuple-element.231), channel_id=1, source_target_pairs={{0,16},{4,20},{8,24},{12,28},{16,0},{20,4},{24,8},{28,12},{1,17},{... | collective-permute-start | bytes 4454408 | tf_op jit(solution)/shard_map/ppermute | solution.py:699
  86.1 37.7 %collective-permute-start.17 = (bf16[4,29,8,800]{3,2,1,0:T(8,128)(2,1)}, bf16[4,29,8,800]{3,2,1,0:T(8,128)(2,1)}, u32[]{:S(2)}, u32[]{:S(2)}) collective-permute-start(bf16[4,29,8,800]{3,2,1,0:T(8,128)(2,1)} %get-tuple-element.231), channel_id=1, source_target_pairs={{0,4},{4,0},{8,12},{12,8},{16,20},{20,16},{24,28},{28,24},{1,5},{5... | collective-permute-start | bytes 4454408 | tf_op jit(solution)/shard_map/ppermute | solution.py:699
  88.8 21.1 %collective-permute-start.13 = (bf16[16,8,800]{2,1,0:T(8,128)(2,1)S(1)}, bf16[16,8,800]{2,1,0:T(8,128)(2,1)S(1)}, u32[]{:S(2)}, u32[]{:S(2)}) collective-permute-start(bf16[16,8,800]{2,1,0:T(8,128)(2,1)S(1)} %fusion.33), channel_id=1, source_target_pairs={{0,3},{1,2},{2,1},{3,0},{4,7},{5,6},{6,5},{7,4},{8,11},{9,10},{10,... | collective-permute-start | bytes 614408 | tf_op jit(solution)/shard_map/ppermute | solution.py:699
  123.8 10.8 %collective-permute-start.20 = (bf16[4,29,8,800]{3,2,1,0:T(8,128)(2,1)}, bf16[4,29,8,800]{3,2,1,0:T(8,128)(2,1)}, u32[]{:S(2)}, u32[]{:S(2)}) collective-permute-start(bf16[4,29,8,800]{3,2,1,0:T(8,128)(2,1)} %collective-permute-done.14), channel_id=1, source_target_pairs={{0,4},{4,0},{8,12},{12,8},{16,20},{20,16},{24,28},{28,24},{1,5},{5... | collective-permute-start | bytes 4454408 | tf_op jit(solution)/shard_map/ppermute | solution.py:699
  123.8 10.8 %collective-permute-start.21 = (bf16[4,29,8,800]{3,2,1,0:T(8,128)(2,1)}, bf16[4,29,8,800]{3,2,1,0:T(8,128)(2,1)}, u32[]{:S(2)}, u32[]{:S(2)}) collective-permute-start(bf16[4,29,8,800]{3,2,1,0:T(8,128)(2,1)} %collective-permute-done.16), channel_id=1, source_target_pairs={{0,4},{4,0},{8,12},{12,8},{16,20},{20,16},{24,28},{28,24},{1,5},{5... | collective-permute-start | bytes 4454408 | tf_op jit(solution)/shard_map/ppermute | solution.py:699
  124.4 9.6 %collective-permute-start.18 = (bf16[4,16,800]{2,1,0:T(8,128)(2,1)S(1)}, bf16[4,16,800]{2,1,0:T(8,128)(2,1)S(1)}, u32[]{:S(2)}, u32[]{:S(2)}) collective-permute-start(bf16[4,16,800]{2,1,0:T(8,128)(2,1)S(1)} %get-tuple-element.217), channel_id=1, source_target_pairs={{0,4},{4,8},{8,12},{12,16},{16,20},{20,24},{24,28},{1,5},{5,9},{9,... | collective-permute-start | bytes 307208 | tf_op jit(solution)/shard_map/ppermute | solution.py:690
  126.3 8.3 %collective-permute-start.19 = (bf16[4,16,800]{2,1,0:T(8,128)(2,1)S(1)}, bf16[4,16,800]{2,1,0:T(8,128)(2,1)S(1)}, u32[]{:S(2)}, u32[]{:S(2)}) collective-permute-start(bf16[4,16,800]{2,1,0:T(8,128)(2,1)S(1)} %get-tuple-element.218), channel_id=1, source_target_pairs={{4,0},{8,4},{12,8},{16,12},{20,16},{24,20},{28,24},{5,1},{9,5},{13... | collective-permute-start | bytes 307208 | tf_op jit(solution)/shard_map/ppermute | solution.py:695
  129.4 45.3 %collective-permute-start.22 = (bf16[2,16,8,800]{3,2,1,0:T(8,128)(2,1)S(1)}, bf16[2,16,8,800]{3,2,1,0:T(8,128)(2,1)S(1)}, u32[]{:S(2)}, u32[]{:S(2)}) collective-permute-start(bf16[2,16,8,800]{3,2,1,0:T(8,128)(2,1)S(1)} %pad_maximum_fusion.11), channel_id=1, source_target_pairs={{0,16},{4,20},{8,24},{12,28},{16,0},{20,4},{24,8},{28,12},{1,17},{... | collective-permute-start | bytes 1228808 | tf_op jit(solution)/shard_map/ppermute | solution.py:699
  134.0 40.7 %collective-permute-start.23 = (bf16[2,16,8,800]{3,2,1,0:T(8,128)(2,1)S(1)}, bf16[2,16,8,800]{3,2,1,0:T(8,128)(2,1)S(1)}, u32[]{:S(2)}, u32[]{:S(2)}) collective-permute-start(bf16[2,16,8,800]{3,2,1,0:T(8,128)(2,1)S(1)} %pad_maximum_fusion.12), channel_id=1, source_target_pairs={{0,8},{4,12},{8,0},{12,4},{16,24},{20,28},{24,16},{28,20},{1,9},{5... | collective-permute-start | bytes 1228808 | tf_op jit(solution)/shard_map/ppermute | solution.py:699
  175.0 22.4 %collective-permute-start.24 = (bf16[4,16,8,800]{3,2,1,0:T(8,128)(2,1)S(1)}, bf16[4,16,8,800]{3,2,1,0:T(8,128)(2,1)}, u32[]{:S(2)}, u32[]{:S(2)}) collective-permute-start(bf16[4,16,8,800]{3,2,1,0:T(8,128)(2,1)S(1)} %pad_maximum_fusion.4), channel_id=1, source_target_pairs={{0,8},{4,12},{8,0},{12,4},{16,24},{20,28},{24,16},{28,20},{1,9},{5... | collective-permute-start | bytes 2457608 | tf_op jit(solution)/shard_map/ppermute | solution.py:699
  176.5 21.0 %collective-permute-start.25 = (bf16[4,16,8,800]{3,2,1,0:T(8,128)(2,1)S(1)}, bf16[4,16,8,800]{3,2,1,0:T(8,128)(2,1)}, u32[]{:S(2)}, u32[]{:S(2)}) collective-permute-start(bf16[4,16,8,800]{3,2,1,0:T(8,128)(2,1)S(1)} %pad_maximum_fusion.4), channel_id=1, source_target_pairs={{0,4},{4,0},{8,12},{12,8},{16,20},{20,16},{24,28},{28,24},{1,5},{5... | collective-permute-start | bytes 2457608 | tf_op jit(solution)/shard_map/ppermute | solution.py:699
  176.5 22.8 %collective-permute-start.26 = (bf16[4,16,8,800]{3,2,1,0:T(8,128)(2,1)S(1)}, bf16[4,16,8,800]{3,2,1,0:T(8,128)(2,1)}, u32[]{:S(2)}, u32[]{:S(2)}) collective-permute-start(bf16[4,16,8,800]{3,2,1,0:T(8,128)(2,1)S(1)} %pad_maximum_fusion.5), channel_id=1, source_target_pairs={{0,16},{4,20},{8,24},{12,28},{16,0},{20,4},{24,8},{28,12},{1,17},{... | collective-permute-start | bytes 2457608 | tf_op jit(solution)/shard_map/ppermute | solution.py:699
  176.5 22.8 %collective-permute-start.27 = (bf16[4,16,8,800]{3,2,1,0:T(8,128)(2,1)S(1)}, bf16[4,16,8,800]{3,2,1,0:T(8,128)(2,1)}, u32[]{:S(2)}, u32[]{:S(2)}) collective-permute-start(bf16[4,16,8,800]{3,2,1,0:T(8,128)(2,1)S(1)} %pad_maximum_fusion.5), channel_id=1, source_target_pairs={{0,4},{4,0},{8,12},{12,8},{16,20},{20,16},{24,28},{28,24},{1,5},{5... | collective-permute-start | bytes 2457608 | tf_op jit(solution)/shard_map/ppermute | solution.py:699
  295.8 55.3 %collective-permute-start.34 = (bf16[16,176,800]{2,1,0:T(8,128)(2,1)}, bf16[16,176,800]{2,1,0:T(8,128)(2,1)}, u32[]{:S(2)}, u32[]{:S(2)}) collective-permute-start(bf16[16,176,800]{2,1,0:T(8,128)(2,1)} %get-tuple-element.276), channel_id=1, source_target_pairs={{0,4},{4,0},{8,12},{12,8},{16,20},{20,16},{24,28},{28,24},{1,5},{5... | collective-permute-start | bytes 13516808 | tf_op jit(solution)/shard_map/ppermute | solution.py:699
  347.9 12.1 %collective-permute-start.32 = (bf16[4,16,800]{2,1,0:T(8,128)(2,1)S(1)}, bf16[4,16,800]{2,1,0:T(8,128)(2,1)S(1)}, u32[]{:S(2)}, u32[]{:S(2)}) collective-permute-start(bf16[4,16,800]{2,1,0:T(8,128)(2,1)S(1)} %get-tuple-element.562), channel_id=1, source_target_pairs={{0,4},{4,8},{8,12},{12,16},{16,20},{20,24},{24,28},{1,5},{5,9},{9,... | collective-permute-start | bytes 307208 | tf_op jit(solution)/shard_map/ppermute | solution.py:690
  349.9 10.2 %collective-permute-start.33 = (bf16[4,16,800]{2,1,0:T(8,128)(2,1)S(1)}, bf16[4,16,800]{2,1,0:T(8,128)(2,1)S(1)}, u32[]{:S(2)}, u32[]{:S(2)}) collective-permute-start(bf16[4,16,800]{2,1,0:T(8,128)(2,1)S(1)} %get-tuple-element.561), channel_id=1, source_target_pairs={{4,0},{8,4},{12,8},{16,12},{20,16},{24,20},{28,24},{5,1},{9,5},{13... | collective-permute-start | bytes 307208 | tf_op jit(solution)/shard_map/ppermute | solution.py:695
  355.7 32.6 %collective-permute-start.35 = (bf16[2,2,176,800]{3,2,1,0:T(8,128)(2,1)}, bf16[2,2,176,800]{3,2,1,0:T(8,128)(2,1)S(1)}, u32[]{:S(2)}, u32[]{:S(2)}) collective-permute-start(bf16[2,2,176,800]{3,2,1,0:T(8,128)(2,1)} %bitcast.52), channel_id=1, source_target_pairs={{0,16},{4,20},{8,24},{12,28},{16,0},{20,4},{24,8},{28,12},{1,17},{... | collective-permute-start | bytes 3379208 | tf_op jit(solution)/shard_map/ppermute | solution.py:699
  359.6 28.7 %collective-permute-start.36 = (bf16[2,2,176,800]{3,2,1,0:T(8,128)(2,1)}, bf16[2,2,176,800]{3,2,1,0:T(8,128)(2,1)S(1)}, u32[]{:S(2)}, u32[]{:S(2)}) collective-permute-start(bf16[2,2,176,800]{3,2,1,0:T(8,128)(2,1)} %bitcast.53), channel_id=1, source_target_pairs={{0,8},{4,12},{8,0},{12,4},{16,24},{20,28},{24,16},{28,20},{1,9},{5... | collective-permute-start | bytes 3379208 | tf_op jit(solution)/shard_map/ppermute | solution.py:699
  392.3 26.7 %collective-permute-start.39 = (bf16[16,176,800]{2,1,0:T(8,128)(2,1)}, bf16[16,176,800]{2,1,0:T(8,128)(2,1)}, u32[]{:S(2)}, u32[]{:S(2)}) collective-permute-start(bf16[16,176,800]{2,1,0:T(8,128)(2,1)} %get-tuple-element.288), channel_id=1, source_target_pairs={{0,4},{4,0},{8,12},{12,8},{16,20},{20,16},{24,28},{28,24},{1,5},{5... | collective-permute-start | bytes 13516808 | tf_op jit(solution)/shard_map/ppermute | solution.py:699
  396.8 20.0 %collective-permute-start.38 = (bf16[1,2,176,800]{3,2,1,0:T(8,128)(2,1)}, bf16[1,2,176,800]{3,2,1,0:T(8,128)(2,1)}, u32[]{:S(2)}, u32[]{:S(2)}) collective-permute-start(bf16[1,2,176,800]{3,2,1,0:T(8,128)(2,1)} %get-tuple-element.286), channel_id=1, source_target_pairs={{0,16},{4,20},{8,24},{12,28},{16,0},{20,4},{24,8},{28,12},{1,17},{... | collective-permute-start | bytes 1689608 | tf_op jit(solution)/shard_map/ppermute | solution.py:699
  398.1 16.6 %collective-permute-start.37 = (bf16[1,2,176,800]{3,2,1,0:T(8,128)(2,1)}, bf16[1,2,176,800]{3,2,1,0:T(8,128)(2,1)}, u32[]{:S(2)}, u32[]{:S(2)}) collective-permute-start(bf16[1,2,176,800]{3,2,1,0:T(8,128)(2,1)} %get-tuple-element.285), channel_id=1, source_target_pairs={{0,8},{4,12},{8,0},{12,4},{16,24},{20,28},{24,16},{28,20},{1,9},{5... | collective-permute-start | bytes 1689608 | tf_op jit(solution)/shard_map/ppermute | solution.py:699
  423.5 42.1 %collective-permute-start.43 = (bf16[2,2,176,800]{3,2,1,0:T(8,128)(2,1)}, bf16[2,2,176,800]{3,2,1,0:T(8,128)(2,1)}, u32[]{:S(2)}, u32[]{:S(2)}) collective-permute-start(bf16[2,2,176,800]{3,2,1,0:T(8,128)(2,1)} %bitcast.62), channel_id=1, source_target_pairs={{0,16},{4,20},{8,24},{12,28},{16,0},{20,4},{24,8},{28,12},{1,17},{... | collective-permute-start | bytes 3379208 | tf_op jit(solution)/shard_map/ppermute | solution.py:699
  424.2 41.4 %collective-permute-start.44 = (bf16[2,2,176,800]{3,2,1,0:T(8,128)(2,1)}, bf16[2,2,176,800]{3,2,1,0:T(8,128)(2,1)}, u32[]{:S(2)}, u32[]{:S(2)}) collective-permute-start(bf16[2,2,176,800]{3,2,1,0:T(8,128)(2,1)} %bitcast.63), channel_id=1, source_target_pairs={{0,8},{4,12},{8,0},{12,4},{16,24},{20,28},{24,16},{28,20},{1,9},{5... | collective-permute-start | bytes 3379208 | tf_op jit(solution)/shard_map/ppermute | solution.py:699
  425.0 39.2 %collective-permute-start.40 = (bf16[176,800]{1,0:T(8,128)(2,1)}, bf16[176,800]{1,0:T(8,128)(2,1)S(1)}, u32[]{:S(2)}, u32[]{:S(2)}) collective-permute-start(bf16[176,800]{1,0:T(8,128)(2,1)} %fusion.23), channel_id=1, source_target_pairs={{0,1},{1,0},{2,3},{3,2},{4,5},{5,4},{6,7},{7,6},{8,9},{9,8},{10,11... | collective-permute-start | bytes 844808 | tf_op jit(solution)/shard_map/ppermute | solution.py:699
  434.5 29.7 %collective-permute-start.41 = (bf16[176,800]{1,0:T(8,128)(2,1)}, bf16[176,800]{1,0:T(8,128)(2,1)S(1)}, u32[]{:S(2)}, u32[]{:S(2)}) collective-permute-start(bf16[176,800]{1,0:T(8,128)(2,1)} %get-tuple-element.295), channel_id=1, source_target_pairs={{0,2},{1,3},{2,0},{3,1},{4,6},{5,7},{6,4},{7,5},{8,10},{9,11},{10,... | collective-permute-start | bytes 844808 | tf_op jit(solution)/shard_map/ppermute | solution.py:699
  434.5 29.7 %collective-permute-start.42 = (bf16[176,800]{1,0:T(8,128)(2,1)}, bf16[176,800]{1,0:T(8,128)(2,1)S(1)}, u32[]{:S(2)}, u32[]{:S(2)}) collective-permute-start(bf16[176,800]{1,0:T(8,128)(2,1)} %get-tuple-element.296), channel_id=1, source_target_pairs={{0,3},{1,2},{2,1},{3,0},{4,7},{5,6},{6,5},{7,4},{8,11},{9,10},{10,... | collective-permute-start | bytes 844808 | tf_op jit(solution)/shard_map/ppermute | solution.py:699
  469.1 30.7 %collective-permute-start.48 = (bf16[16,56,800]{2,1,0:T(8,128)(2,1)}, bf16[16,56,800]{2,1,0:T(8,128)(2,1)}, u32[]{:S(2)}, u32[]{:S(2)}) collective-permute-start(bf16[16,56,800]{2,1,0:T(8,128)(2,1)} %get-tuple-element.308), channel_id=1, source_target_pairs={{0,4},{4,0},{8,12},{12,8},{16,20},{20,16},{24,28},{28,24},{1,5},{5... | collective-permute-start | bytes 4300808 | tf_op jit(solution)/shard_map/ppermute | solution.py:699
  470.5 24.8 %collective-permute-start.46 = (bf16[1,2,176,800]{3,2,1,0:T(8,128)(2,1)}, bf16[1,2,176,800]{3,2,1,0:T(8,128)(2,1)}, u32[]{:S(2)}, u32[]{:S(2)}) collective-permute-start(bf16[1,2,176,800]{3,2,1,0:T(8,128)(2,1)} %get-tuple-element.305), channel_id=1, source_target_pairs={{0,8},{4,12},{8,0},{12,4},{16,24},{20,28},{24,16},{28,20},{1,9},{5... | collective-permute-start | bytes 1689608 | tf_op jit(solution)/shard_map/ppermute | solution.py:699
  472.8 21.5 %collective-permute-start.45 = (bf16[1,176,800]{2,1,0:T(8,128)(2,1)S(1)}, bf16[1,176,800]{2,1,0:T(8,128)(2,1)}, u32[]{:S(2)}, u32[]{:S(2)}) collective-permute-start(bf16[1,176,800]{2,1,0:T(8,128)(2,1)S(1)} %fusion.29), channel_id=1, source_target_pairs={{0,8},{4,12},{8,0},{12,4},{16,24},{20,28},{24,16},{28,20},{1,9},{5... | collective-permute-start | bytes 844808 | tf_op jit(solution)/shard_map/ppermute | solution.py:699
  473.8 23.5 %collective-permute-start.47 = (bf16[1,2,176,800]{3,2,1,0:T(8,128)(2,1)}, bf16[1,2,176,800]{3,2,1,0:T(8,128)(2,1)}, u32[]{:S(2)}, u32[]{:S(2)}) collective-permute-start(bf16[1,2,176,800]{3,2,1,0:T(8,128)(2,1)} %get-tuple-element.306), channel_id=1, source_target_pairs={{0,16},{4,20},{8,24},{12,28},{16,0},{20,4},{24,8},{28,12},{1,17},{... | collective-permute-start | bytes 1689608 | tf_op jit(solution)/shard_map/ppermute | solution.py:699
  502.0 30.5 %collective-permute-start.53 = (bf16[2,2,56,800]{3,2,1,0:T(8,128)(2,1)}, bf16[2,2,56,800]{3,2,1,0:T(8,128)(2,1)}, u32[]{:S(2)}, u32[]{:S(2)}) collective-permute-start(bf16[2,2,56,800]{3,2,1,0:T(8,128)(2,1)} %bitcast.75), channel_id=1, source_target_pairs={{0,16},{4,20},{8,24},{12,28},{16,0},{20,4},{24,8},{28,12},{1,17},{... | collective-permute-start | bytes 1075208 | tf_op jit(solution)/shard_map/ppermute | solution.py:699
  503.3 29.2 %collective-permute-start.54 = (bf16[2,2,56,800]{3,2,1,0:T(8,128)(2,1)}, bf16[2,2,56,800]{3,2,1,0:T(8,128)(2,1)}, u32[]{:S(2)}, u32[]{:S(2)}) collective-permute-start(bf16[2,2,56,800]{3,2,1,0:T(8,128)(2,1)} %bitcast.76), channel_id=1, source_target_pairs={{0,8},{4,12},{8,0},{12,4},{16,24},{20,28},{24,16},{28,20},{1,9},{5... | collective-permute-start | bytes 1075208 | tf_op jit(solution)/shard_map/ppermute | solution.py:699
  504.6 19.2 %collective-permute-start.50 = (bf16[176,800]{1,0:T(8,128)(2,1)}, bf16[176,800]{1,0:T(8,128)(2,1)S(1)}, u32[]{:S(2)}, u32[]{:S(2)}) collective-permute-start(bf16[176,800]{1,0:T(8,128)(2,1)} %fusion.26), channel_id=1, source_target_pairs={{0,1},{1,0},{2,3},{3,2},{4,5},{5,4},{6,7},{7,6},{8,9},{9,8},{10,11... | collective-permute-start | bytes 844808 | tf_op jit(solution)/shard_map/ppermute | solution.py:699
  505.7 25.1 %collective-permute-start.51 = (bf16[176,800]{1,0:T(8,128)(2,1)}, bf16[176,800]{1,0:T(8,128)(2,1)}, u32[]{:S(2)}, u32[]{:S(2)}) collective-permute-start(bf16[176,800]{1,0:T(8,128)(2,1)} %get-tuple-element.314), channel_id=1, source_target_pairs={{0,2},{1,3},{2,0},{3,1},{4,6},{5,7},{6,4},{7,5},{8,10},{9,11},{10,... | collective-permute-start | bytes 844808 | tf_op jit(solution)/shard_map/ppermute | solution.py:699
  506.6 24.2 %collective-permute-start.52 = (bf16[176,800]{1,0:T(8,128)(2,1)}, bf16[176,800]{1,0:T(8,128)(2,1)}, u32[]{:S(2)}, u32[]{:S(2)}) collective-permute-start(bf16[176,800]{1,0:T(8,128)(2,1)} %get-tuple-element.315), channel_id=1, source_target_pairs={{0,3},{1,2},{2,1},{3,0},{4,7},{5,6},{6,5},{7,4},{8,11},{9,10},{10,... | collective-permute-start | bytes 844808 | tf_op jit(solution)/shard_map/ppermute | solution.py:699
  523.7 14.6 %collective-permute-start.49 = (bf16[2,176,800]{2,1,0:T(8,128)(2,1)S(1)}, bf16[2,176,800]{2,1,0:T(8,128)(2,1)}, u32[]{:S(2)}, u32[]{:S(2)}) collective-permute-start(bf16[2,176,800]{2,1,0:T(8,128)(2,1)S(1)} %pad_maximum_fusion.9), channel_id=1, source_target_pairs={{0,16},{4,20},{8,24},{12,28},{16,0},{20,4},{24,8},{28,12},{1,17},{... | collective-permute-start | bytes 1689608 | tf_op jit(solution)/shard_map/ppermute | solution.py:699
  539.6 10.9 %collective-permute-start.58 = (f32[18,1600]{1,0:T(8,128)S(1)}, f32[18,1600]{1,0:T(8,128)S(1)}, u32[]{:S(2)}, u32[]{:S(2)}) collective-permute-start(f32[18,1600]{1,0:T(8,128)S(1)} %concatenate.66), channel_id=1, source_target_pairs={{0,4},{4,0},{8,12},{12,8},{16,20},{20,16},{24,28},{28,24},{1,5},{5... | collective-permute-start | bytes 345608 | tf_op jit(solution)/shard_map/ppermute | solution.py:699
  539.6 11.9 %collective-permute-start.57 = (bf16[1,2,56,800]{3,2,1,0:T(8,128)(2,1)S(1)}, bf16[1,2,56,800]{3,2,1,0:T(8,128)(2,1)}, u32[]{:S(2)}, u32[]{:S(2)}) collective-permute-start(bf16[1,2,56,800]{3,2,1,0:T(8,128)(2,1)S(1)} %get-tuple-element.331), channel_id=1, source_target_pairs={{0,16},{4,20},{8,24},{12,28},{16,0},{20,4},{24,8},{28,12},{1,17},{... | collective-permute-start | bytes 537608 | tf_op jit(solution)/shard_map/ppermute | solution.py:699
  540.3 10.2 %collective-permute-start.56 = (bf16[1,2,56,800]{3,2,1,0:T(8,128)(2,1)S(1)}, bf16[1,2,56,800]{3,2,1,0:T(8,128)(2,1)S(1)}, u32[]{:S(2)}, u32[]{:S(2)}) collective-permute-start(bf16[1,2,56,800]{3,2,1,0:T(8,128)(2,1)S(1)} %get-tuple-element.330), channel_id=1, source_target_pairs={{0,8},{4,12},{8,0},{12,4},{16,24},{20,28},{24,16},{28,20},{1,9},{5... | collective-permute-start | bytes 537608 | tf_op jit(solution)/shard_map/ppermute | solution.py:699
  541.2 12.9 %collective-permute-start.55 = (bf16[1,176,800]{2,1,0:T(8,128)(2,1)S(1)}, bf16[1,176,800]{2,1,0:T(8,128)(2,1)S(1)}, u32[]{:S(2)}, u32[]{:S(2)}) collective-permute-start(bf16[1,176,800]{2,1,0:T(8,128)(2,1)S(1)} %fusion.30), channel_id=1, source_target_pairs={{0,8},{4,12},{8,0},{12,4},{16,24},{20,28},{24,16},{28,20},{1,9},{5... | collective-permute-start | bytes 844808 | tf_op jit(solution)/shard_map/ppermute | solution.py:699
  542.3 32.8 %collective-permute-start.59 = (bf16[4,176,800]{2,1,0:T(8,128)(2,1)S(1)}, bf16[4,176,800]{2,1,0:T(8,128)(2,1)}, u32[]{:S(2)}, u32[]{:S(2)}) collective-permute-start(bf16[4,176,800]{2,1,0:T(8,128)(2,1)S(1)} %pad_maximum_fusion.2.refs_1_), channel_id=1, source_target_pairs={{0,4},{4,0},{8,12},{12,8},{16,20},{20,16},{24,28},{28,24},{1,5},{5... | collective-permute-start | bytes 3379208 | tf_op jit(solution)/shard_map/ppermute | solution.py:699
  554.2 19.6 %collective-permute-start.60 = (bf16[2,176,800]{2,1,0:T(8,128)(2,1)S(1)}, bf16[2,176,800]{2,1,0:T(8,128)(2,1)}, u32[]{:S(2)}, u32[]{:S(2)}) collective-permute-start(bf16[2,176,800]{2,1,0:T(8,128)(2,1)S(1)} %pad_maximum_fusion.10), channel_id=1, source_target_pairs={{0,16},{4,20},{8,24},{12,28},{16,0},{20,4},{24,8},{28,12},{1,17},{... | collective-permute-start | bytes 1689608 | tf_op jit(solution)/shard_map/ppermute | solution.py:699
  555.7 12.8 %collective-permute-start.61 = (bf16[56,800]{1,0:T(8,128)(2,1)S(1)}, bf16[56,800]{1,0:T(8,128)(2,1)S(1)}, u32[]{:S(2)}, u32[]{:S(2)}) collective-permute-start(bf16[56,800]{1,0:T(8,128)(2,1)S(1)} %fusion.39), channel_id=1, source_target_pairs={{0,1},{1,0},{2,3},{3,2},{4,5},{5,4},{6,7},{7,6},{8,9},{9,8},{10,11... | collective-permute-start | bytes 268808 | tf_op jit(solution)/shard_map/ppermute | solution.py:699
  556.6 12.7 %collective-permute-start.62 = (bf16[56,800]{1,0:T(8,128)(2,1)}, bf16[56,800]{1,0:T(8,128)(2,1)S(1)}, u32[]{:S(2)}, u32[]{:S(2)}) collective-permute-start(bf16[56,800]{1,0:T(8,128)(2,1)} %get-tuple-element.341), channel_id=1, source_target_pairs={{0,2},{1,3},{2,0},{3,1},{4,6},{5,7},{6,4},{7,5},{8,10},{9,11},{10,... | collective-permute-start | bytes 268808 | tf_op jit(solution)/shard_map/ppermute | solution.py:699
  557.7 11.5 %collective-permute-start.63 = (bf16[56,800]{1,0:T(8,128)(2,1)S(1)}, bf16[56,800]{1,0:T(8,128)(2,1)S(1)}, u32[]{:S(2)}, u32[]{:S(2)}) collective-permute-start(bf16[56,800]{1,0:T(8,128)(2,1)S(1)} %get-tuple-element.342), channel_id=1, source_target_pairs={{0,3},{1,2},{2,1},{3,0},{4,7},{5,6},{6,5},{7,4},{8,11},{9,10},{10,... | collective-permute-start | bytes 268808 | tf_op jit(solution)/shard_map/ppermute | solution.py:699
  580.1 7.0 %collective-permute-start.65 = (bf16[4,176,800]{2,1,0:T(8,128)(2,1)S(1)}, bf16[4,176,800]{2,1,0:T(8,128)(2,1)S(1)}, u32[]{:S(2)}, u32[]{:S(2)}) collective-permute-start(bf16[4,176,800]{2,1,0:T(8,128)(2,1)S(1)} %pad_maximum_fusion.3.refs_1_), channel_id=1, source_target_pairs={{0,4},{4,0},{8,12},{12,8},{16,20},{20,16},{24,28},{28,24},{1,5},{5... | collective-permute-start | bytes 3379208 | tf_op jit(solution)/shard_map/ppermute | solution.py:699
  592.9 6.3 %collective-permute-start.68 = (bf16[2,56,800]{2,1,0:T(8,128)(2,1)S(1)}, bf16[2,56,800]{2,1,0:T(8,128)(2,1)S(1)}, u32[]{:S(2)}, u32[]{:S(2)}) collective-permute-start(bf16[2,56,800]{2,1,0:T(8,128)(2,1)S(1)} %pad_maximum_fusion.15), channel_id=1, source_target_pairs={{0,16},{4,20},{8,24},{12,28},{16,0},{20,4},{24,8},{28,12},{1,17},{... | collective-permute-start | bytes 537608 | tf_op jit(solution)/shard_map/ppermute | solution.py:699
  599.2 8.3 %collective-permute-start.71 = (f32[18,1600]{1,0:T(8,128)S(1)}, f32[18,1600]{1,0:T(8,128)S(1)}, u32[]{:S(2)}, u32[]{:S(2)}) collective-permute-start(f32[18,1600]{1,0:T(8,128)S(1)} %add.567), channel_id=1, source_target_pairs={{0,2},{1,3},{2,0},{3,1},{4,6},{5,7},{6,4},{7,5},{8,10},{9,11},{10,... | collective-permute-start | bytes 345608 | tf_op jit(solution)/shard_map/ppermute | solution.py:699
  599.3 12.1 %collective-permute-start.70 = (bf16[4,56,800]{2,1,0:T(8,128)(2,1)S(1)}, bf16[4,56,800]{2,1,0:T(8,128)(2,1)S(1)}, u32[]{:S(2)}, u32[]{:S(2)}) collective-permute-start(bf16[4,56,800]{2,1,0:T(8,128)(2,1)S(1)} %pad_maximum_fusion.13.refs_1_), channel_id=1, source_target_pairs={{0,4},{4,0},{8,12},{12,8},{16,20},{20,16},{24,28},{28,24},{1,5},{5... | collective-permute-start | bytes 1075208 | tf_op jit(solution)/shard_map/ppermute | solution.py:699
  (45 other events, 263.3 us)

commit v3 on v2

--- a/solution.py
+++ b/solution.py
@@ -37,21 +37,17 @@
     return centred * scale, scale
 
 
-def logistic(inner):
-    return 0.5 * jnp.tanh(0.5 * inner) + 0.5
-
-
 def norm_silu(values, gain, shift):
     unit, _ = normalized(values)
-    inner = unit * gain + shift
-    return inner * logistic(inner)
+    half = unit * gain + shift
+    return half * (1.0 + jnp.tanh(half))
 
 
 def norm_silu_back(values, gain, shift, grad):
     unit, scale = normalized(values)
-    inner = unit * gain + shift
-    gate = logistic(inner)
-    grad_inner = grad * (gate + inner * gate * (1.0 - gate))
+    half = unit * gain + shift
+    slope = jnp.tanh(half)
+    grad_inner = grad * ((1.0 + slope) * (1.0 + half * (1.0 - slope)))
     grad_unit = grad_inner * gain
     along = jnp.mean(grad_unit * unit, axis=-1, keepdims=True)
     level = jnp.mean(grad_unit, axis=-1, keepdims=True)
@@ -928,7 +924,7 @@
     entry_piece = jnp.concatenate([half_piece(encproject), vector_piece], axis=0)
     entry_columns = along_fsdp(tiled(entry_piece))
     entry_spread = Spread(entry_columns, range(fsdp_count), [2])
-    (enc_own,) = move([entry_spread], [], (enc_own,))
+    move([entry_spread], [])
     enc_spreads = spread_pair(along_fsdp(enc_own))
     vector_shards = jnp.stack(
         [column[-vector_rows // 8 :].reshape(-1)[: vector_local.size] for column in entry_columns]
@@ -947,6 +943,8 @@
 
     wides = whole_vectors(vector_shards[:, : wide_local.size], wide_local)
     inners = whole_vectors(vector_shards[:, wide_local.size :], inner_local)
+    wides = wides * jnp.array([0.5, 0.5, 1.0] * 2, F32)[:, None]
+    inners = inners * jnp.array(([0.5] * 4 + [1.0] * 2) * 2, F32)[:, None]
     enc_wide, dec_wide = wides[:3], wides[3:]
     enc_inner, dec_inner = inners[:6], inners[6:]
 
@@ -1285,7 +1283,9 @@
                 finished[index] = finish(chains[index], entry)
         output, finished = slot((output, finished), *chains)
     finished = [entry or finish(chain, kinds) for entry, chain, kinds in zip(finished, chains, names)]
-    sums = vector_reduce.finish() * factor
+    norm_sums = [0.5, 0.5, 1.0]
+    shares = jnp.array(norm_sums[:2] + norm_sums + [1.0] + norm_sums * 4, F32)
+    sums = vector_reduce.finish() * (shares * factor)[:, None]
     wide_sums = sums[:6]
     order = [wide_sums[:2], wide_sums[4:5], wide_sums[2:4], wide_sums[5:]]
     wide_own = own_columns(jnp.concatenate(order))

time: 624 us -> 618 us (level)
  transfers between devices with their start and end apart: 72 -> 72, of which waited for: 25 -> 24; matrix products, arithmetic and copies ran while one was open for 10% -> 10% of each run, Pallas kernels for 38% -> 38%
where the time goes in v3:
time: 618 us; the launch traced here: 610 us
  Pallas kernels  325 us (53%)
  waiting for transfers between devices  101 us (16%)
  starting transfers between devices  96.4 us (16%)
  other arithmetic  53.9 us (9%)
  local copies, waits for them, and re-layouts  31.2 us (5%)
    pallas_call x14, Pallas kernels, call(): pl.pallas_call(kernel, grid=(steps,), in_specs=in_specs, out_specs=[stepp...  313 us
    ppermute x66, waiting for transfers between devices, exchanged(): lax.ppermute(block, axis, [(i, i ^ bit) for i in range(lax.axis_size(axis...  97.3 us
    ppermute x66, starting transfers between devices, exchanged(): lax.ppermute(block, axis, [(i, i ^ bit) for i in range(lax.axis_size(axis...  86.8 us
    convert_element_type x6, other arithmetic, add_low(): return total.astype(BF16)  21 us
  transfers between devices with their start and end apart: 72, of which 24 were waited for; matrix products, arithmetic and copies ran while one was open for 10% of the time, Pallas kernels for 38%

profile of v3, /device:TPU:0, one launch (start us, length us, event | category | flops | bytes accessed | tf_op | source)
XLA Modules:
  0.0 609.6 jit_solution(16111151398456011707)
XLA Ops:
  4.8 3.0 collective-permute-start.3
  7.8 2.6 collective-permute-start.4
  12.8 2.0 collective-permute-start.1
  14.8 2.0 collective-permute-start.2
  19.6 24.7 %collective-permute-done.4 = bf16[15,8,800]{2,1,0:T(8,128)(2,1)} collective-permute-done((bf16[15,8,800]{2,1,0:T(8,128)(2,1)}, bf16[15,8,800]{2,1,0:T(8,128)(2,1)}, u32[]{:S(2)}, u32[]{:S(2)}) %collective-permute-start.4) | collective-permute-done | bytes 192032 | tf_op jit(solution)/shard_map/ppermute | solution.py:695
  50.3 7.4 %collective-permute-done.1 = bf16[29,8,800]{2,1,0:T(8,128)(2,1)S(1)} collective-permute-done((bf16[29,8,800]{2,1,0:T(8,128)(2,1)S(1)}, bf16[29,8,800]{2,1,0:T(8,128)(2,1)S(1)}, u32[]{:S(2)}, u32[]{:S(2)}) %collective-permute-start.1) | collective-permute-done | bytes 371232 | tf_op jit(solution)/shard_map/ppermute | solution.py:695
  62.2 10.8 %collective-permute-start.11 = (bf16[16,8,800]{2,1,0:T(8,128)(2,1)S(1)}, bf16[16,8,800]{2,1,0:T(8,128)(2,1)S(1)}, u32[]{:S(2)}, u32[]{:S(2)}) collective-permute-start(bf16[16,8,800]{2,1,0:T(8,128)(2,1)S(1)} %fusion.32), channel_id=1, source_target_pairs={{0,1},{1,0},{2,3},{3,2},{4,5},{5,4},{6,7},{7,6},{8,9},{9,8},{10,11... | collective-permute-start | bytes 614408 | tf_op jit(solution)/shard_map/ppermute | solution.py:695
  74.7 2.1 collective-permute-done.10
  78.0 1.6 pad_maximum_fusion
  79.7 2.7 collective-permute-done.12
  85.3 2.5 collective-permute-start.13
  87.8 18.8 %shard_map.315 = (bf16[4,480,1600]{2,1,0:T(8,128)(2,1)}, f32[4,480,800]{2,1,0:T(8,128)}, bf16[4,480,800]{2,1,0:T(8,128)(2,1)}, bf16[1600,800]{1,0:T(8,128)(2,1)}) custom-call(s32[3]{0:T(128)} %pad_add_fusion.2.refs_0_, bf16[4,480,1600]{2,1,0:T(8,128)(2,1)} %bitcast.181, bf16[4,120,800]{2,1,0:T(8,128)(2,1)} %bitcast.17.refs_2_, ...), custom_call_target="tpu_custom_call" | custom-call | flops 4915200000 | bytes 27174400 | tf_op jit(solution)/shard_map/pallas_call | solution.py:654
  107.6 7.6 %collective-permute-done.14 = bf16[4,29,8,800]{3,2,1,0:T(8,128)(2,1)} collective-permute-done((bf16[4,29,8,800]{3,2,1,0:T(8,128)(2,1)S(1)}, bf16[4,29,8,800]{3,2,1,0:T(8,128)(2,1)}, u32[]{:S(2)}, u32[]{:S(2)}) %collective-permute-start.14) | collective-permute-done | bytes 1484832 | tf_op jit(solution)/shard_map/ppermute | solution.py:695
  115.2 6.7 %collective-permute-done.16 = bf16[4,29,8,800]{3,2,1,0:T(8,128)(2,1)} collective-permute-done((bf16[4,29,8,800]{3,2,1,0:T(8,128)(2,1)}, bf16[4,29,8,800]{3,2,1,0:T(8,128)(2,1)}, u32[]{:S(2)}, u32[]{:S(2)}) %collective-permute-start.16) | collective-permute-done | bytes 1484832 | tf_op jit(solution)/shard_map/ppermute | solution.py:695
  122.6 1.9 collective-permute-start.18
  126.9 3.8 collective-permute-start.22
  131.9 39.1 %shard_map.316 = (f32[4,480,800]{2,1,0:T(8,128)}, bf16[4,480,800]{2,1,0:T(8,128)(2,1)}, f32[4,480,1600]{2,1,0:T(8,128)}, bf16[800,1600]{1,0:T(8,128)(2,1)}, bf16...) custom-call(s32[3]{0:T(128)} %pad_add_fusion.2.refs_0_, bf16[4,480,800]{2,1,0:T(8,128)(2,1)} %get-tuple-element.207.refs_1_.refs_5_, ...), custom_call_target="tpu_custom_call" | custom-call | flops 17203200000 | bytes 54380800 | tf_op jit(solution)/shard_map/pallas_call | solution.py:654
  173.9 17.2 %shard_map.317 = (bf16[4,480,1600]{2,1,0:T(8,128)(2,1)}, f32[4,480,800]{2,1,0:T(8,128)}, bf16[4,480,800]{2,1,0:T(8,128)(2,1)}) custom-call(f32[4,480,1600]{2,1,0:T(8,128)} %get-tuple-element.229.refs_0_.refs_1_, f32[3,1600]{1,0:T(4,128)} %get-tuple-element.329.refs_1_.refs_6_.refs_3_, f32[6,800]{1,0:T(8,128)} %get-tuple-element.237.refs_2_.refs_13_.refs_8_, ...), custom_call_target="tpu_custom_call" | custom-call | flops 4915200000 | bytes 30246400 | tf_op jit(solution)/shard_map/pallas_call | solution.py:654
  192.0 1.9 collective-permute-done.24
  193.9 2.3 collective-permute-done.26
  196.7 1.9 collective-permute-start.28
  201.3 42.0 %shard_map.318 = (bf16[4,480,800]{2,1,0:T(8,128)(2,1)}, bf16[4,480,800]{2,1,0:T(8,128)(2,1)}, bf16[800,1600]{1,0:T(8,128)(2,1)}, bf16[800,2400]{1,0:T(8,128)(2,1...) custom-call(s32[3]{0:T(128)} %pad_add_fusion.2.refs_0_, ...), custom_call_target="tpu_custom_call" | custom-call | flops 17203200000 | bytes 31237120 | tf_op jit(solution)/shard_map/pallas_call | solution.py:654
  246.6 3.3 collective-permute-done.31.refs_2_
  250.6 41.8 %shard_map.319 = (bf16[4,480,800]{2,1,0:T(8,128)(2,1)}, bf16[16,176,800]{2,1,0:T(8,128)(2,1)}, bf16[16,176,800]{2,1,0:T(8,128)(2,1)}, f32[3,8,800]{2,1,0:T(8,128)}) custom-call(s32[3]{0:T(128)} %pad_add_fusion.2.refs_0_, bf16[4,480,800]{2,1,0:T(8,128)(2,1)} %get-tuple-element.257.refs_1_, bf16[4,32,800]{2,1,0:T(8,128)(2,1)} %copy-done.35, ...), custom_call_target="tpu_custom_call" | custom-call | flops 19660800000 | bytes 37227520 | tf_op jit(solution)/shard_map/pallas_call | solution.py:654
  292.4 5.3 collective-permute-start.34
  298.9 43.5 %shard_map.320 = (f32[4,480,1600]{2,1,0:T(8,128)}, bf16[4,480,800]{2,1,0:T(8,128)(2,1)}, bf16[800,1600]{1,0:T(8,128)(2,1)}, f32[3,8,1600]{2,1,0:T(8,128)}, f32[3,8,800]{2,1,0:T(8,128)}) custom-call(bf16[4,480,800]{2,1,0:T(8,128)(2,1)} %get-tuple-element.264.refs_0_, f32[4,480,1600]{2,1,0:T(8,128)} %get-tuple-element.229.refs_0_.refs_1_, ...), custom_call_target="tpu_custom_call" | custom-call | flops 14745600000 | bytes 54028800 | tf_op jit(solution)/shard_map/pallas_call | solution.py:654
  343.5 1.9 collective-permute-start.32
  346.7 4.5 add_convert_fusion.2
  351.2 3.8 collective-permute-start.35
  356.5 24.8 %shard_map.321 = (bf16[16,176,800]{2,1,0:T(8,128)(2,1)}, bf16[16,176,800]{2,1,0:T(8,128)(2,1)}) custom-call(s32[3]{0:T(128)} %pad_add_fusion.2.refs_0_, bf16[4,480,800]{2,1,0:T(8,128)(2,1)} %get-tuple-element.268.refs_1_.refs_0_, bf16[4,16,800]{2,1,0:T(8,128)(2,1)} %copy-done.36, bf16[4,16,800]{2,1,0:T(8,128)(2,1)} %copy-done.37, ...), custom_call_target="tpu_custom_call" | custom-call | flops 12288000000 | bytes 17939200 | tf_op jit(solution)/shard_map/pallas_call | solution.py:654
  381.3 2.1 collective-permute-done.35
  383.4 4.1 fusion.2
  393.7 15.1 %shard_map.322 = (bf16[4,480,800]{2,1,0:T(8,128)(2,1)}, f32[3,8,800]{2,1,0:T(8,128)}) custom-call(bf16[4,480,800]{2,1,0:T(8,128)(2,1)} %get-tuple-element.268.refs_1_.refs_0_, bf16[4,16,800]{2,1,0:T(8,128)(2,1)} %copy-done.36, bf16[4,16,800]{2,1,0:T(8,128)(2,1)} %copy-done.37, bf16[4,480,5]{2,1,0:T(8,128)(2,1)} %convert_element_type.476.refs_4_.refs_3_, ...), custom_call_target="tpu_custom_call" | custom-call | flops 6144000000 | bytes 19008000 | tf_op jit(solution)/shard_map/pallas_call | solution.py:654
  409.9 2.0 fusion.22
  411.9 2.2 fusion.24
  414.2 4.5 add_convert_fusion
  420.0 8.3 %collective-permute-start.40 = (bf16[176,800]{1,0:T(8,128)(2,1)}, bf16[176,800]{1,0:T(8,128)(2,1)S(1)}, u32[]{:S(2)}, u32[]{:S(2)}) collective-permute-start(bf16[176,800]{1,0:T(8,128)(2,1)} %fusion.22), channel_id=1, source_target_pairs={{0,1},{1,0},{2,3},{3,2},{4,5},{5,4},{6,7},{7,6},{8,9},{9,8},{10,11... | collective-permute-start | bytes 844808 | tf_op jit(solution)/shard_map/ppermute | solution.py:695
  430.8 15.0 %shard_map.323 = (bf16[4,480,800]{2,1,0:T(8,128)(2,1)}, f32[3,8,800]{2,1,0:T(8,128)}) custom-call(bf16[4,480,800]{2,1,0:T(8,128)(2,1)} %get-tuple-element.268.refs_1_.refs_0_, bf16[4,16,800]{2,1,0:T(8,128)(2,1)} %copy-done.36, bf16[4,16,800]{2,1,0:T(8,128)(2,1)} %copy-done.37, ...), custom_call_target="tpu_custom_call", output_to_operand_aliasing={{0}: (7, {})} | custom-call | flops 6144000000 | bytes 19008000 | tf_op jit(solution)/shard_map/pallas_call | solution.py:654
  445.8 12.3 %shard_map.324 = (bf16[16,56,800]{2,1,0:T(8,128)(2,1)}, bf16[16,56,800]{2,1,0:T(8,128)(2,1)}) custom-call(s32[3]{0:T(128)} %pad_add_fusion.2.refs_0_, bf16[4,480,1600]{2,1,0:T(8,128)(2,1)} %get-tuple-element.295.refs_1_, bf16[4,480,800]{2,1,0:T(8,128)(2,1)} %get-tuple-element.287.refs_2_.refs_0_), custom_call_target="tpu_custom_call" | custom-call | flops 4915200000 | bytes 12083200 | tf_op jit(solution)/shard_map/pallas_call | solution.py:654
  459.5 3.5 fusion
  469.0 13.4 %shard_map.325 = (bf16[4,480,1600]{2,1,0:T(8,128)(2,1)}, f32[2,8,1600]{2,1,0:T(8,128)}) custom-call(bf16[4,480,800]{2,1,0:T(8,128)(2,1)} %get-tuple-element.287.refs_2_.refs_0_, bf16[4,480,1600]{2,1,0:T(8,128)(2,1)} %bitcast.183, f32[4,480,1600]{2,1,0:T(8,128)} %get-tuple-element.288.refs_2_, bf16[1600,800]{1,0:T(8,128)(2,1)} %get-tuple-element.289.refs_3_, ...), custom_call_target="tpu_custom_call" | custom-call | flops 2457600000 | bytes 30329600 | tf_op jit(solution)/shard_map/pallas_call | solution.py:654
  482.5 5.6 collective-permute-done.45
  489.2 1.9 fusion.25
  491.1 2.5 fusion.27
  493.7 2.2 add_convert_fusion.4
  499.6 1.9 collective-permute-start.51
  504.0 13.5 %shard_map.326 = (bf16[4,480,1600]{2,1,0:T(8,128)(2,1)}, f32[2,8,1600]{2,1,0:T(8,128)}) custom-call(bf16[4,480,800]{2,1,0:T(8,128)(2,1)} %get-tuple-element.287.refs_2_.refs_0_, bf16[4,480,1600]{2,1,0:T(8,128)(2,1)} %bitcast.184, f32[4,480,1600]{2,1,0:T(8,128)} %get-tuple-element.288.refs_2_, ...), custom_call_target="tpu_custom_call", output_to_operand_aliasing={{0}: (5, {})} | custom-call | flops 2457600000 | bytes 30329600 | tf_op jit(solution)/shard_map/pallas_call | solution.py:654
  519.4 5.3 collective-permute-done.51
  524.7 1.6 fusion.29
  526.4 2.2 fusion.20
  528.6 3.5 collective-permute-done.49
  536.0 8.1 %shard_map.327.refs_4_ = bf16[4,480,1600]{2,1,0:T(8,128)(2,1)} custom-call(bf16[4,480,800]{2,1,0:T(8,128)(2,1)} %get-tuple-element.255.refs_0_, f32[4,480,1600]{2,1,0:T(8,128)} %get-tuple-element.229.refs_0_.refs_1_, bf16[800,1600]{1,0:T(8,128)(2,1)} %get-tuple-element.256.refs_2_, f32[3,1600]{1,0:T(4,128)} %get-tuple-element.329.refs_1_.refs_6_.refs_3_), custom_call_target="tpu_custom_call" | custom-call | flops 2457600000 | bytes 24083200 | tf_op jit(solution)/shard_map/pallas_call | solution.py:654
  546.3 1.7 collective-permute-done.55
  549.7 1.7 collective-permute-start.61
  554.0 8.4 %shard_map.328 = bf16[4,480,1600]{2,1,0:T(8,128)(2,1)} custom-call(bf16[4,480,800]{2,1,0:T(8,128)(2,1)} %get-tuple-element.255.refs_0_, f32[4,480,1600]{2,1,0:T(8,128)} %get-tuple-element.229.refs_0_.refs_1_, bf16[800,1600]{1,0:T(8,128)(2,1)} %get-tuple-element.256.refs_2_, ...), custom_call_target="tpu_custom_call", output_to_operand_aliasing={{}: (4, {})} | custom-call | flops 2457600000 | bytes 24083200 | tf_op jit(solution)/shard_map/pallas_call | solution.py:654
  564.1 3.6 collective-permute-done.64
  569.1 5.0 shard_map.329
  575.4 3.9 collective-permute-done.66
  579.3 1.6 collective-permute-done.67
  582.1 4.7 shard_map.330
  588.3 4.5 collective-permute-done.69
  593.1 1.8 collective-permute-start.71
  594.9 7.1 %collective-permute-done.71 = f32[18,1600]{1,0:T(8,128)S(1)} collective-permute-done((f32[18,1600]{1,0:T(8,128)S(1)}, f32[18,1600]{1,0:T(8,128)S(1)}, u32[]{:S(2)}, u32[]{:S(2)}) %collective-permute-start.71) | collective-permute-done | bytes 115232 | tf_op jit(solution)/shard_map/ppermute | solution.py:695
  606.7 2.4 shard_map.331
  (310 shorter events, 96.7 us)
Async XLA Ops:
  4.8 14.3 %collective-permute-start.3 = (bf16[15,8,800]{2,1,0:T(8,128)(2,1)}, bf16[15,8,800]{2,1,0:T(8,128)(2,1)}, u32[]{:S(2)}, u32[]{:S(2)}) collective-permute-start(bf16[15,8,800]{2,1,0:T(8,128)(2,1)} %get-tuple-element.580), channel_id=1, source_target_pairs={{0,1},{1,0},{2,3},{3,2},{4,5},{5,4},{6,7},{7,6},{8,9},{9,8},{10,11... | collective-permute-start | bytes 576008 | tf_op jit(solution)/shard_map/ppermute | solution.py:695
  7.8 36.5 %collective-permute-start.4 = (bf16[15,8,800]{2,1,0:T(8,128)(2,1)}, bf16[15,8,800]{2,1,0:T(8,128)(2,1)}, u32[]{:S(2)}, u32[]{:S(2)}) collective-permute-start(bf16[15,8,800]{2,1,0:T(8,128)(2,1)} %get-tuple-element.580), channel_id=1, source_target_pairs={{0,2},{1,3},{2,0},{3,1},{4,6},{5,7},{6,4},{7,5},{8,10},{9,11},{10,... | collective-permute-start | bytes 576008 | tf_op jit(solution)/shard_map/ppermute | solution.py:695
  10.4 33.9 %collective-permute-start.5 = (bf16[15,8,800]{2,1,0:T(8,128)(2,1)}, bf16[15,8,800]{2,1,0:T(8,128)(2,1)}, u32[]{:S(2)}, u32[]{:S(2)}) collective-permute-start(bf16[15,8,800]{2,1,0:T(8,128)(2,1)} %get-tuple-element.580), channel_id=1, source_target_pairs={{0,3},{1,2},{2,1},{3,0},{4,7},{5,6},{6,5},{7,4},{8,11},{9,10},{10,... | collective-permute-start | bytes 576008 | tf_op jit(solution)/shard_map/ppermute | solution.py:695
  12.8 44.9 %collective-permute-start.1 = (bf16[29,8,800]{2,1,0:T(8,128)(2,1)S(1)}, bf16[29,8,800]{2,1,0:T(8,128)(2,1)S(1)}, u32[]{:S(2)}, u32[]{:S(2)}) collective-permute-start(bf16[29,8,800]{2,1,0:T(8,128)(2,1)S(1)} %bitcast.187), channel_id=1, source_target_pairs={{0,2},{1,3},{2,0},{3,1},{4,6},{5,7},{6,4},{7,5},{8,10},{9,11},{10,... | collective-permute-start | bytes 1113608 | tf_op jit(solution)/shard_map/ppermute | solution.py:695
  14.8 43.0 %collective-permute-start.2 = (bf16[29,8,800]{2,1,0:T(8,128)(2,1)S(1)}, bf16[29,8,800]{2,1,0:T(8,128)(2,1)}, u32[]{:S(2)}, u32[]{:S(2)}) collective-permute-start(bf16[29,8,800]{2,1,0:T(8,128)(2,1)S(1)} %bitcast.188), channel_id=1, source_target_pairs={{0,3},{1,2},{2,1},{3,0},{4,7},{5,6},{6,5},{7,4},{8,11},{9,10},{10,... | collective-permute-start | bytes 1113608 | tf_op jit(solution)/shard_map/ppermute | solution.py:695
  19.1 39.8 %collective-permute-start = (bf16[29,8,800]{2,1,0:T(8,128)(2,1)S(1)}, bf16[29,8,800]{2,1,0:T(8,128)(2,1)S(1)}, u32[]{:S(2)}, u32[]{:S(2)}) collective-permute-start(bf16[29,8,800]{2,1,0:T(8,128)(2,1)S(1)} %bitcast.189), channel_id=1, source_target_pairs={{0,1},{1,0},{2,3},{3,2},{4,5},{5,4},{6,7},{7,6},{8,9},{9,8},{10,11... | collective-permute-start | bytes 1113608 | tf_op jit(solution)/shard_map/ppermute | solution.py:695
  45.7 13.4 %collective-permute-start.6 = (bf16[4,15,8,800]{3,2,1,0:T(8,128)(2,1)S(1)}, bf16[4,15,8,800]{3,2,1,0:T(8,128)(2,1)}, u32[]{:S(2)}, u32[]{:S(2)}) collective-permute-start(bf16[4,15,8,800]{3,2,1,0:T(8,128)(2,1)S(1)} %pad_maximum_fusion.6), channel_id=1, source_target_pairs={{0,8},{4,12},{8,0},{12,4},{16,24},{20,28},{24,16},{28,20},{1,9},{5... | collective-permute-start | bytes 2304008 | tf_op jit(solution)/shard_map/ppermute | solution.py:695
  47.2 11.8 %collective-permute-start.7 = (bf16[4,15,8,800]{3,2,1,0:T(8,128)(2,1)S(1)}, bf16[4,15,8,800]{3,2,1,0:T(8,128)(2,1)}, u32[]{:S(2)}, u32[]{:S(2)}) collective-permute-start(bf16[4,15,8,800]{3,2,1,0:T(8,128)(2,1)S(1)} %pad_maximum_fusion.6), channel_id=1, source_target_pairs={{0,4},{4,0},{8,12},{12,8},{16,20},{20,16},{24,28},{28,24},{1,5},{5... | collective-permute-start | bytes 2304008 | tf_op jit(solution)/shard_map/ppermute | solution.py:695
  59.0 17.8 %collective-permute-start.10 = (bf16[2,29,8,800]{3,2,1,0:T(8,128)(2,1)S(1)}, bf16[2,29,8,800]{3,2,1,0:T(8,128)(2,1)S(1)}, u32[]{:S(2)}, u32[]{:S(2)}) collective-permute-start(bf16[2,29,8,800]{3,2,1,0:T(8,128)(2,1)S(1)} %pad_maximum_fusion.8), channel_id=1, source_target_pairs={{0,8},{4,12},{8,0},{12,4},{16,24},{20,28},{24,16},{28,20},{1,9},{5... | collective-permute-start | bytes 2227208 | tf_op jit(solution)/shard_map/ppermute | solution.py:695
  60.6 17.4 %collective-permute-start.9 = (bf16[2,29,8,800]{3,2,1,0:T(8,128)(2,1)S(1)}, bf16[2,29,8,800]{3,2,1,0:T(8,128)(2,1)S(1)}, u32[]{:S(2)}, u32[]{:S(2)}) collective-permute-start(bf16[2,29,8,800]{3,2,1,0:T(8,128)(2,1)S(1)} %pad_maximum_fusion.7), channel_id=1, source_target_pairs={{0,16},{4,20},{8,24},{12,28},{16,0},{20,4},{24,8},{28,12},{1,17},{... | collective-permute-start | bytes 2227208 | tf_op jit(solution)/shard_map/ppermute | solution.py:695
  62.2 17.4 %collective-permute-start.11 = (bf16[16,8,800]{2,1,0:T(8,128)(2,1)S(1)}, bf16[16,8,800]{2,1,0:T(8,128)(2,1)S(1)}, u32[]{:S(2)}, u32[]{:S(2)}) collective-permute-start(bf16[16,8,800]{2,1,0:T(8,128)(2,1)S(1)} %fusion.32), channel_id=1, source_target_pairs={{0,1},{1,0},{2,3},{3,2},{4,5},{5,4},{6,7},{7,6},{8,9},{9,8},{10,11... | collective-permute-start | bytes 614408 | tf_op jit(solution)/shard_map/ppermute | solution.py:695
  73.0 9.4 %collective-permute-start.12 = (bf16[16,8,800]{2,1,0:T(8,128)(2,1)S(1)}, bf16[16,8,800]{2,1,0:T(8,128)(2,1)S(1)}, u32[]{:S(2)}, u32[]{:S(2)}) collective-permute-start(bf16[16,8,800]{2,1,0:T(8,128)(2,1)S(1)} %fusion.32), channel_id=1, source_target_pairs={{0,2},{1,3},{2,0},{3,1},{4,6},{5,7},{6,4},{7,5},{8,10},{9,11},{10,... | collective-permute-start | bytes 614408 | tf_op jit(solution)/shard_map/ppermute | solution.py:695
  74.7 10.6 %collective-permute-start.8 = (bf16[4,15,8,800]{3,2,1,0:T(8,128)(2,1)}, bf16[4,15,8,800]{3,2,1,0:T(8,128)(2,1)}, u32[]{:S(2)}, u32[]{:S(2)}) collective-permute-start(bf16[4,15,8,800]{3,2,1,0:T(8,128)(2,1)} %collective-permute-done.6), channel_id=1, source_target_pairs={{0,4},{4,0},{8,12},{12,8},{16,20},{20,16},{24,28},{28,24},{1,5},{5... | collective-permute-start | bytes 2304008 | tf_op jit(solution)/shard_map/ppermute | solution.py:695
  82.4 32.9 %collective-permute-start.14 = (bf16[4,29,8,800]{3,2,1,0:T(8,128)(2,1)S(1)}, bf16[4,29,8,800]{3,2,1,0:T(8,128)(2,1)}, u32[]{:S(2)}, u32[]{:S(2)}) collective-permute-start(bf16[4,29,8,800]{3,2,1,0:T(8,128)(2,1)S(1)} %get-tuple-element.224), channel_id=1, source_target_pairs={{0,8},{4,12},{8,0},{12,4},{16,24},{20,28},{24,16},{28,20},{1,9},{5... | collective-permute-start | bytes 4454408 | tf_op jit(solution)/shard_map/ppermute | solution.py:695
  82.9 32.3 %collective-permute-start.15 = (bf16[4,29,8,800]{3,2,1,0:T(8,128)(2,1)S(1)}, bf16[4,29,8,800]{3,2,1,0:T(8,128)(2,1)}, u32[]{:S(2)}, u32[]{:S(2)}) collective-permute-start(bf16[4,29,8,800]{3,2,1,0:T(8,128)(2,1)S(1)} %get-tuple-element.224), channel_id=1, source_target_pairs={{0,4},{4,0},{8,12},{12,8},{16,20},{20,16},{24,28},{28,24},{1,5},{5... | collective-permute-start | bytes 4454408 | tf_op jit(solution)/shard_map/ppermute | solution.py:695
  82.9 39.1 %collective-permute-start.16 = (bf16[4,29,8,800]{3,2,1,0:T(8,128)(2,1)}, bf16[4,29,8,800]{3,2,1,0:T(8,128)(2,1)}, u32[]{:S(2)}, u32[]{:S(2)}) collective-permute-start(bf16[4,29,8,800]{3,2,1,0:T(8,128)(2,1)} %get-tuple-element.227), channel_id=1, source_target_pairs={{0,16},{4,20},{8,24},{12,28},{16,0},{20,4},{24,8},{28,12},{1,17},{... | collective-permute-start | bytes 4454408 | tf_op jit(solution)/shard_map/ppermute | solution.py:695
  83.4 38.6 %collective-permute-start.17 = (bf16[4,29,8,800]{3,2,1,0:T(8,128)(2,1)}, bf16[4,29,8,800]{3,2,1,0:T(8,128)(2,1)}, u32[]{:S(2)}, u32[]{:S(2)}) collective-permute-start(bf16[4,29,8,800]{3,2,1,0:T(8,128)(2,1)} %get-tuple-element.227), channel_id=1, source_target_pairs={{0,4},{4,0},{8,12},{12,8},{16,20},{20,16},{24,28},{28,24},{1,5},{5... | collective-permute-start | bytes 4454408 | tf_op jit(solution)/shard_map/ppermute | solution.py:695
  85.3 22.3 %collective-permute-start.13 = (bf16[16,8,800]{2,1,0:T(8,128)(2,1)S(1)}, bf16[16,8,800]{2,1,0:T(8,128)(2,1)S(1)}, u32[]{:S(2)}, u32[]{:S(2)}) collective-permute-start(bf16[16,8,800]{2,1,0:T(8,128)(2,1)S(1)} %fusion.32), channel_id=1, source_target_pairs={{0,3},{1,2},{2,1},{3,0},{4,7},{5,6},{6,5},{7,4},{8,11},{9,10},{10,... | collective-permute-start | bytes 614408 | tf_op jit(solution)/shard_map/ppermute | solution.py:695
  122.0 9.3 %collective-permute-start.20 = (bf16[4,29,8,800]{3,2,1,0:T(8,128)(2,1)}, bf16[4,29,8,800]{3,2,1,0:T(8,128)(2,1)}, u32[]{:S(2)}, u32[]{:S(2)}) collective-permute-start(bf16[4,29,8,800]{3,2,1,0:T(8,128)(2,1)} %collective-permute-done.14), channel_id=1, source_target_pairs={{0,4},{4,0},{8,12},{12,8},{16,20},{20,16},{24,28},{28,24},{1,5},{5... | collective-permute-start | bytes 4454408 | tf_op jit(solution)/shard_map/ppermute | solution.py:695
  122.0 9.3 %collective-permute-start.21 = (bf16[4,29,8,800]{3,2,1,0:T(8,128)(2,1)}, bf16[4,29,8,800]{3,2,1,0:T(8,128)(2,1)}, u32[]{:S(2)}, u32[]{:S(2)}) collective-permute-start(bf16[4,29,8,800]{3,2,1,0:T(8,128)(2,1)} %collective-permute-done.16), channel_id=1, source_target_pairs={{0,4},{4,0},{8,12},{12,8},{16,20},{20,16},{24,28},{28,24},{1,5},{5... | collective-permute-start | bytes 4454408 | tf_op jit(solution)/shard_map/ppermute | solution.py:695
  122.6 8.1 %collective-permute-start.18 = (bf16[4,16,800]{2,1,0:T(8,128)(2,1)S(1)}, bf16[4,16,800]{2,1,0:T(8,128)(2,1)S(1)}, u32[]{:S(2)}, u32[]{:S(2)}) collective-permute-start(bf16[4,16,800]{2,1,0:T(8,128)(2,1)S(1)} %get-tuple-element.213), channel_id=1, source_target_pairs={{0,4},{4,8},{8,12},{12,16},{16,20},{20,24},{24,28},{1,5},{5,9},{9,... | collective-permute-start | bytes 307208 | tf_op jit(solution)/shard_map/ppermute | solution.py:686
  124.5 6.7 %collective-permute-start.19 = (bf16[4,16,800]{2,1,0:T(8,128)(2,1)S(1)}, bf16[4,16,800]{2,1,0:T(8,128)(2,1)S(1)}, u32[]{:S(2)}, u32[]{:S(2)}) collective-permute-start(bf16[4,16,800]{2,1,0:T(8,128)(2,1)S(1)} %get-tuple-element.214), channel_id=1, source_target_pairs={{4,0},{8,4},{12,8},{16,12},{20,16},{24,20},{28,24},{5,1},{9,5},{13... | collective-permute-start | bytes 307208 | tf_op jit(solution)/shard_map/ppermute | solution.py:691
  126.9 44.1 %collective-permute-start.22 = (bf16[2,16,8,800]{3,2,1,0:T(8,128)(2,1)S(1)}, bf16[2,16,8,800]{3,2,1,0:T(8,128)(2,1)S(1)}, u32[]{:S(2)}, u32[]{:S(2)}) collective-permute-start(bf16[2,16,8,800]{3,2,1,0:T(8,128)(2,1)S(1)} %pad_maximum_fusion.11), channel_id=1, source_target_pairs={{0,16},{4,20},{8,24},{12,28},{16,0},{20,4},{24,8},{28,12},{1,17},{... | collective-permute-start | bytes 1228808 | tf_op jit(solution)/shard_map/ppermute | solution.py:695
  130.7 40.4 %collective-permute-start.23 = (bf16[2,16,8,800]{3,2,1,0:T(8,128)(2,1)S(1)}, bf16[2,16,8,800]{3,2,1,0:T(8,128)(2,1)S(1)}, u32[]{:S(2)}, u32[]{:S(2)}) collective-permute-start(bf16[2,16,8,800]{3,2,1,0:T(8,128)(2,1)S(1)} %pad_maximum_fusion.12), channel_id=1, source_target_pairs={{0,8},{4,12},{8,0},{12,4},{16,24},{20,28},{24,16},{28,20},{1,9},{5... | collective-permute-start | bytes 1228808 | tf_op jit(solution)/shard_map/ppermute | solution.py:695
  171.3 22.6 %collective-permute-start.24 = (bf16[4,16,8,800]{3,2,1,0:T(8,128)(2,1)S(1)}, bf16[4,16,8,800]{3,2,1,0:T(8,128)(2,1)}, u32[]{:S(2)}, u32[]{:S(2)}) collective-permute-start(bf16[4,16,8,800]{3,2,1,0:T(8,128)(2,1)S(1)} %pad_maximum_fusion.4), channel_id=1, source_target_pairs={{0,8},{4,12},{8,0},{12,4},{16,24},{20,28},{24,16},{28,20},{1,9},{5... | collective-permute-start | bytes 2457608 | tf_op jit(solution)/shard_map/ppermute | solution.py:695
  172.8 21.1 %collective-permute-start.25 = (bf16[4,16,8,800]{3,2,1,0:T(8,128)(2,1)S(1)}, bf16[4,16,8,800]{3,2,1,0:T(8,128)(2,1)}, u32[]{:S(2)}, u32[]{:S(2)}) collective-permute-start(bf16[4,16,8,800]{3,2,1,0:T(8,128)(2,1)S(1)} %pad_maximum_fusion.4), channel_id=1, source_target_pairs={{0,4},{4,0},{8,12},{12,8},{16,20},{20,16},{24,28},{28,24},{1,5},{5... | collective-permute-start | bytes 2457608 | tf_op jit(solution)/shard_map/ppermute | solution.py:695
  173.9 22.4 %collective-permute-start.26 = (bf16[4,16,8,800]{3,2,1,0:T(8,128)(2,1)S(1)}, bf16[4,16,8,800]{3,2,1,0:T(8,128)(2,1)}, u32[]{:S(2)}, u32[]{:S(2)}) collective-permute-start(bf16[4,16,8,800]{3,2,1,0:T(8,128)(2,1)S(1)} %pad_maximum_fusion.5), channel_id=1, source_target_pairs={{0,16},{4,20},{8,24},{12,28},{16,0},{20,4},{24,8},{28,12},{1,17},{... | collective-permute-start | bytes 2457608 | tf_op jit(solution)/shard_map/ppermute | solution.py:695
  173.9 22.4 %collective-permute-start.27 = (bf16[4,16,8,800]{3,2,1,0:T(8,128)(2,1)S(1)}, bf16[4,16,8,800]{3,2,1,0:T(8,128)(2,1)}, u32[]{:S(2)}, u32[]{:S(2)}) collective-permute-start(bf16[4,16,8,800]{3,2,1,0:T(8,128)(2,1)S(1)} %pad_maximum_fusion.5), channel_id=1, source_target_pairs={{0,4},{4,0},{8,12},{12,8},{16,20},{20,16},{24,28},{28,24},{1,5},{5... | collective-permute-start | bytes 2457608 | tf_op jit(solution)/shard_map/ppermute | solution.py:695
  292.4 54.4 %collective-permute-start.34 = (bf16[16,176,800]{2,1,0:T(8,128)(2,1)}, bf16[16,176,800]{2,1,0:T(8,128)(2,1)}, u32[]{:S(2)}, u32[]{:S(2)}) collective-permute-start(bf16[16,176,800]{2,1,0:T(8,128)(2,1)} %get-tuple-element.272), channel_id=1, source_target_pairs={{0,4},{4,0},{8,12},{12,8},{16,20},{20,16},{24,28},{28,24},{1,5},{5... | collective-permute-start | bytes 13516808 | tf_op jit(solution)/shard_map/ppermute | solution.py:695
  343.5 11.7 %collective-permute-start.32 = (bf16[4,16,800]{2,1,0:T(8,128)(2,1)S(1)}, bf16[4,16,800]{2,1,0:T(8,128)(2,1)S(1)}, u32[]{:S(2)}, u32[]{:S(2)}) collective-permute-start(bf16[4,16,800]{2,1,0:T(8,128)(2,1)S(1)} %get-tuple-element.558), channel_id=1, source_target_pairs={{0,4},{4,8},{8,12},{12,16},{16,20},{20,24},{24,28},{1,5},{5,9},{9,... | collective-permute-start | bytes 307208 | tf_op jit(solution)/shard_map/ppermute | solution.py:686
  345.4 9.8 %collective-permute-start.33 = (bf16[4,16,800]{2,1,0:T(8,128)(2,1)S(1)}, bf16[4,16,800]{2,1,0:T(8,128)(2,1)S(1)}, u32[]{:S(2)}, u32[]{:S(2)}) collective-permute-start(bf16[4,16,800]{2,1,0:T(8,128)(2,1)S(1)} %get-tuple-element.557), channel_id=1, source_target_pairs={{4,0},{8,4},{12,8},{16,12},{20,16},{24,20},{28,24},{5,1},{9,5},{13... | collective-permute-start | bytes 307208 | tf_op jit(solution)/shard_map/ppermute | solution.py:691
  351.2 32.2 %collective-permute-start.35 = (bf16[2,2,176,800]{3,2,1,0:T(8,128)(2,1)}, bf16[2,2,176,800]{3,2,1,0:T(8,128)(2,1)S(1)}, u32[]{:S(2)}, u32[]{:S(2)}) collective-permute-start(bf16[2,2,176,800]{3,2,1,0:T(8,128)(2,1)} %bitcast.52), channel_id=1, source_target_pairs={{0,16},{4,20},{8,24},{12,28},{16,0},{20,4},{24,8},{28,12},{1,17},{... | collective-permute-start | bytes 3379208 | tf_op jit(solution)/shard_map/ppermute | solution.py:695
  355.0 28.4 %collective-permute-start.36 = (bf16[2,2,176,800]{3,2,1,0:T(8,128)(2,1)}, bf16[2,2,176,800]{3,2,1,0:T(8,128)(2,1)S(1)}, u32[]{:S(2)}, u32[]{:S(2)}) collective-permute-start(bf16[2,2,176,800]{3,2,1,0:T(8,128)(2,1)} %bitcast.53), channel_id=1, source_target_pairs={{0,8},{4,12},{8,0},{12,4},{16,24},{20,28},{24,16},{28,20},{1,9},{5... | collective-permute-start | bytes 3379208 | tf_op jit(solution)/shard_map/ppermute | solution.py:695
  387.5 26.7 %collective-permute-start.39 = (bf16[16,176,800]{2,1,0:T(8,128)(2,1)}, bf16[16,176,800]{2,1,0:T(8,128)(2,1)}, u32[]{:S(2)}, u32[]{:S(2)}) collective-permute-start(bf16[16,176,800]{2,1,0:T(8,128)(2,1)} %get-tuple-element.284), channel_id=1, source_target_pairs={{0,4},{4,0},{8,12},{12,8},{16,20},{20,16},{24,28},{28,24},{1,5},{5... | collective-permute-start | bytes 13516808 | tf_op jit(solution)/shard_map/ppermute | solution.py:695
  392.0 20.0 %collective-permute-start.38 = (bf16[1,2,176,800]{3,2,1,0:T(8,128)(2,1)}, bf16[1,2,176,800]{3,2,1,0:T(8,128)(2,1)}, u32[]{:S(2)}, u32[]{:S(2)}) collective-permute-start(bf16[1,2,176,800]{3,2,1,0:T(8,128)(2,1)} %get-tuple-element.282), channel_id=1, source_target_pairs={{0,16},{4,20},{8,24},{12,28},{16,0},{20,4},{24,8},{28,12},{1,17},{... | collective-permute-start | bytes 1689608 | tf_op jit(solution)/shard_map/ppermute | solution.py:695
  393.3 16.6 %collective-permute-start.37 = (bf16[1,2,176,800]{3,2,1,0:T(8,128)(2,1)}, bf16[1,2,176,800]{3,2,1,0:T(8,128)(2,1)}, u32[]{:S(2)}, u32[]{:S(2)}) collective-permute-start(bf16[1,2,176,800]{3,2,1,0:T(8,128)(2,1)} %get-tuple-element.281), channel_id=1, source_target_pairs={{0,8},{4,12},{8,0},{12,4},{16,24},{20,28},{24,16},{28,20},{1,9},{5... | collective-permute-start | bytes 1689608 | tf_op jit(solution)/shard_map/ppermute | solution.py:695
  418.7 40.8 %collective-permute-start.43 = (bf16[2,2,176,800]{3,2,1,0:T(8,128)(2,1)}, bf16[2,2,176,800]{3,2,1,0:T(8,128)(2,1)}, u32[]{:S(2)}, u32[]{:S(2)}) collective-permute-start(bf16[2,2,176,800]{3,2,1,0:T(8,128)(2,1)} %bitcast.62), channel_id=1, source_target_pairs={{0,16},{4,20},{8,24},{12,28},{16,0},{20,4},{24,8},{28,12},{1,17},{... | collective-permute-start | bytes 3379208 | tf_op jit(solution)/shard_map/ppermute | solution.py:695
  419.4 40.0 %collective-permute-start.44 = (bf16[2,2,176,800]{3,2,1,0:T(8,128)(2,1)}, bf16[2,2,176,800]{3,2,1,0:T(8,128)(2,1)}, u32[]{:S(2)}, u32[]{:S(2)}) collective-permute-start(bf16[2,2,176,800]{3,2,1,0:T(8,128)(2,1)} %bitcast.63), channel_id=1, source_target_pairs={{0,8},{4,12},{8,0},{12,4},{16,24},{20,28},{24,16},{28,20},{1,9},{5... | collective-permute-start | bytes 3379208 | tf_op jit(solution)/shard_map/ppermute | solution.py:695
  420.0 38.0 %collective-permute-start.40 = (bf16[176,800]{1,0:T(8,128)(2,1)}, bf16[176,800]{1,0:T(8,128)(2,1)S(1)}, u32[]{:S(2)}, u32[]{:S(2)}) collective-permute-start(bf16[176,800]{1,0:T(8,128)(2,1)} %fusion.22), channel_id=1, source_target_pairs={{0,1},{1,0},{2,3},{3,2},{4,5},{5,4},{6,7},{7,6},{8,9},{9,8},{10,11... | collective-permute-start | bytes 844808 | tf_op jit(solution)/shard_map/ppermute | solution.py:695
  428.4 29.7 %collective-permute-start.41 = (bf16[176,800]{1,0:T(8,128)(2,1)}, bf16[176,800]{1,0:T(8,128)(2,1)S(1)}, u32[]{:S(2)}, u32[]{:S(2)}) collective-permute-start(bf16[176,800]{1,0:T(8,128)(2,1)} %get-tuple-element.291), channel_id=1, source_target_pairs={{0,2},{1,3},{2,0},{3,1},{4,6},{5,7},{6,4},{7,5},{8,10},{9,11},{10,... | collective-permute-start | bytes 844808 | tf_op jit(solution)/shard_map/ppermute | solution.py:695
  429.4 28.7 %collective-permute-start.42 = (bf16[176,800]{1,0:T(8,128)(2,1)}, bf16[176,800]{1,0:T(8,128)(2,1)S(1)}, u32[]{:S(2)}, u32[]{:S(2)}) collective-permute-start(bf16[176,800]{1,0:T(8,128)(2,1)} %get-tuple-element.292), channel_id=1, source_target_pairs={{0,3},{1,2},{2,1},{3,0},{4,7},{5,6},{6,5},{7,4},{8,11},{9,10},{10,... | collective-permute-start | bytes 844808 | tf_op jit(solution)/shard_map/ppermute | solution.py:695
  463.0 30.7 %collective-permute-start.48 = (bf16[16,56,800]{2,1,0:T(8,128)(2,1)}, bf16[16,56,800]{2,1,0:T(8,128)(2,1)}, u32[]{:S(2)}, u32[]{:S(2)}) collective-permute-start(bf16[16,56,800]{2,1,0:T(8,128)(2,1)} %get-tuple-element.304), channel_id=1, source_target_pairs={{0,4},{4,0},{8,12},{12,8},{16,20},{20,16},{24,28},{28,24},{1,5},{5... | collective-permute-start | bytes 4300808 | tf_op jit(solution)/shard_map/ppermute | solution.py:695
  464.4 24.8 %collective-permute-start.46 = (bf16[1,2,176,800]{3,2,1,0:T(8,128)(2,1)}, bf16[1,2,176,800]{3,2,1,0:T(8,128)(2,1)}, u32[]{:S(2)}, u32[]{:S(2)}) collective-permute-start(bf16[1,2,176,800]{3,2,1,0:T(8,128)(2,1)} %get-tuple-element.301), channel_id=1, source_target_pairs={{0,8},{4,12},{8,0},{12,4},{16,24},{20,28},{24,16},{28,20},{1,9},{5... | collective-permute-start | bytes 1689608 | tf_op jit(solution)/shard_map/ppermute | solution.py:695
  466.7 21.4 %collective-permute-start.45 = (bf16[1,176,800]{2,1,0:T(8,128)(2,1)S(1)}, bf16[1,176,800]{2,1,0:T(8,128)(2,1)}, u32[]{:S(2)}, u32[]{:S(2)}) collective-permute-start(bf16[1,176,800]{2,1,0:T(8,128)(2,1)S(1)} %fusion.28), channel_id=1, source_target_pairs={{0,8},{4,12},{8,0},{12,4},{16,24},{20,28},{24,16},{28,20},{1,9},{5... | collective-permute-start | bytes 844808 | tf_op jit(solution)/shard_map/ppermute | solution.py:695
  467.7 23.5 %collective-permute-start.47 = (bf16[1,2,176,800]{3,2,1,0:T(8,128)(2,1)}, bf16[1,2,176,800]{3,2,1,0:T(8,128)(2,1)}, u32[]{:S(2)}, u32[]{:S(2)}) collective-permute-start(bf16[1,2,176,800]{3,2,1,0:T(8,128)(2,1)} %get-tuple-element.302), channel_id=1, source_target_pairs={{0,16},{4,20},{8,24},{12,28},{16,0},{20,4},{24,8},{28,12},{1,17},{... | collective-permute-start | bytes 1689608 | tf_op jit(solution)/shard_map/ppermute | solution.py:695
  495.9 30.5 %collective-permute-start.53 = (bf16[2,2,56,800]{3,2,1,0:T(8,128)(2,1)}, bf16[2,2,56,800]{3,2,1,0:T(8,128)(2,1)}, u32[]{:S(2)}, u32[]{:S(2)}) collective-permute-start(bf16[2,2,56,800]{3,2,1,0:T(8,128)(2,1)} %bitcast.75), channel_id=1, source_target_pairs={{0,16},{4,20},{8,24},{12,28},{16,0},{20,4},{24,8},{28,12},{1,17},{... | collective-permute-start | bytes 1075208 | tf_op jit(solution)/shard_map/ppermute | solution.py:695
  497.2 29.2 %collective-permute-start.54 = (bf16[2,2,56,800]{3,2,1,0:T(8,128)(2,1)}, bf16[2,2,56,800]{3,2,1,0:T(8,128)(2,1)}, u32[]{:S(2)}, u32[]{:S(2)}) collective-permute-start(bf16[2,2,56,800]{3,2,1,0:T(8,128)(2,1)} %bitcast.76), channel_id=1, source_target_pairs={{0,8},{4,12},{8,0},{12,4},{16,24},{20,28},{24,16},{28,20},{1,9},{5... | collective-permute-start | bytes 1075208 | tf_op jit(solution)/shard_map/ppermute | solution.py:695
  498.6 18.9 %collective-permute-start.50 = (bf16[176,800]{1,0:T(8,128)(2,1)}, bf16[176,800]{1,0:T(8,128)(2,1)S(1)}, u32[]{:S(2)}, u32[]{:S(2)}) collective-permute-start(bf16[176,800]{1,0:T(8,128)(2,1)} %fusion.25), channel_id=1, source_target_pairs={{0,1},{1,0},{2,3},{3,2},{4,5},{5,4},{6,7},{7,6},{8,9},{9,8},{10,11... | collective-permute-start | bytes 844808 | tf_op jit(solution)/shard_map/ppermute | solution.py:695
  499.6 25.1 %collective-permute-start.51 = (bf16[176,800]{1,0:T(8,128)(2,1)}, bf16[176,800]{1,0:T(8,128)(2,1)}, u32[]{:S(2)}, u32[]{:S(2)}) collective-permute-start(bf16[176,800]{1,0:T(8,128)(2,1)} %get-tuple-element.310), channel_id=1, source_target_pairs={{0,2},{1,3},{2,0},{3,1},{4,6},{5,7},{6,4},{7,5},{8,10},{9,11},{10,... | collective-permute-start | bytes 844808 | tf_op jit(solution)/shard_map/ppermute | solution.py:695
  501.5 23.2 %collective-permute-start.52 = (bf16[176,800]{1,0:T(8,128)(2,1)}, bf16[176,800]{1,0:T(8,128)(2,1)}, u32[]{:S(2)}, u32[]{:S(2)}) collective-permute-start(bf16[176,800]{1,0:T(8,128)(2,1)} %get-tuple-element.311), channel_id=1, source_target_pairs={{0,3},{1,2},{2,1},{3,0},{4,7},{5,6},{6,5},{7,4},{8,11},{9,10},{10,... | collective-permute-start | bytes 844808 | tf_op jit(solution)/shard_map/ppermute | solution.py:695
  517.5 14.5 %collective-permute-start.49 = (bf16[2,176,800]{2,1,0:T(8,128)(2,1)S(1)}, bf16[2,176,800]{2,1,0:T(8,128)(2,1)}, u32[]{:S(2)}, u32[]{:S(2)}) collective-permute-start(bf16[2,176,800]{2,1,0:T(8,128)(2,1)S(1)} %pad_maximum_fusion.9), channel_id=1, source_target_pairs={{0,16},{4,20},{8,24},{12,28},{16,0},{20,4},{24,8},{28,12},{1,17},{... | collective-permute-start | bytes 1689608 | tf_op jit(solution)/shard_map/ppermute | solution.py:695
  533.3 10.9 %collective-permute-start.58 = (f32[18,1600]{1,0:T(8,128)S(1)}, f32[18,1600]{1,0:T(8,128)S(1)}, u32[]{:S(2)}, u32[]{:S(2)}) collective-permute-start(f32[18,1600]{1,0:T(8,128)S(1)} %concatenate.66), channel_id=1, source_target_pairs={{0,4},{4,0},{8,12},{12,8},{16,20},{20,16},{24,28},{28,24},{1,5},{5... | collective-permute-start | bytes 345608 | tf_op jit(solution)/shard_map/ppermute | solution.py:695
  533.4 11.9 %collective-permute-start.57 = (bf16[1,2,56,800]{3,2,1,0:T(8,128)(2,1)S(1)}, bf16[1,2,56,800]{3,2,1,0:T(8,128)(2,1)S(1)}, u32[]{:S(2)}, u32[]{:S(2)}) collective-permute-start(bf16[1,2,56,800]{3,2,1,0:T(8,128)(2,1)S(1)} %get-tuple-element.327), channel_id=1, source_target_pairs={{0,16},{4,20},{8,24},{12,28},{16,0},{20,4},{24,8},{28,12},{1,17},{... | collective-permute-start | bytes 537608 | tf_op jit(solution)/shard_map/ppermute | solution.py:695
  534.0 10.2 %collective-permute-start.56 = (bf16[1,2,56,800]{3,2,1,0:T(8,128)(2,1)}, bf16[1,2,56,800]{3,2,1,0:T(8,128)(2,1)S(1)}, u32[]{:S(2)}, u32[]{:S(2)}) collective-permute-start(bf16[1,2,56,800]{3,2,1,0:T(8,128)(2,1)} %get-tuple-element.326), channel_id=1, source_target_pairs={{0,8},{4,12},{8,0},{12,4},{16,24},{20,28},{24,16},{28,20},{1,9},{5... | collective-permute-start | bytes 537608 | tf_op jit(solution)/shard_map/ppermute | solution.py:695
  534.8 13.2 %collective-permute-start.55 = (bf16[1,176,800]{2,1,0:T(8,128)(2,1)S(1)}, bf16[1,176,800]{2,1,0:T(8,128)(2,1)S(1)}, u32[]{:S(2)}, u32[]{:S(2)}) collective-permute-start(bf16[1,176,800]{2,1,0:T(8,128)(2,1)S(1)} %fusion.29), channel_id=1, source_target_pairs={{0,8},{4,12},{8,0},{12,4},{16,24},{20,28},{24,16},{28,20},{1,9},{5... | collective-permute-start | bytes 844808 | tf_op jit(solution)/shard_map/ppermute | solution.py:695
  536.0 33.0 %collective-permute-start.59 = (bf16[4,176,800]{2,1,0:T(8,128)(2,1)S(1)}, bf16[4,176,800]{2,1,0:T(8,128)(2,1)}, u32[]{:S(2)}, u32[]{:S(2)}) collective-permute-start(bf16[4,176,800]{2,1,0:T(8,128)(2,1)S(1)} %pad_maximum_fusion.2.refs_1_), channel_id=1, source_target_pairs={{0,4},{4,0},{8,12},{12,8},{16,20},{20,16},{24,28},{28,24},{1,5},{5... | collective-permute-start | bytes 3379208 | tf_op jit(solution)/shard_map/ppermute | solution.py:695
  548.1 19.7 %collective-permute-start.60 = (bf16[2,176,800]{2,1,0:T(8,128)(2,1)S(1)}, bf16[2,176,800]{2,1,0:T(8,128)(2,1)}, u32[]{:S(2)}, u32[]{:S(2)}) collective-permute-start(bf16[2,176,800]{2,1,0:T(8,128)(2,1)S(1)} %pad_maximum_fusion.10), channel_id=1, source_target_pairs={{0,16},{4,20},{8,24},{12,28},{16,0},{20,4},{24,8},{28,12},{1,17},{... | collective-permute-start | bytes 1689608 | tf_op jit(solution)/shard_map/ppermute | solution.py:695
  549.7 12.8 %collective-permute-start.61 = (bf16[56,800]{1,0:T(8,128)(2,1)S(1)}, bf16[56,800]{1,0:T(8,128)(2,1)S(1)}, u32[]{:S(2)}, u32[]{:S(2)}) collective-permute-start(bf16[56,800]{1,0:T(8,128)(2,1)S(1)} %fusion.38), channel_id=1, source_target_pairs={{0,1},{1,0},{2,3},{3,2},{4,5},{5,4},{6,7},{7,6},{8,9},{9,8},{10,11... | collective-permute-start | bytes 268808 | tf_op jit(solution)/shard_map/ppermute | solution.py:695
  551.3 11.8 %collective-permute-start.62 = (bf16[56,800]{1,0:T(8,128)(2,1)S(1)}, bf16[56,800]{1,0:T(8,128)(2,1)S(1)}, u32[]{:S(2)}, u32[]{:S(2)}) collective-permute-start(bf16[56,800]{1,0:T(8,128)(2,1)S(1)} %get-tuple-element.337), channel_id=1, source_target_pairs={{0,2},{1,3},{2,0},{3,1},{4,6},{5,7},{6,4},{7,5},{8,10},{9,11},{10,... | collective-permute-start | bytes 268808 | tf_op jit(solution)/shard_map/ppermute | solution.py:695
  552.6 10.5 %collective-permute-start.63 = (bf16[56,800]{1,0:T(8,128)(2,1)S(1)}, bf16[56,800]{1,0:T(8,128)(2,1)S(1)}, u32[]{:S(2)}, u32[]{:S(2)}) collective-permute-start(bf16[56,800]{1,0:T(8,128)(2,1)S(1)} %get-tuple-element.338), channel_id=1, source_target_pairs={{0,3},{1,2},{2,1},{3,0},{4,7},{5,6},{6,5},{7,4},{8,11},{9,10},{10,... | collective-permute-start | bytes 268808 | tf_op jit(solution)/shard_map/ppermute | solution.py:695
  574.1 6.9 %collective-permute-start.65 = (bf16[4,176,800]{2,1,0:T(8,128)(2,1)S(1)}, bf16[4,176,800]{2,1,0:T(8,128)(2,1)S(1)}, u32[]{:S(2)}, u32[]{:S(2)}) collective-permute-start(bf16[4,176,800]{2,1,0:T(8,128)(2,1)S(1)} %pad_maximum_fusion.3.refs_1_), channel_id=1, source_target_pairs={{0,4},{4,0},{8,12},{12,8},{16,20},{20,16},{24,28},{28,24},{1,5},{5... | collective-permute-start | bytes 3379208 | tf_op jit(solution)/shard_map/ppermute | solution.py:695
  586.7 6.3 %collective-permute-start.68 = (bf16[2,56,800]{2,1,0:T(8,128)(2,1)S(1)}, bf16[2,56,800]{2,1,0:T(8,128)(2,1)S(1)}, u32[]{:S(2)}, u32[]{:S(2)}) collective-permute-start(bf16[2,56,800]{2,1,0:T(8,128)(2,1)S(1)} %pad_maximum_fusion.15), channel_id=1, source_target_pairs={{0,16},{4,20},{8,24},{12,28},{16,0},{20,4},{24,8},{28,12},{1,17},{... | collective-permute-start | bytes 537608 | tf_op jit(solution)/shard_map/ppermute | solution.py:695
  593.1 8.9 %collective-permute-start.71 = (f32[18,1600]{1,0:T(8,128)S(1)}, f32[18,1600]{1,0:T(8,128)S(1)}, u32[]{:S(2)}, u32[]{:S(2)}) collective-permute-start(f32[18,1600]{1,0:T(8,128)S(1)} %add.567), channel_id=1, source_target_pairs={{0,2},{1,3},{2,0},{3,1},{4,6},{5,7},{6,4},{7,5},{8,10},{9,11},{10,... | collective-permute-start | bytes 345608 | tf_op jit(solution)/shard_map/ppermute | solution.py:695
  594.9 11.0 %collective-permute-start.70 = (bf16[4,56,800]{2,1,0:T(8,128)(2,1)S(1)}, bf16[4,56,800]{2,1,0:T(8,128)(2,1)S(1)}, u32[]{:S(2)}, u32[]{:S(2)}) collective-permute-start(bf16[4,56,800]{2,1,0:T(8,128)(2,1)S(1)} %pad_maximum_fusion.13.refs_1_), channel_id=1, source_target_pairs={{0,4},{4,0},{8,12},{12,8},{16,20},{20,16},{24,28},{28,24},{1,5},{5... | collective-permute-start | bytes 1075208 | tf_op jit(solution)/shard_map/ppermute | solution.py:695
  (48 other events, 333.1 us)

commit v4 on v3

--- a/solution.py
+++ b/solution.py
@@ -826,6 +826,8 @@
 
 
 def add_low(*blocks):
+    if len(blocks) == 2:
+        return blocks[0] + blocks[1]
     total = blocks[0].astype(F32)
     for block in blocks[1:]:
         total = total + block.astype(F32)

time: 618 us -> 618 us (level)
    convert_element_type x6 -> x3, other arithmetic: 21 us -> 9.77 us  [add_low(): return total.astype(BF16)]
    add x0 -> x3, other arithmetic: none -> 10.4 us  [add_low(): return blocks[0] + blocks[1]]
where the time goes in v4:
time: 618 us; the launch traced here: 609 us
  Pallas kernels  325 us (53%)
  waiting for transfers between devices  101 us (16%)
  starting transfers between devices  96.3 us (16%)
  other arithmetic  53.2 us (9%)
  local copies, waits for them, and re-layouts  31.2 us (5%)
    pallas_call x14, Pallas kernels, call(): pl.pallas_call(kernel, grid=(steps,), in_specs=in_specs, out_specs=[stepp...  313 us
    ppermute x66, waiting for transfers between devices, exchanged(): lax.ppermute(block, axis, [(i, i ^ bit) for i in range(lax.axis_size(axis...  97.4 us
    ppermute x66, starting transfers between devices, exchanged(): lax.ppermute(block, axis, [(i, i ^ bit) for i in range(lax.axis_size(axis...  86.7 us
  transfers between devices with their start and end apart: 72, of which 24 were waited for; matrix products, arithmetic and copies ran while one was open for 10% of the time, Pallas kernels for 38%

profile of v4, /device:TPU:0, one launch (start us, length us, event | category | flops | bytes accessed | tf_op | source)
XLA Modules:
  0.0 608.9 jit_solution(5023628527188207897)
XLA Ops:
  4.8 3.0 collective-permute-start.3
  7.8 2.6 collective-permute-start.4
  12.8 2.0 collective-permute-start.1
  14.8 2.0 collective-permute-start.2
  19.6 24.7 %collective-permute-done.4 = bf16[15,8,800]{2,1,0:T(8,128)(2,1)} collective-permute-done((bf16[15,8,800]{2,1,0:T(8,128)(2,1)}, bf16[15,8,800]{2,1,0:T(8,128)(2,1)}, u32[]{:S(2)}, u32[]{:S(2)}) %collective-permute-start.4) | collective-permute-done | bytes 192032 | tf_op jit(solution)/shard_map/ppermute | solution.py:695
  50.3 7.4 %collective-permute-done.1 = bf16[29,8,800]{2,1,0:T(8,128)(2,1)S(1)} collective-permute-done((bf16[29,8,800]{2,1,0:T(8,128)(2,1)S(1)}, bf16[29,8,800]{2,1,0:T(8,128)(2,1)S(1)}, u32[]{:S(2)}, u32[]{:S(2)}) %collective-permute-start.1) | collective-permute-done | bytes 371232 | tf_op jit(solution)/shard_map/ppermute | solution.py:695
  62.2 10.8 %collective-permute-start.11 = (bf16[16,8,800]{2,1,0:T(8,128)(2,1)S(1)}, bf16[16,8,800]{2,1,0:T(8,128)(2,1)S(1)}, u32[]{:S(2)}, u32[]{:S(2)}) collective-permute-start(bf16[16,8,800]{2,1,0:T(8,128)(2,1)S(1)} %fusion.32), channel_id=1, source_target_pairs={{0,1},{1,0},{2,3},{3,2},{4,5},{5,4},{6,7},{7,6},{8,9},{9,8},{10,11... | collective-permute-start | bytes 614408 | tf_op jit(solution)/shard_map/ppermute | solution.py:695
  74.7 2.1 collective-permute-done.10
  78.0 1.6 pad_maximum_fusion
  79.7 2.7 collective-permute-done.12
  85.3 2.5 collective-permute-start.13
  87.8 18.8 %shard_map.315 = (bf16[4,480,1600]{2,1,0:T(8,128)(2,1)}, f32[4,480,800]{2,1,0:T(8,128)}, bf16[4,480,800]{2,1,0:T(8,128)(2,1)}, bf16[1600,800]{1,0:T(8,128)(2,1)}) custom-call(s32[3]{0:T(128)} %pad_add_fusion.2.refs_0_, bf16[4,480,1600]{2,1,0:T(8,128)(2,1)} %bitcast.181, bf16[4,120,800]{2,1,0:T(8,128)(2,1)} %bitcast.17.refs_2_, ...), custom_call_target="tpu_custom_call" | custom-call | flops 4915200000 | bytes 27174400 | tf_op jit(solution)/shard_map/pallas_call | solution.py:654
  107.6 7.6 %collective-permute-done.14 = bf16[4,29,8,800]{3,2,1,0:T(8,128)(2,1)} collective-permute-done((bf16[4,29,8,800]{3,2,1,0:T(8,128)(2,1)S(1)}, bf16[4,29,8,800]{3,2,1,0:T(8,128)(2,1)}, u32[]{:S(2)}, u32[]{:S(2)}) %collective-permute-start.14) | collective-permute-done | bytes 1484832 | tf_op jit(solution)/shard_map/ppermute | solution.py:695
  115.2 6.7 %collective-permute-done.16 = bf16[4,29,8,800]{3,2,1,0:T(8,128)(2,1)} collective-permute-done((bf16[4,29,8,800]{3,2,1,0:T(8,128)(2,1)}, bf16[4,29,8,800]{3,2,1,0:T(8,128)(2,1)}, u32[]{:S(2)}, u32[]{:S(2)}) %collective-permute-start.16) | collective-permute-done | bytes 1484832 | tf_op jit(solution)/shard_map/ppermute | solution.py:695
  122.6 1.9 collective-permute-start.18
  126.9 3.8 collective-permute-start.22
  131.9 39.1 %shard_map.316 = (f32[4,480,800]{2,1,0:T(8,128)}, bf16[4,480,800]{2,1,0:T(8,128)(2,1)}, f32[4,480,1600]{2,1,0:T(8,128)}, bf16[800,1600]{1,0:T(8,128)(2,1)}, bf16...) custom-call(s32[3]{0:T(128)} %pad_add_fusion.2.refs_0_, bf16[4,480,800]{2,1,0:T(8,128)(2,1)} %get-tuple-element.207.refs_1_.refs_5_, ...), custom_call_target="tpu_custom_call" | custom-call | flops 17203200000 | bytes 54380800 | tf_op jit(solution)/shard_map/pallas_call | solution.py:654
  173.9 17.2 %shard_map.317 = (bf16[4,480,1600]{2,1,0:T(8,128)(2,1)}, f32[4,480,800]{2,1,0:T(8,128)}, bf16[4,480,800]{2,1,0:T(8,128)(2,1)}) custom-call(f32[4,480,1600]{2,1,0:T(8,128)} %get-tuple-element.229.refs_0_.refs_1_, f32[3,1600]{1,0:T(4,128)} %get-tuple-element.329.refs_1_.refs_6_.refs_3_, f32[6,800]{1,0:T(8,128)} %get-tuple-element.237.refs_2_.refs_13_.refs_8_, ...), custom_call_target="tpu_custom_call" | custom-call | flops 4915200000 | bytes 30246400 | tf_op jit(solution)/shard_map/pallas_call | solution.py:654
  192.0 1.9 collective-permute-done.24
  193.9 2.3 collective-permute-done.26
  196.7 1.9 collective-permute-start.28
  201.3 42.0 %shard_map.318 = (bf16[4,480,800]{2,1,0:T(8,128)(2,1)}, bf16[4,480,800]{2,1,0:T(8,128)(2,1)}, bf16[800,1600]{1,0:T(8,128)(2,1)}, bf16[800,2400]{1,0:T(8,128)(2,1...) custom-call(s32[3]{0:T(128)} %pad_add_fusion.2.refs_0_, ...), custom_call_target="tpu_custom_call" | custom-call | flops 17203200000 | bytes 31237120 | tf_op jit(solution)/shard_map/pallas_call | solution.py:654
  246.6 3.3 collective-permute-done.31.refs_2_
  250.6 41.8 %shard_map.319 = (bf16[4,480,800]{2,1,0:T(8,128)(2,1)}, bf16[16,176,800]{2,1,0:T(8,128)(2,1)}, bf16[16,176,800]{2,1,0:T(8,128)(2,1)}, f32[3,8,800]{2,1,0:T(8,128)}) custom-call(s32[3]{0:T(128)} %pad_add_fusion.2.refs_0_, bf16[4,480,800]{2,1,0:T(8,128)(2,1)} %get-tuple-element.257.refs_1_, bf16[4,32,800]{2,1,0:T(8,128)(2,1)} %copy-done.35, ...), custom_call_target="tpu_custom_call" | custom-call | flops 19660800000 | bytes 37227520 | tf_op jit(solution)/shard_map/pallas_call | solution.py:654
  292.4 5.3 collective-permute-start.34
  298.9 43.5 %shard_map.320 = (f32[4,480,1600]{2,1,0:T(8,128)}, bf16[4,480,800]{2,1,0:T(8,128)(2,1)}, bf16[800,1600]{1,0:T(8,128)(2,1)}, f32[3,8,1600]{2,1,0:T(8,128)}, f32[3,8,800]{2,1,0:T(8,128)}) custom-call(bf16[4,480,800]{2,1,0:T(8,128)(2,1)} %get-tuple-element.264.refs_0_, f32[4,480,1600]{2,1,0:T(8,128)} %get-tuple-element.229.refs_0_.refs_1_, ...), custom_call_target="tpu_custom_call" | custom-call | flops 14745600000 | bytes 54028800 | tf_op jit(solution)/shard_map/pallas_call | solution.py:654
  343.5 1.9 collective-permute-start.32
  346.7 4.2 slice_add_fusion.2
  350.9 3.8 collective-permute-start.35
  356.2 24.8 %shard_map.321 = (bf16[16,176,800]{2,1,0:T(8,128)(2,1)}, bf16[16,176,800]{2,1,0:T(8,128)(2,1)}) custom-call(s32[3]{0:T(128)} %pad_add_fusion.2.refs_0_, bf16[4,480,800]{2,1,0:T(8,128)(2,1)} %get-tuple-element.268.refs_1_.refs_0_, bf16[4,16,800]{2,1,0:T(8,128)(2,1)} %copy-done.36, bf16[4,16,800]{2,1,0:T(8,128)(2,1)} %copy-done.37, ...), custom_call_target="tpu_custom_call" | custom-call | flops 12288000000 | bytes 17939200 | tf_op jit(solution)/shard_map/pallas_call | solution.py:654
  381.0 2.1 collective-permute-done.35
  383.1 4.1 fusion.2
  393.4 15.1 %shard_map.322 = (bf16[4,480,800]{2,1,0:T(8,128)(2,1)}, f32[3,8,800]{2,1,0:T(8,128)}) custom-call(bf16[4,480,800]{2,1,0:T(8,128)(2,1)} %get-tuple-element.268.refs_1_.refs_0_, bf16[4,16,800]{2,1,0:T(8,128)(2,1)} %copy-done.36, bf16[4,16,800]{2,1,0:T(8,128)(2,1)} %copy-done.37, bf16[4,480,5]{2,1,0:T(8,128)(2,1)} %convert_element_type.392.refs_4_.refs_3_, ...), custom_call_target="tpu_custom_call" | custom-call | flops 6144000000 | bytes 19008000 | tf_op jit(solution)/shard_map/pallas_call | solution.py:654
  409.6 2.0 fusion.22
  411.6 2.2 fusion.24
  413.8 4.2 slice_add_fusion
  419.4 8.3 %collective-permute-start.40 = (bf16[176,800]{1,0:T(8,128)(2,1)}, bf16[176,800]{1,0:T(8,128)(2,1)S(1)}, u32[]{:S(2)}, u32[]{:S(2)}) collective-permute-start(bf16[176,800]{1,0:T(8,128)(2,1)} %fusion.22), channel_id=1, source_target_pairs={{0,1},{1,0},{2,3},{3,2},{4,5},{5,4},{6,7},{7,6},{8,9},{9,8},{10,11... | collective-permute-start | bytes 844808 | tf_op jit(solution)/shard_map/ppermute | solution.py:695
  430.2 15.0 %shard_map.323 = (bf16[4,480,800]{2,1,0:T(8,128)(2,1)}, f32[3,8,800]{2,1,0:T(8,128)}) custom-call(bf16[4,480,800]{2,1,0:T(8,128)(2,1)} %get-tuple-element.268.refs_1_.refs_0_, bf16[4,16,800]{2,1,0:T(8,128)(2,1)} %copy-done.36, bf16[4,16,800]{2,1,0:T(8,128)(2,1)} %copy-done.37, ...), custom_call_target="tpu_custom_call", output_to_operand_aliasing={{0}: (7, {})} | custom-call | flops 6144000000 | bytes 19008000 | tf_op jit(solution)/shard_map/pallas_call | solution.py:654
  445.1 12.3 %shard_map.324 = (bf16[16,56,800]{2,1,0:T(8,128)(2,1)}, bf16[16,56,800]{2,1,0:T(8,128)(2,1)}) custom-call(s32[3]{0:T(128)} %pad_add_fusion.2.refs_0_, bf16[4,480,1600]{2,1,0:T(8,128)(2,1)} %get-tuple-element.295.refs_1_, bf16[4,480,800]{2,1,0:T(8,128)(2,1)} %get-tuple-element.287.refs_2_.refs_0_), custom_call_target="tpu_custom_call" | custom-call | flops 4915200000 | bytes 12083200 | tf_op jit(solution)/shard_map/pallas_call | solution.py:654
  458.8 3.5 fusion
  468.4 13.4 %shard_map.325 = (bf16[4,480,1600]{2,1,0:T(8,128)(2,1)}, f32[2,8,1600]{2,1,0:T(8,128)}) custom-call(bf16[4,480,800]{2,1,0:T(8,128)(2,1)} %get-tuple-element.287.refs_2_.refs_0_, bf16[4,480,1600]{2,1,0:T(8,128)(2,1)} %bitcast.183, f32[4,480,1600]{2,1,0:T(8,128)} %get-tuple-element.288.refs_2_, bf16[1600,800]{1,0:T(8,128)(2,1)} %get-tuple-element.289.refs_3_, ...), custom_call_target="tpu_custom_call" | custom-call | flops 2457600000 | bytes 30329600 | tf_op jit(solution)/shard_map/pallas_call | solution.py:654
  481.8 5.6 collective-permute-done.45
  488.5 1.9 fusion.25
  490.5 2.5 fusion.27
  493.0 2.1 slice_add_fusion.4
  498.9 1.9 collective-permute-start.51
  503.3 13.5 %shard_map.326 = (bf16[4,480,1600]{2,1,0:T(8,128)(2,1)}, f32[2,8,1600]{2,1,0:T(8,128)}) custom-call(bf16[4,480,800]{2,1,0:T(8,128)(2,1)} %get-tuple-element.287.refs_2_.refs_0_, bf16[4,480,1600]{2,1,0:T(8,128)(2,1)} %bitcast.184, f32[4,480,1600]{2,1,0:T(8,128)} %get-tuple-element.288.refs_2_, ...), custom_call_target="tpu_custom_call", output_to_operand_aliasing={{0}: (5, {})} | custom-call | flops 2457600000 | bytes 30329600 | tf_op jit(solution)/shard_map/pallas_call | solution.py:654
  518.7 5.3 collective-permute-done.51
  524.0 1.6 fusion.29
  525.6 2.2 fusion.20
  527.8 3.5 collective-permute-done.49
  535.3 8.1 %shard_map.327.refs_4_ = bf16[4,480,1600]{2,1,0:T(8,128)(2,1)} custom-call(bf16[4,480,800]{2,1,0:T(8,128)(2,1)} %get-tuple-element.255.refs_0_, f32[4,480,1600]{2,1,0:T(8,128)} %get-tuple-element.229.refs_0_.refs_1_, bf16[800,1600]{1,0:T(8,128)(2,1)} %get-tuple-element.256.refs_2_, f32[3,1600]{1,0:T(4,128)} %get-tuple-element.329.refs_1_.refs_6_.refs_3_), custom_call_target="tpu_custom_call" | custom-call | flops 2457600000 | bytes 24083200 | tf_op jit(solution)/shard_map/pallas_call | solution.py:654
  545.6 1.7 collective-permute-done.55
  548.9 1.7 collective-permute-start.61
  553.3 8.4 %shard_map.328 = bf16[4,480,1600]{2,1,0:T(8,128)(2,1)} custom-call(bf16[4,480,800]{2,1,0:T(8,128)(2,1)} %get-tuple-element.255.refs_0_, f32[4,480,1600]{2,1,0:T(8,128)} %get-tuple-element.229.refs_0_.refs_1_, bf16[800,1600]{1,0:T(8,128)(2,1)} %get-tuple-element.256.refs_2_, ...), custom_call_target="tpu_custom_call", output_to_operand_aliasing={{}: (4, {})} | custom-call | flops 2457600000 | bytes 24083200 | tf_op jit(solution)/shard_map/pallas_call | solution.py:654
  563.4 3.6 collective-permute-done.64
  568.3 5.0 shard_map.329
  574.7 3.9 collective-permute-done.66
  578.6 1.6 collective-permute-done.67
  581.3 4.7 shard_map.330
  587.5 4.5 collective-permute-done.69
  592.4 1.8 collective-permute-start.71
  594.2 7.1 %collective-permute-done.71 = f32[18,1600]{1,0:T(8,128)S(1)} collective-permute-done((f32[18,1600]{1,0:T(8,128)S(1)}, f32[18,1600]{1,0:T(8,128)S(1)}, u32[]{:S(2)}, u32[]{:S(2)}) %collective-permute-start.71) | collective-permute-done | bytes 115232 | tf_op jit(solution)/shard_map/ppermute | solution.py:695
  606.0 2.4 shard_map.331
  (310 shorter events, 96.7 us)
Async XLA Ops:
  4.8 14.3 %collective-permute-start.3 = (bf16[15,8,800]{2,1,0:T(8,128)(2,1)}, bf16[15,8,800]{2,1,0:T(8,128)(2,1)}, u32[]{:S(2)}, u32[]{:S(2)}) collective-permute-start(bf16[15,8,800]{2,1,0:T(8,128)(2,1)} %get-tuple-element.580), channel_id=1, source_target_pairs={{0,1},{1,0},{2,3},{3,2},{4,5},{5,4},{6,7},{7,6},{8,9},{9,8},{10,11... | collective-permute-start | bytes 576008 | tf_op jit(solution)/shard_map/ppermute | solution.py:695
  7.8 36.5 %collective-permute-start.4 = (bf16[15,8,800]{2,1,0:T(8,128)(2,1)}, bf16[15,8,800]{2,1,0:T(8,128)(2,1)}, u32[]{:S(2)}, u32[]{:S(2)}) collective-permute-start(bf16[15,8,800]{2,1,0:T(8,128)(2,1)} %get-tuple-element.580), channel_id=1, source_target_pairs={{0,2},{1,3},{2,0},{3,1},{4,6},{5,7},{6,4},{7,5},{8,10},{9,11},{10,... | collective-permute-start | bytes 576008 | tf_op jit(solution)/shard_map/ppermute | solution.py:695
  10.4 33.9 %collective-permute-start.5 = (bf16[15,8,800]{2,1,0:T(8,128)(2,1)}, bf16[15,8,800]{2,1,0:T(8,128)(2,1)}, u32[]{:S(2)}, u32[]{:S(2)}) collective-permute-start(bf16[15,8,800]{2,1,0:T(8,128)(2,1)} %get-tuple-element.580), channel_id=1, source_target_pairs={{0,3},{1,2},{2,1},{3,0},{4,7},{5,6},{6,5},{7,4},{8,11},{9,10},{10,... | collective-permute-start | bytes 576008 | tf_op jit(solution)/shard_map/ppermute | solution.py:695
  12.8 44.9 %collective-permute-start.1 = (bf16[29,8,800]{2,1,0:T(8,128)(2,1)S(1)}, bf16[29,8,800]{2,1,0:T(8,128)(2,1)S(1)}, u32[]{:S(2)}, u32[]{:S(2)}) collective-permute-start(bf16[29,8,800]{2,1,0:T(8,128)(2,1)S(1)} %bitcast.187), channel_id=1, source_target_pairs={{0,2},{1,3},{2,0},{3,1},{4,6},{5,7},{6,4},{7,5},{8,10},{9,11},{10,... | collective-permute-start | bytes 1113608 | tf_op jit(solution)/shard_map/ppermute | solution.py:695
  14.8 43.0 %collective-permute-start.2 = (bf16[29,8,800]{2,1,0:T(8,128)(2,1)S(1)}, bf16[29,8,800]{2,1,0:T(8,128)(2,1)}, u32[]{:S(2)}, u32[]{:S(2)}) collective-permute-start(bf16[29,8,800]{2,1,0:T(8,128)(2,1)S(1)} %bitcast.188), channel_id=1, source_target_pairs={{0,3},{1,2},{2,1},{3,0},{4,7},{5,6},{6,5},{7,4},{8,11},{9,10},{10,... | collective-permute-start | bytes 1113608 | tf_op jit(solution)/shard_map/ppermute | solution.py:695
  19.1 39.8 %collective-permute-start = (bf16[29,8,800]{2,1,0:T(8,128)(2,1)S(1)}, bf16[29,8,800]{2,1,0:T(8,128)(2,1)S(1)}, u32[]{:S(2)}, u32[]{:S(2)}) collective-permute-start(bf16[29,8,800]{2,1,0:T(8,128)(2,1)S(1)} %bitcast.189), channel_id=1, source_target_pairs={{0,1},{1,0},{2,3},{3,2},{4,5},{5,4},{6,7},{7,6},{8,9},{9,8},{10,11... | collective-permute-start | bytes 1113608 | tf_op jit(solution)/shard_map/ppermute | solution.py:695
  45.7 13.4 %collective-permute-start.6 = (bf16[4,15,8,800]{3,2,1,0:T(8,128)(2,1)S(1)}, bf16[4,15,8,800]{3,2,1,0:T(8,128)(2,1)}, u32[]{:S(2)}, u32[]{:S(2)}) collective-permute-start(bf16[4,15,8,800]{3,2,1,0:T(8,128)(2,1)S(1)} %pad_maximum_fusion.6), channel_id=1, source_target_pairs={{0,8},{4,12},{8,0},{12,4},{16,24},{20,28},{24,16},{28,20},{1,9},{5... | collective-permute-start | bytes 2304008 | tf_op jit(solution)/shard_map/ppermute | solution.py:695
  47.2 11.8 %collective-permute-start.7 = (bf16[4,15,8,800]{3,2,1,0:T(8,128)(2,1)S(1)}, bf16[4,15,8,800]{3,2,1,0:T(8,128)(2,1)}, u32[]{:S(2)}, u32[]{:S(2)}) collective-permute-start(bf16[4,15,8,800]{3,2,1,0:T(8,128)(2,1)S(1)} %pad_maximum_fusion.6), channel_id=1, source_target_pairs={{0,4},{4,0},{8,12},{12,8},{16,20},{20,16},{24,28},{28,24},{1,5},{5... | collective-permute-start | bytes 2304008 | tf_op jit(solution)/shard_map/ppermute | solution.py:695
  59.0 17.8 %collective-permute-start.10 = (bf16[2,29,8,800]{3,2,1,0:T(8,128)(2,1)S(1)}, bf16[2,29,8,800]{3,2,1,0:T(8,128)(2,1)S(1)}, u32[]{:S(2)}, u32[]{:S(2)}) collective-permute-start(bf16[2,29,8,800]{3,2,1,0:T(8,128)(2,1)S(1)} %pad_maximum_fusion.8), channel_id=1, source_target_pairs={{0,8},{4,12},{8,0},{12,4},{16,24},{20,28},{24,16},{28,20},{1,9},{5... | collective-permute-start | bytes 2227208 | tf_op jit(solution)/shard_map/ppermute | solution.py:695
  60.6 17.4 %collective-permute-start.9 = (bf16[2,29,8,800]{3,2,1,0:T(8,128)(2,1)S(1)}, bf16[2,29,8,800]{3,2,1,0:T(8,128)(2,1)S(1)}, u32[]{:S(2)}, u32[]{:S(2)}) collective-permute-start(bf16[2,29,8,800]{3,2,1,0:T(8,128)(2,1)S(1)} %pad_maximum_fusion.7), channel_id=1, source_target_pairs={{0,16},{4,20},{8,24},{12,28},{16,0},{20,4},{24,8},{28,12},{1,17},{... | collective-permute-start | bytes 2227208 | tf_op jit(solution)/shard_map/ppermute | solution.py:695
  62.2 17.4 %collective-permute-start.11 = (bf16[16,8,800]{2,1,0:T(8,128)(2,1)S(1)}, bf16[16,8,800]{2,1,0:T(8,128)(2,1)S(1)}, u32[]{:S(2)}, u32[]{:S(2)}) collective-permute-start(bf16[16,8,800]{2,1,0:T(8,128)(2,1)S(1)} %fusion.32), channel_id=1, source_target_pairs={{0,1},{1,0},{2,3},{3,2},{4,5},{5,4},{6,7},{7,6},{8,9},{9,8},{10,11... | collective-permute-start | bytes 614408 | tf_op jit(solution)/shard_map/ppermute | solution.py:695
  73.0 9.4 %collective-permute-start.12 = (bf16[16,8,800]{2,1,0:T(8,128)(2,1)S(1)}, bf16[16,8,800]{2,1,0:T(8,128)(2,1)S(1)}, u32[]{:S(2)}, u32[]{:S(2)}) collective-permute-start(bf16[16,8,800]{2,1,0:T(8,128)(2,1)S(1)} %fusion.32), channel_id=1, source_target_pairs={{0,2},{1,3},{2,0},{3,1},{4,6},{5,7},{6,4},{7,5},{8,10},{9,11},{10,... | collective-permute-start | bytes 614408 | tf_op jit(solution)/shard_map/ppermute | solution.py:695
  74.7 10.6 %collective-permute-start.8 = (bf16[4,15,8,800]{3,2,1,0:T(8,128)(2,1)}, bf16[4,15,8,800]{3,2,1,0:T(8,128)(2,1)}, u32[]{:S(2)}, u32[]{:S(2)}) collective-permute-start(bf16[4,15,8,800]{3,2,1,0:T(8,128)(2,1)} %collective-permute-done.6), channel_id=1, source_target_pairs={{0,4},{4,0},{8,12},{12,8},{16,20},{20,16},{24,28},{28,24},{1,5},{5... | collective-permute-start | bytes 2304008 | tf_op jit(solution)/shard_map/ppermute | solution.py:695
  82.4 32.9 %collective-permute-start.14 = (bf16[4,29,8,800]{3,2,1,0:T(8,128)(2,1)S(1)}, bf16[4,29,8,800]{3,2,1,0:T(8,128)(2,1)}, u32[]{:S(2)}, u32[]{:S(2)}) collective-permute-start(bf16[4,29,8,800]{3,2,1,0:T(8,128)(2,1)S(1)} %get-tuple-element.224), channel_id=1, source_target_pairs={{0,8},{4,12},{8,0},{12,4},{16,24},{20,28},{24,16},{28,20},{1,9},{5... | collective-permute-start | bytes 4454408 | tf_op jit(solution)/shard_map/ppermute | solution.py:695
  82.9 32.3 %collective-permute-start.15 = (bf16[4,29,8,800]{3,2,1,0:T(8,128)(2,1)S(1)}, bf16[4,29,8,800]{3,2,1,0:T(8,128)(2,1)}, u32[]{:S(2)}, u32[]{:S(2)}) collective-permute-start(bf16[4,29,8,800]{3,2,1,0:T(8,128)(2,1)S(1)} %get-tuple-element.224), channel_id=1, source_target_pairs={{0,4},{4,0},{8,12},{12,8},{16,20},{20,16},{24,28},{28,24},{1,5},{5... | collective-permute-start | bytes 4454408 | tf_op jit(solution)/shard_map/ppermute | solution.py:695
  82.9 39.1 %collective-permute-start.16 = (bf16[4,29,8,800]{3,2,1,0:T(8,128)(2,1)}, bf16[4,29,8,800]{3,2,1,0:T(8,128)(2,1)}, u32[]{:S(2)}, u32[]{:S(2)}) collective-permute-start(bf16[4,29,8,800]{3,2,1,0:T(8,128)(2,1)} %get-tuple-element.227), channel_id=1, source_target_pairs={{0,16},{4,20},{8,24},{12,28},{16,0},{20,4},{24,8},{28,12},{1,17},{... | collective-permute-start | bytes 4454408 | tf_op jit(solution)/shard_map/ppermute | solution.py:695
  83.4 38.6 %collective-permute-start.17 = (bf16[4,29,8,800]{3,2,1,0:T(8,128)(2,1)}, bf16[4,29,8,800]{3,2,1,0:T(8,128)(2,1)}, u32[]{:S(2)}, u32[]{:S(2)}) collective-permute-start(bf16[4,29,8,800]{3,2,1,0:T(8,128)(2,1)} %get-tuple-element.227), channel_id=1, source_target_pairs={{0,4},{4,0},{8,12},{12,8},{16,20},{20,16},{24,28},{28,24},{1,5},{5... | collective-permute-start | bytes 4454408 | tf_op jit(solution)/shard_map/ppermute | solution.py:695
  85.3 22.3 %collective-permute-start.13 = (bf16[16,8,800]{2,1,0:T(8,128)(2,1)S(1)}, bf16[16,8,800]{2,1,0:T(8,128)(2,1)S(1)}, u32[]{:S(2)}, u32[]{:S(2)}) collective-permute-start(bf16[16,8,800]{2,1,0:T(8,128)(2,1)S(1)} %fusion.32), channel_id=1, source_target_pairs={{0,3},{1,2},{2,1},{3,0},{4,7},{5,6},{6,5},{7,4},{8,11},{9,10},{10,... | collective-permute-start | bytes 614408 | tf_op jit(solution)/shard_map/ppermute | solution.py:695
  122.0 9.3 %collective-permute-start.20 = (bf16[4,29,8,800]{3,2,1,0:T(8,128)(2,1)}, bf16[4,29,8,800]{3,2,1,0:T(8,128)(2,1)}, u32[]{:S(2)}, u32[]{:S(2)}) collective-permute-start(bf16[4,29,8,800]{3,2,1,0:T(8,128)(2,1)} %collective-permute-done.14), channel_id=1, source_target_pairs={{0,4},{4,0},{8,12},{12,8},{16,20},{20,16},{24,28},{28,24},{1,5},{5... | collective-permute-start | bytes 4454408 | tf_op jit(solution)/shard_map/ppermute | solution.py:695
  122.0 9.3 %collective-permute-start.21 = (bf16[4,29,8,800]{3,2,1,0:T(8,128)(2,1)}, bf16[4,29,8,800]{3,2,1,0:T(8,128)(2,1)}, u32[]{:S(2)}, u32[]{:S(2)}) collective-permute-start(bf16[4,29,8,800]{3,2,1,0:T(8,128)(2,1)} %collective-permute-done.16), channel_id=1, source_target_pairs={{0,4},{4,0},{8,12},{12,8},{16,20},{20,16},{24,28},{28,24},{1,5},{5... | collective-permute-start | bytes 4454408 | tf_op jit(solution)/shard_map/ppermute | solution.py:695
  122.6 8.1 %collective-permute-start.18 = (bf16[4,16,800]{2,1,0:T(8,128)(2,1)S(1)}, bf16[4,16,800]{2,1,0:T(8,128)(2,1)S(1)}, u32[]{:S(2)}, u32[]{:S(2)}) collective-permute-start(bf16[4,16,800]{2,1,0:T(8,128)(2,1)S(1)} %get-tuple-element.213), channel_id=1, source_target_pairs={{0,4},{4,8},{8,12},{12,16},{16,20},{20,24},{24,28},{1,5},{5,9},{9,... | collective-permute-start | bytes 307208 | tf_op jit(solution)/shard_map/ppermute | solution.py:686
  124.5 6.7 %collective-permute-start.19 = (bf16[4,16,800]{2,1,0:T(8,128)(2,1)S(1)}, bf16[4,16,800]{2,1,0:T(8,128)(2,1)S(1)}, u32[]{:S(2)}, u32[]{:S(2)}) collective-permute-start(bf16[4,16,800]{2,1,0:T(8,128)(2,1)S(1)} %get-tuple-element.214), channel_id=1, source_target_pairs={{4,0},{8,4},{12,8},{16,12},{20,16},{24,20},{28,24},{5,1},{9,5},{13... | collective-permute-start | bytes 307208 | tf_op jit(solution)/shard_map/ppermute | solution.py:691
  126.9 44.1 %collective-permute-start.22 = (bf16[2,16,8,800]{3,2,1,0:T(8,128)(2,1)S(1)}, bf16[2,16,8,800]{3,2,1,0:T(8,128)(2,1)S(1)}, u32[]{:S(2)}, u32[]{:S(2)}) collective-permute-start(bf16[2,16,8,800]{3,2,1,0:T(8,128)(2,1)S(1)} %pad_maximum_fusion.11), channel_id=1, source_target_pairs={{0,16},{4,20},{8,24},{12,28},{16,0},{20,4},{24,8},{28,12},{1,17},{... | collective-permute-start | bytes 1228808 | tf_op jit(solution)/shard_map/ppermute | solution.py:695
  130.7 40.4 %collective-permute-start.23 = (bf16[2,16,8,800]{3,2,1,0:T(8,128)(2,1)S(1)}, bf16[2,16,8,800]{3,2,1,0:T(8,128)(2,1)S(1)}, u32[]{:S(2)}, u32[]{:S(2)}) collective-permute-start(bf16[2,16,8,800]{3,2,1,0:T(8,128)(2,1)S(1)} %pad_maximum_fusion.12), channel_id=1, source_target_pairs={{0,8},{4,12},{8,0},{12,4},{16,24},{20,28},{24,16},{28,20},{1,9},{5... | collective-permute-start | bytes 1228808 | tf_op jit(solution)/shard_map/ppermute | solution.py:695
  171.3 22.6 %collective-permute-start.24 = (bf16[4,16,8,800]{3,2,1,0:T(8,128)(2,1)S(1)}, bf16[4,16,8,800]{3,2,1,0:T(8,128)(2,1)}, u32[]{:S(2)}, u32[]{:S(2)}) collective-permute-start(bf16[4,16,8,800]{3,2,1,0:T(8,128)(2,1)S(1)} %pad_maximum_fusion.4), channel_id=1, source_target_pairs={{0,8},{4,12},{8,0},{12,4},{16,24},{20,28},{24,16},{28,20},{1,9},{5... | collective-permute-start | bytes 2457608 | tf_op jit(solution)/shard_map/ppermute | solution.py:695
  172.8 21.1 %collective-permute-start.25 = (bf16[4,16,8,800]{3,2,1,0:T(8,128)(2,1)S(1)}, bf16[4,16,8,800]{3,2,1,0:T(8,128)(2,1)}, u32[]{:S(2)}, u32[]{:S(2)}) collective-permute-start(bf16[4,16,8,800]{3,2,1,0:T(8,128)(2,1)S(1)} %pad_maximum_fusion.4), channel_id=1, source_target_pairs={{0,4},{4,0},{8,12},{12,8},{16,20},{20,16},{24,28},{28,24},{1,5},{5... | collective-permute-start | bytes 2457608 | tf_op jit(solution)/shard_map/ppermute | solution.py:695
  173.9 22.4 %collective-permute-start.26 = (bf16[4,16,8,800]{3,2,1,0:T(8,128)(2,1)S(1)}, bf16[4,16,8,800]{3,2,1,0:T(8,128)(2,1)}, u32[]{:S(2)}, u32[]{:S(2)}) collective-permute-start(bf16[4,16,8,800]{3,2,1,0:T(8,128)(2,1)S(1)} %pad_maximum_fusion.5), channel_id=1, source_target_pairs={{0,16},{4,20},{8,24},{12,28},{16,0},{20,4},{24,8},{28,12},{1,17},{... | collective-permute-start | bytes 2457608 | tf_op jit(solution)/shard_map/ppermute | solution.py:695
  173.9 22.4 %collective-permute-start.27 = (bf16[4,16,8,800]{3,2,1,0:T(8,128)(2,1)S(1)}, bf16[4,16,8,800]{3,2,1,0:T(8,128)(2,1)}, u32[]{:S(2)}, u32[]{:S(2)}) collective-permute-start(bf16[4,16,8,800]{3,2,1,0:T(8,128)(2,1)S(1)} %pad_maximum_fusion.5), channel_id=1, source_target_pairs={{0,4},{4,0},{8,12},{12,8},{16,20},{20,16},{24,28},{28,24},{1,5},{5... | collective-permute-start | bytes 2457608 | tf_op jit(solution)/shard_map/ppermute | solution.py:695
  292.4 54.4 %collective-permute-start.34 = (bf16[16,176,800]{2,1,0:T(8,128)(2,1)}, bf16[16,176,800]{2,1,0:T(8,128)(2,1)}, u32[]{:S(2)}, u32[]{:S(2)}) collective-permute-start(bf16[16,176,800]{2,1,0:T(8,128)(2,1)} %get-tuple-element.272), channel_id=1, source_target_pairs={{0,4},{4,0},{8,12},{12,8},{16,20},{20,16},{24,28},{28,24},{1,5},{5... | collective-permute-start | bytes 13516808 | tf_op jit(solution)/shard_map/ppermute | solution.py:695
  343.5 11.4 %collective-permute-start.32 = (bf16[4,16,800]{2,1,0:T(8,128)(2,1)S(1)}, bf16[4,16,800]{2,1,0:T(8,128)(2,1)S(1)}, u32[]{:S(2)}, u32[]{:S(2)}) collective-permute-start(bf16[4,16,800]{2,1,0:T(8,128)(2,1)S(1)} %get-tuple-element.558), channel_id=1, source_target_pairs={{0,4},{4,8},{8,12},{12,16},{16,20},{20,24},{24,28},{1,5},{5,9},{9,... | collective-permute-start | bytes 307208 | tf_op jit(solution)/shard_map/ppermute | solution.py:686
  345.4 9.5 %collective-permute-start.33 = (bf16[4,16,800]{2,1,0:T(8,128)(2,1)S(1)}, bf16[4,16,800]{2,1,0:T(8,128)(2,1)S(1)}, u32[]{:S(2)}, u32[]{:S(2)}) collective-permute-start(bf16[4,16,800]{2,1,0:T(8,128)(2,1)S(1)} %get-tuple-element.557), channel_id=1, source_target_pairs={{4,0},{8,4},{12,8},{16,12},{20,16},{24,20},{28,24},{5,1},{9,5},{13... | collective-permute-start | bytes 307208 | tf_op jit(solution)/shard_map/ppermute | solution.py:691
  350.9 32.2 %collective-permute-start.35 = (bf16[2,2,176,800]{3,2,1,0:T(8,128)(2,1)}, bf16[2,2,176,800]{3,2,1,0:T(8,128)(2,1)S(1)}, u32[]{:S(2)}, u32[]{:S(2)}) collective-permute-start(bf16[2,2,176,800]{3,2,1,0:T(8,128)(2,1)} %bitcast.52), channel_id=1, source_target_pairs={{0,16},{4,20},{8,24},{12,28},{16,0},{20,4},{24,8},{28,12},{1,17},{... | collective-permute-start | bytes 3379208 | tf_op jit(solution)/shard_map/ppermute | solution.py:695
  354.7 28.4 %collective-permute-start.36 = (bf16[2,2,176,800]{3,2,1,0:T(8,128)(2,1)}, bf16[2,2,176,800]{3,2,1,0:T(8,128)(2,1)S(1)}, u32[]{:S(2)}, u32[]{:S(2)}) collective-permute-start(bf16[2,2,176,800]{3,2,1,0:T(8,128)(2,1)} %bitcast.53), channel_id=1, source_target_pairs={{0,8},{4,12},{8,0},{12,4},{16,24},{20,28},{24,16},{28,20},{1,9},{5... | collective-permute-start | bytes 3379208 | tf_op jit(solution)/shard_map/ppermute | solution.py:695
  387.2 26.7 %collective-permute-start.39 = (bf16[16,176,800]{2,1,0:T(8,128)(2,1)}, bf16[16,176,800]{2,1,0:T(8,128)(2,1)}, u32[]{:S(2)}, u32[]{:S(2)}) collective-permute-start(bf16[16,176,800]{2,1,0:T(8,128)(2,1)} %get-tuple-element.284), channel_id=1, source_target_pairs={{0,4},{4,0},{8,12},{12,8},{16,20},{20,16},{24,28},{28,24},{1,5},{5... | collective-permute-start | bytes 13516808 | tf_op jit(solution)/shard_map/ppermute | solution.py:695
  391.6 20.0 %collective-permute-start.38 = (bf16[1,2,176,800]{3,2,1,0:T(8,128)(2,1)}, bf16[1,2,176,800]{3,2,1,0:T(8,128)(2,1)}, u32[]{:S(2)}, u32[]{:S(2)}) collective-permute-start(bf16[1,2,176,800]{3,2,1,0:T(8,128)(2,1)} %get-tuple-element.282), channel_id=1, source_target_pairs={{0,16},{4,20},{8,24},{12,28},{16,0},{20,4},{24,8},{28,12},{1,17},{... | collective-permute-start | bytes 1689608 | tf_op jit(solution)/shard_map/ppermute | solution.py:695
  393.0 16.6 %collective-permute-start.37 = (bf16[1,2,176,800]{3,2,1,0:T(8,128)(2,1)}, bf16[1,2,176,800]{3,2,1,0:T(8,128)(2,1)}, u32[]{:S(2)}, u32[]{:S(2)}) collective-permute-start(bf16[1,2,176,800]{3,2,1,0:T(8,128)(2,1)} %get-tuple-element.281), channel_id=1, source_target_pairs={{0,8},{4,12},{8,0},{12,4},{16,24},{20,28},{24,16},{28,20},{1,9},{5... | collective-permute-start | bytes 1689608 | tf_op jit(solution)/shard_map/ppermute | solution.py:695
  418.0 40.8 %collective-permute-start.43 = (bf16[2,2,176,800]{3,2,1,0:T(8,128)(2,1)}, bf16[2,2,176,800]{3,2,1,0:T(8,128)(2,1)}, u32[]{:S(2)}, u32[]{:S(2)}) collective-permute-start(bf16[2,2,176,800]{3,2,1,0:T(8,128)(2,1)} %bitcast.62), channel_id=1, source_target_pairs={{0,16},{4,20},{8,24},{12,28},{16,0},{20,4},{24,8},{28,12},{1,17},{... | collective-permute-start | bytes 3379208 | tf_op jit(solution)/shard_map/ppermute | solution.py:695
  418.8 40.0 %collective-permute-start.44 = (bf16[2,2,176,800]{3,2,1,0:T(8,128)(2,1)}, bf16[2,2,176,800]{3,2,1,0:T(8,128)(2,1)}, u32[]{:S(2)}, u32[]{:S(2)}) collective-permute-start(bf16[2,2,176,800]{3,2,1,0:T(8,128)(2,1)} %bitcast.63), channel_id=1, source_target_pairs={{0,8},{4,12},{8,0},{12,4},{16,24},{20,28},{24,16},{28,20},{1,9},{5... | collective-permute-start | bytes 3379208 | tf_op jit(solution)/shard_map/ppermute | solution.py:695
  419.4 38.0 %collective-permute-start.40 = (bf16[176,800]{1,0:T(8,128)(2,1)}, bf16[176,800]{1,0:T(8,128)(2,1)S(1)}, u32[]{:S(2)}, u32[]{:S(2)}) collective-permute-start(bf16[176,800]{1,0:T(8,128)(2,1)} %fusion.22), channel_id=1, source_target_pairs={{0,1},{1,0},{2,3},{3,2},{4,5},{5,4},{6,7},{7,6},{8,9},{9,8},{10,11... | collective-permute-start | bytes 844808 | tf_op jit(solution)/shard_map/ppermute | solution.py:695
  427.7 29.7 %collective-permute-start.41 = (bf16[176,800]{1,0:T(8,128)(2,1)}, bf16[176,800]{1,0:T(8,128)(2,1)S(1)}, u32[]{:S(2)}, u32[]{:S(2)}) collective-permute-start(bf16[176,800]{1,0:T(8,128)(2,1)} %get-tuple-element.291), channel_id=1, source_target_pairs={{0,2},{1,3},{2,0},{3,1},{4,6},{5,7},{6,4},{7,5},{8,10},{9,11},{10,... | collective-permute-start | bytes 844808 | tf_op jit(solution)/shard_map/ppermute | solution.py:695
  428.7 28.7 %collective-permute-start.42 = (bf16[176,800]{1,0:T(8,128)(2,1)}, bf16[176,800]{1,0:T(8,128)(2,1)S(1)}, u32[]{:S(2)}, u32[]{:S(2)}) collective-permute-start(bf16[176,800]{1,0:T(8,128)(2,1)} %get-tuple-element.292), channel_id=1, source_target_pairs={{0,3},{1,2},{2,1},{3,0},{4,7},{5,6},{6,5},{7,4},{8,11},{9,10},{10,... | collective-permute-start | bytes 844808 | tf_op jit(solution)/shard_map/ppermute | solution.py:695
  462.3 30.7 %collective-permute-start.48 = (bf16[16,56,800]{2,1,0:T(8,128)(2,1)}, bf16[16,56,800]{2,1,0:T(8,128)(2,1)}, u32[]{:S(2)}, u32[]{:S(2)}) collective-permute-start(bf16[16,56,800]{2,1,0:T(8,128)(2,1)} %get-tuple-element.304), channel_id=1, source_target_pairs={{0,4},{4,0},{8,12},{12,8},{16,20},{20,16},{24,28},{28,24},{1,5},{5... | collective-permute-start | bytes 4300808 | tf_op jit(solution)/shard_map/ppermute | solution.py:695
  463.8 24.8 %collective-permute-start.46 = (bf16[1,2,176,800]{3,2,1,0:T(8,128)(2,1)}, bf16[1,2,176,800]{3,2,1,0:T(8,128)(2,1)}, u32[]{:S(2)}, u32[]{:S(2)}) collective-permute-start(bf16[1,2,176,800]{3,2,1,0:T(8,128)(2,1)} %get-tuple-element.301), channel_id=1, source_target_pairs={{0,8},{4,12},{8,0},{12,4},{16,24},{20,28},{24,16},{28,20},{1,9},{5... | collective-permute-start | bytes 1689608 | tf_op jit(solution)/shard_map/ppermute | solution.py:695
  466.1 21.4 %collective-permute-start.45 = (bf16[1,176,800]{2,1,0:T(8,128)(2,1)S(1)}, bf16[1,176,800]{2,1,0:T(8,128)(2,1)}, u32[]{:S(2)}, u32[]{:S(2)}) collective-permute-start(bf16[1,176,800]{2,1,0:T(8,128)(2,1)S(1)} %fusion.28), channel_id=1, source_target_pairs={{0,8},{4,12},{8,0},{12,4},{16,24},{20,28},{24,16},{28,20},{1,9},{5... | collective-permute-start | bytes 844808 | tf_op jit(solution)/shard_map/ppermute | solution.py:695
  467.0 23.5 %collective-permute-start.47 = (bf16[1,2,176,800]{3,2,1,0:T(8,128)(2,1)}, bf16[1,2,176,800]{3,2,1,0:T(8,128)(2,1)}, u32[]{:S(2)}, u32[]{:S(2)}) collective-permute-start(bf16[1,2,176,800]{3,2,1,0:T(8,128)(2,1)} %get-tuple-element.302), channel_id=1, source_target_pairs={{0,16},{4,20},{8,24},{12,28},{16,0},{20,4},{24,8},{28,12},{1,17},{... | collective-permute-start | bytes 1689608 | tf_op jit(solution)/shard_map/ppermute | solution.py:695
  495.1 30.5 %collective-permute-start.53 = (bf16[2,2,56,800]{3,2,1,0:T(8,128)(2,1)}, bf16[2,2,56,800]{3,2,1,0:T(8,128)(2,1)}, u32[]{:S(2)}, u32[]{:S(2)}) collective-permute-start(bf16[2,2,56,800]{3,2,1,0:T(8,128)(2,1)} %bitcast.75), channel_id=1, source_target_pairs={{0,16},{4,20},{8,24},{12,28},{16,0},{20,4},{24,8},{28,12},{1,17},{... | collective-permute-start | bytes 1075208 | tf_op jit(solution)/shard_map/ppermute | solution.py:695
  496.4 29.2 %collective-permute-start.54 = (bf16[2,2,56,800]{3,2,1,0:T(8,128)(2,1)}, bf16[2,2,56,800]{3,2,1,0:T(8,128)(2,1)}, u32[]{:S(2)}, u32[]{:S(2)}) collective-permute-start(bf16[2,2,56,800]{3,2,1,0:T(8,128)(2,1)} %bitcast.76), channel_id=1, source_target_pairs={{0,8},{4,12},{8,0},{12,4},{16,24},{20,28},{24,16},{28,20},{1,9},{5... | collective-permute-start | bytes 1075208 | tf_op jit(solution)/shard_map/ppermute | solution.py:695
  497.8 18.9 %collective-permute-start.50 = (bf16[176,800]{1,0:T(8,128)(2,1)}, bf16[176,800]{1,0:T(8,128)(2,1)S(1)}, u32[]{:S(2)}, u32[]{:S(2)}) collective-permute-start(bf16[176,800]{1,0:T(8,128)(2,1)} %fusion.25), channel_id=1, source_target_pairs={{0,1},{1,0},{2,3},{3,2},{4,5},{5,4},{6,7},{7,6},{8,9},{9,8},{10,11... | collective-permute-start | bytes 844808 | tf_op jit(solution)/shard_map/ppermute | solution.py:695
  498.9 25.1 %collective-permute-start.51 = (bf16[176,800]{1,0:T(8,128)(2,1)}, bf16[176,800]{1,0:T(8,128)(2,1)}, u32[]{:S(2)}, u32[]{:S(2)}) collective-permute-start(bf16[176,800]{1,0:T(8,128)(2,1)} %get-tuple-element.310), channel_id=1, source_target_pairs={{0,2},{1,3},{2,0},{3,1},{4,6},{5,7},{6,4},{7,5},{8,10},{9,11},{10,... | collective-permute-start | bytes 844808 | tf_op jit(solution)/shard_map/ppermute | solution.py:695
  500.7 23.2 %collective-permute-start.52 = (bf16[176,800]{1,0:T(8,128)(2,1)}, bf16[176,800]{1,0:T(8,128)(2,1)}, u32[]{:S(2)}, u32[]{:S(2)}) collective-permute-start(bf16[176,800]{1,0:T(8,128)(2,1)} %get-tuple-element.311), channel_id=1, source_target_pairs={{0,3},{1,2},{2,1},{3,0},{4,7},{5,6},{6,5},{7,4},{8,11},{9,10},{10,... | collective-permute-start | bytes 844808 | tf_op jit(solution)/shard_map/ppermute | solution.py:695
  516.8 14.5 %collective-permute-start.49 = (bf16[2,176,800]{2,1,0:T(8,128)(2,1)S(1)}, bf16[2,176,800]{2,1,0:T(8,128)(2,1)}, u32[]{:S(2)}, u32[]{:S(2)}) collective-permute-start(bf16[2,176,800]{2,1,0:T(8,128)(2,1)S(1)} %pad_maximum_fusion.9), channel_id=1, source_target_pairs={{0,16},{4,20},{8,24},{12,28},{16,0},{20,4},{24,8},{28,12},{1,17},{... | collective-permute-start | bytes 1689608 | tf_op jit(solution)/shard_map/ppermute | solution.py:695
  532.6 10.8 %collective-permute-start.58 = (f32[18,1600]{1,0:T(8,128)S(1)}, f32[18,1600]{1,0:T(8,128)S(1)}, u32[]{:S(2)}, u32[]{:S(2)}) collective-permute-start(f32[18,1600]{1,0:T(8,128)S(1)} %concatenate.66), channel_id=1, source_target_pairs={{0,4},{4,0},{8,12},{12,8},{16,20},{20,16},{24,28},{28,24},{1,5},{5... | collective-permute-start | bytes 345608 | tf_op jit(solution)/shard_map/ppermute | solution.py:695
  532.6 11.9 %collective-permute-start.57 = (bf16[1,2,56,800]{3,2,1,0:T(8,128)(2,1)S(1)}, bf16[1,2,56,800]{3,2,1,0:T(8,128)(2,1)S(1)}, u32[]{:S(2)}, u32[]{:S(2)}) collective-permute-start(bf16[1,2,56,800]{3,2,1,0:T(8,128)(2,1)S(1)} %get-tuple-element.327), channel_id=1, source_target_pairs={{0,16},{4,20},{8,24},{12,28},{16,0},{20,4},{24,8},{28,12},{1,17},{... | collective-permute-start | bytes 537608 | tf_op jit(solution)/shard_map/ppermute | solution.py:695
  533.3 10.2 %collective-permute-start.56 = (bf16[1,2,56,800]{3,2,1,0:T(8,128)(2,1)}, bf16[1,2,56,800]{3,2,1,0:T(8,128)(2,1)S(1)}, u32[]{:S(2)}, u32[]{:S(2)}) collective-permute-start(bf16[1,2,56,800]{3,2,1,0:T(8,128)(2,1)} %get-tuple-element.326), channel_id=1, source_target_pairs={{0,8},{4,12},{8,0},{12,4},{16,24},{20,28},{24,16},{28,20},{1,9},{5... | collective-permute-start | bytes 537608 | tf_op jit(solution)/shard_map/ppermute | solution.py:695
  534.1 13.2 %collective-permute-start.55 = (bf16[1,176,800]{2,1,0:T(8,128)(2,1)S(1)}, bf16[1,176,800]{2,1,0:T(8,128)(2,1)S(1)}, u32[]{:S(2)}, u32[]{:S(2)}) collective-permute-start(bf16[1,176,800]{2,1,0:T(8,128)(2,1)S(1)} %fusion.29), channel_id=1, source_target_pairs={{0,8},{4,12},{8,0},{12,4},{16,24},{20,28},{24,16},{28,20},{1,9},{5... | collective-permute-start | bytes 844808 | tf_op jit(solution)/shard_map/ppermute | solution.py:695
  535.3 33.0 %collective-permute-start.59 = (bf16[4,176,800]{2,1,0:T(8,128)(2,1)S(1)}, bf16[4,176,800]{2,1,0:T(8,128)(2,1)}, u32[]{:S(2)}, u32[]{:S(2)}) collective-permute-start(bf16[4,176,800]{2,1,0:T(8,128)(2,1)S(1)} %pad_maximum_fusion.2.refs_1_), channel_id=1, source_target_pairs={{0,4},{4,0},{8,12},{12,8},{16,20},{20,16},{24,28},{28,24},{1,5},{5... | collective-permute-start | bytes 3379208 | tf_op jit(solution)/shard_map/ppermute | solution.py:695
  547.4 19.7 %collective-permute-start.60 = (bf16[2,176,800]{2,1,0:T(8,128)(2,1)S(1)}, bf16[2,176,800]{2,1,0:T(8,128)(2,1)}, u32[]{:S(2)}, u32[]{:S(2)}) collective-permute-start(bf16[2,176,800]{2,1,0:T(8,128)(2,1)S(1)} %pad_maximum_fusion.10), channel_id=1, source_target_pairs={{0,16},{4,20},{8,24},{12,28},{16,0},{20,4},{24,8},{28,12},{1,17},{... | collective-permute-start | bytes 1689608 | tf_op jit(solution)/shard_map/ppermute | solution.py:695
  548.9 12.8 %collective-permute-start.61 = (bf16[56,800]{1,0:T(8,128)(2,1)S(1)}, bf16[56,800]{1,0:T(8,128)(2,1)S(1)}, u32[]{:S(2)}, u32[]{:S(2)}) collective-permute-start(bf16[56,800]{1,0:T(8,128)(2,1)S(1)} %fusion.38), channel_id=1, source_target_pairs={{0,1},{1,0},{2,3},{3,2},{4,5},{5,4},{6,7},{7,6},{8,9},{9,8},{10,11... | collective-permute-start | bytes 268808 | tf_op jit(solution)/shard_map/ppermute | solution.py:695
  550.6 11.8 %collective-permute-start.62 = (bf16[56,800]{1,0:T(8,128)(2,1)S(1)}, bf16[56,800]{1,0:T(8,128)(2,1)S(1)}, u32[]{:S(2)}, u32[]{:S(2)}) collective-permute-start(bf16[56,800]{1,0:T(8,128)(2,1)S(1)} %get-tuple-element.337), channel_id=1, source_target_pairs={{0,2},{1,3},{2,0},{3,1},{4,6},{5,7},{6,4},{7,5},{8,10},{9,11},{10,... | collective-permute-start | bytes 268808 | tf_op jit(solution)/shard_map/ppermute | solution.py:695
  551.9 10.5 %collective-permute-start.63 = (bf16[56,800]{1,0:T(8,128)(2,1)S(1)}, bf16[56,800]{1,0:T(8,128)(2,1)S(1)}, u32[]{:S(2)}, u32[]{:S(2)}) collective-permute-start(bf16[56,800]{1,0:T(8,128)(2,1)S(1)} %get-tuple-element.338), channel_id=1, source_target_pairs={{0,3},{1,2},{2,1},{3,0},{4,7},{5,6},{6,5},{7,4},{8,11},{9,10},{10,... | collective-permute-start | bytes 268808 | tf_op jit(solution)/shard_map/ppermute | solution.py:695
  573.3 6.9 %collective-permute-start.65 = (bf16[4,176,800]{2,1,0:T(8,128)(2,1)S(1)}, bf16[4,176,800]{2,1,0:T(8,128)(2,1)S(1)}, u32[]{:S(2)}, u32[]{:S(2)}) collective-permute-start(bf16[4,176,800]{2,1,0:T(8,128)(2,1)S(1)} %pad_maximum_fusion.3.refs_1_), channel_id=1, source_target_pairs={{0,4},{4,0},{8,12},{12,8},{16,20},{20,16},{24,28},{28,24},{1,5},{5... | collective-permute-start | bytes 3379208 | tf_op jit(solution)/shard_map/ppermute | solution.py:695
  586.0 6.3 %collective-permute-start.68 = (bf16[2,56,800]{2,1,0:T(8,128)(2,1)S(1)}, bf16[2,56,800]{2,1,0:T(8,128)(2,1)S(1)}, u32[]{:S(2)}, u32[]{:S(2)}) collective-permute-start(bf16[2,56,800]{2,1,0:T(8,128)(2,1)S(1)} %pad_maximum_fusion.15), channel_id=1, source_target_pairs={{0,16},{4,20},{8,24},{12,28},{16,0},{20,4},{24,8},{28,12},{1,17},{... | collective-permute-start | bytes 537608 | tf_op jit(solution)/shard_map/ppermute | solution.py:695
  592.4 8.9 %collective-permute-start.71 = (f32[18,1600]{1,0:T(8,128)S(1)}, f32[18,1600]{1,0:T(8,128)S(1)}, u32[]{:S(2)}, u32[]{:S(2)}) collective-permute-start(f32[18,1600]{1,0:T(8,128)S(1)} %add.585), channel_id=1, source_target_pairs={{0,2},{1,3},{2,0},{3,1},{4,6},{5,7},{6,4},{7,5},{8,10},{9,11},{10,... | collective-permute-start | bytes 345608 | tf_op jit(solution)/shard_map/ppermute | solution.py:695
  594.2 11.0 %collective-permute-start.70 = (bf16[4,56,800]{2,1,0:T(8,128)(2,1)S(1)}, bf16[4,56,800]{2,1,0:T(8,128)(2,1)S(1)}, u32[]{:S(2)}, u32[]{:S(2)}) collective-permute-start(bf16[4,56,800]{2,1,0:T(8,128)(2,1)S(1)} %pad_maximum_fusion.13.refs_1_), channel_id=1, source_target_pairs={{0,4},{4,0},{8,12},{12,8},{16,20},{20,16},{24,28},{28,24},{1,5},{5... | collective-permute-start | bytes 1075208 | tf_op jit(solution)/shard_map/ppermute | solution.py:695
  (48 other events, 333.1 us)
